TPU v7x, 512 devices: a whole 4x4x16 slice. The times are simulated.
512 devices in a mesh: replica: 16 (over z_hi, y), fsdp: 32 (over x, z_lo, core).
Axes of the slice: x: 4, y: 4, z: 16 (z_hi: 4, z_lo: 4; z = z_hi * 4 + z_lo), core: 2. Of those that a mesh axis runs over, the one named last changes fastest.
Arguments:
- activations: bfloat16 [16, 8192, 4096], P('replica', 'fsdp'), may hold values from -6 to 6
- cotangent: bfloat16 [16, 8192, 512], P('replica', 'fsdp'), may hold values from -6 to 6
- local_weight: float32 [16, 3, 4096, 512], P('replica', None, 'fsdp'), may hold values from -6 to 6
- outer_weight: float32 [3, 4096, 512], P(None, 'fsdp'), may hold values from -6 to 6
- outer_moment: float32 [3, 4096, 512], P(None, 'fsdp'), may hold values from -3 to 3
- fragment_index: int32 [1], replicated, may hold values from 0 to 2
Outputs:
- keys: bfloat16 [16, 8192, 512], P('replica', 'fsdp')
- local_new: float32 [16, 3, 4096, 512], P('replica', None, 'fsdp')
- outer_new: float32 [4096, 512], P('fsdp')
- moment_new: float32 [4096, 512], P('fsdp')
All inputs are finite; a program needn't handle non-finite values.
Results may differ from a plain program's by a relative error of at most 0.0085.
Values may be sent and summed in bfloat16 or wider, within the bound.
No kernel may reach another device: no remote copies, remote signals or barrier semaphores. Data moves between devices by JAX's collectives and lax.ppermute only.
A program may use at most 64 MiB of HBM per device.

v0:
```python
import jax
import jax.numpy as jnp
from jax import lax
from jax.sharding import PartitionSpec as P

inner_rate = 0.25
outer_rate = 0.7
momentum_factor = 0.9
mixing = 0.5


def shards(activations, cotangent, local_weight, outer_weight, outer_moment, fragment_index):
    inputs = activations[0]
    upstream = cotangent[0]
    layers = local_weight[0]
    scale = inputs.shape[1] ** (-0.5)
    trained = layers[0].astype(jnp.bfloat16)
    chosen = fragment_index[0]
    replicas = lax.axis_size("replica")
    old_outer = lax.dynamic_index_in_dim(outer_weight, chosen, 0, keepdims=False)
    old_moment = lax.dynamic_index_in_dim(outer_moment, chosen, 0, keepdims=False)
    columns = inputs
    summed = jnp.dot(
        columns,
        lax.all_gather(trained, "fsdp", axis=0, tiled=True),
        preferred_element_type=jnp.float32,
    )
    keys = (summed * scale).astype(jnp.bfloat16)[None]
    columns = inputs
    gradient = lax.psum_scatter(
        (
            jnp.einsum("td,tk->dk", columns, upstream, preferred_element_type=jnp.float32) * scale
        ).astype(jnp.bfloat16),
        "fsdp",
        scatter_dimension=0,
        tiled=True,
    ).astype(jnp.float32)
    updated = layers.at[0].set(layers[0] - inner_rate * gradient)
    selected = lax.dynamic_index_in_dim(updated, chosen, 0, keepdims=False)
    delta = old_outer - selected
    total_delta = lax.psum(delta, "replica")
    average = total_delta / replicas
    moment_new = momentum_factor * old_moment + average
    outer_new = old_outer - outer_rate * (average + momentum_factor * moment_new)
    mixed = mixing * selected + (1.0 - mixing) * outer_new
    chosen_mask = (jnp.arange(layers.shape[0]) == chosen)[:, None, None]
    local_new = jnp.where(chosen_mask, mixed[None], updated)[None]
    return (keys, local_new, outer_new, moment_new)


def solution(mesh):
    in_specs = (
        P("replica", "fsdp", None),
        P("replica", "fsdp", None),
        P("replica", None, "fsdp", None),
        P(None, "fsdp", None),
        P(None, "fsdp", None),
        P(),
    )
    out_specs = (
        P("replica", "fsdp", None),
        P("replica", None, "fsdp", None),
        P("fsdp", None),
        P("fsdp", None),
    )
    return jax.shard_map(shards, mesh=mesh, in_specs=in_specs, out_specs=out_specs, check_vma=False)
```

profile of v0, /device:TPU:2, one launch (start us, length us, event | category | flops | bytes accessed | tf_op | source)
XLA Modules:
  0.0 456.5 jit_solution(2113783268691475342)
XLA Ops:
  7.2 0.0 copy-start
  7.2 0.0 reduce-scatter.2.cloned.1.call-start
  7.2 1.5 copy-done
  8.8 4.2 multiply_convert_fusion
  13.0 0.0 reduce-scatter.2.cloned.1.call-update
  13.0 0.0 all-gather.2.cloned.1.call-start
  13.1 1.6 bitcast_convert_fusion
  14.7 0.0 all-gather.2.cloned.1.call-update
  14.7 0.0 all-reduce.2.cloned.1.call-start
  14.8 1.1 copy.10
  16.6 138.9 %reduce-scatter.2.cloned.1.call-done = bf16[128,512]{1,0:T(8,128)(2,1)} async-done(((bf16[4096,512]{1,0:T(8,128)(2,1)}), bf16[128,512]{1,0:T(8,128)(2,1)}) %reduce-scatter.2.cloned.1.call-update) | async-done | bytes 131088 | tf_op jit(solution)/shard_map/reduce_scatter | solution.py:30
  155.5 1.0 bitcast_dynamic-update-slice_fusion
  156.5 1.7 bitcast_subtract_fusion.1
  158.2 0.0 all-reduce.2.cloned.1.call-update
  158.2 84.3 %all-gather.2.cloned.1.call-done = bf16[4096,512]{1,0:T(8,128)(2,1)} async-done(((bf16[128,512]{1,0:T(8,128)(2,1)}), bf16[4096,512]{1,0:T(8,128)(2,1)}) %all-gather.2.cloned.1.call-update) | async-done | bytes 4194320 | tf_op jit(solution)/shard_map/all_gather | solution.py:25
  242.5 4.1 fusion.9
  246.7 200.2 %all-reduce.2.cloned.1.call-done = f32[128,512]{1,0:T(8,128)} async-done(((f32[128,512]{1,0:T(8,128)}), f32[128,512]{1,0:T(8,128)}) %all-reduce.2.cloned.1.call-update) | async-done | bytes 262160 | tf_op jit(solution)/shard_map/psum | solution.py:41
  446.9 2.0 fusion.12
  448.9 1.1 select_bitcast_fusion
  (1 shorter events, 0.0 us)
Async XLA Ops:
  7.2 1.6 copy-start
  7.2 148.3 %reduce-scatter.2.cloned.1.call-start = ((), (), s32[]{:S(2)}) async-start(), calls=%async_computation.2 | async-start | bytes 4325376 | tf_op jit(solution)/shard_map/reduce_scatter | solution.py:30
  13.0 229.5 %all-gather.2.cloned.1.call-start = ((), (), s32[]{:S(2)}) async-start(), calls=%async_computation.1 | async-start | bytes 4325376 | tf_op jit(solution)/shard_map/all_gather | solution.py:25
  14.7 432.2 %all-reduce.2.cloned.1.call-start = ((), (), s32[]{:S(2)}) async-start(), calls=%async_computation.3 | async-start | bytes 524288 | tf_op jit(solution)/shard_map/psum | solution.py:41
Sparse Core Ops, SparseCore 0:
  13.1 142.3 reduce-scatter.1
  158.2 84.2 all-gather.1
  246.0 200.8 all-reduce.1
where the time goes:
time: 457 us
  waiting for transfers between devices  423 us (93%)
  between operations  14.4 us (3%)
  matrix products  8.35 us (2%)
  other arithmetic  5.82 us (1%)
    psum x1, waiting for transfers between devices, shards(): total_delta = lax.psum(delta, 'replica')  200 us
    reduce_scatter x1, waiting for transfers between devices, shards(): lax.psum_scatter((jnp.einsum('td,tk->dk', columns, upstream, preferred_el...  139 us
    all_gather x1, waiting for transfers between devices, shards(): lax.all_gather(trained, 'fsdp', axis=0, tiled=True)  84.3 us
  transfers between devices with their start and end apart: 3, of which 3 were waited for; matrix products, arithmetic and copies ran while one was open for 2% of the time, Pallas kernels for 0%

commit v1 on v0

v1 whole, which is shorter than its diff:
```python
import jax
import jax.numpy as jnp
from jax import lax
from jax.experimental import pallas as pl
from jax.experimental.pallas import tpu as pltpu
from jax.sharding import Mesh, PartitionSpec as P

inner_rate = 0.25
outer_rate = 0.7
momentum_factor = 0.9
mixing = 0.5

SIDE = 4
CORES = 2
PIECE = 128


def pick_kernel(core_ref, all_ref, picked_ref, sems):
    runs = picked_ref.shape[1] // PIECE
    copies = []
    for run in range(runs):
        start = pl.multiple_of((2 * run + core_ref[0]) * PIECE, PIECE)
        copies.append(
            pltpu.make_async_copy(
                all_ref.at[:, pl.ds(start, PIECE)],
                picked_ref.at[:, pl.ds(run * PIECE, PIECE)],
                sems.at[run],
            )
        )
    for copy in copies:
        copy.start()
    for copy in copies:
        copy.wait()


def pick(inputs, core):
    tokens, width = inputs.shape
    return pl.pallas_call(
        pick_kernel,
        out_shape=jax.ShapeDtypeStruct((tokens, width // CORES), inputs.dtype),
        in_specs=[
            pl.BlockSpec(memory_space=pltpu.SMEM),
            pl.BlockSpec(memory_space=pl.ANY),
        ],
        out_specs=pl.BlockSpec(memory_space=pl.ANY),
        scratch_shapes=[pltpu.SemaphoreType.DMA((width // CORES // PIECE,))],
        name="pick_columns",
    )(core, inputs)


def grad_kernel(core_ref, mine_ref, theirs_ref, up_ref, their_up_ref, out_ref):
    scale = 4096 ** (-0.5)
    dims = (((0,), (0,)), ((), ()))
    for run in range(SIDE):
        start = pl.multiple_of((2 * run + core_ref[0]) * PIECE, PIECE)
        total = lax.dot_general(
            mine_ref[:, pl.ds(start, PIECE)], up_ref[...], dims, preferred_element_type=jnp.float32
        )
        total += lax.dot_general(
            theirs_ref[:, run * PIECE : (run + 1) * PIECE],
            their_up_ref[...],
            dims,
            preferred_element_type=jnp.float32,
        )
        out_ref[0, run * PIECE : (run + 1) * PIECE, :] = (total * scale).astype(out_ref.dtype)


def grad(core, mine, theirs, up, their_up):
    tokens, width = mine.shape
    features = up.shape[1]
    rows = SIDE * PIECE
    whole = lambda i, core_ref: (0, 0)
    return pl.pallas_call(
        grad_kernel,
        out_shape=jax.ShapeDtypeStruct((SIDE, rows, features), jnp.bfloat16),
        grid_spec=pltpu.PrefetchScalarGridSpec(
            num_scalar_prefetch=1,
            grid=(SIDE,),
            in_specs=[
                pl.BlockSpec((tokens, CORES * rows), lambda i, core_ref: (0, i)),
                pl.BlockSpec((tokens, rows), lambda i, core_ref: (0, i)),
                pl.BlockSpec((tokens, features), whole),
                pl.BlockSpec((tokens, features), whole),
            ],
            out_specs=pl.BlockSpec((1, rows, features), lambda i, core_ref: (i, 0, 0)),
        ),
        name="gradient",
    )(core, mine, theirs, up, their_up)


def shards(activations, cotangent, local_weight, outer_weight, outer_moment, fragment_index):
    inputs = activations[0]
    upstream = cotangent[0]
    layers = local_weight[0]
    scale = inputs.shape[1] ** (-0.5)
    trained = layers[0].astype(jnp.bfloat16)
    chosen = fragment_index[0]
    replicas = lax.axis_size("zh") * lax.axis_size("y")
    features = upstream.shape[1]
    core = lax.axis_index("c").astype(jnp.int32)

    gathered = lax.all_gather(trained, ("x", "zl", "c"), axis=0, tiled=True)

    swap = [(0, 1), (1, 0)]
    their_up = lax.ppermute(upstream, "c", swap)
    theirs = lax.ppermute(pick(inputs, (1 - core)[None]), "c", swap)
    part = grad(core[None], inputs, theirs, upstream, their_up)

    part = lax.all_to_all(part, "x", 0, 0)
    part = jnp.sum(part.astype(jnp.float32), axis=0).astype(jnp.bfloat16)
    part = lax.all_to_all(part.reshape(SIDE, PIECE, features), "zl", 0, 0)
    gradient = jnp.sum(part.astype(jnp.float32), axis=0)

    old_outer = lax.dynamic_index_in_dim(outer_weight, chosen, 0, keepdims=False)
    old_moment = lax.dynamic_index_in_dim(outer_moment, chosen, 0, keepdims=False)
    stale = lax.dynamic_index_in_dim(layers, chosen, 0, keepdims=False)
    selected = stale - inner_rate * jnp.where(chosen == 0, gradient, 0.0)
    delta = (old_outer - selected).astype(jnp.bfloat16)
    quarter = PIECE // SIDE
    total = lax.all_to_all(delta.reshape(SIDE, quarter, features), "y", 0, 0)
    total = jnp.sum(total.astype(jnp.float32), axis=0).astype(jnp.bfloat16)
    total = jnp.broadcast_to(total[None], (SIDE, quarter, features))
    total = lax.all_to_all(total, "zh", 0, 0)
    average = (jnp.sum(total.astype(jnp.float32), axis=0) / replicas).astype(jnp.bfloat16)
    average = jnp.broadcast_to(average[None], (SIDE, quarter, features))
    average = lax.all_to_all(average, "y", 0, 0).reshape(PIECE, features).astype(jnp.float32)

    summed = jnp.dot(inputs, gathered, preferred_element_type=jnp.float32)
    keys = (summed * scale).astype(jnp.bfloat16)[None]

    moment_new = momentum_factor * old_moment + average
    outer_new = old_outer - outer_rate * (average + momentum_factor * moment_new)
    mixed = mixing * selected + (1.0 - mixing) * outer_new
    number = jnp.arange(layers.shape[0])[:, None, None]
    updated = jnp.where(number == 0, layers - inner_rate * gradient[None], layers)
    local_new = jnp.where(number == chosen, mixed[None], updated)[None]
    return (keys, local_new, outer_new, moment_new)


def solution(mesh):
    fine = Mesh(
        mesh.devices.reshape(SIDE, SIDE, SIDE, SIDE, CORES), ("zh", "y", "x", "zl", "c")
    )
    replica = ("zh", "y")
    fsdp = ("x", "zl", "c")
    in_specs = (
        P(replica, fsdp, None),
        P(replica, fsdp, None),
        P(replica, None, fsdp, None),
        P(None, fsdp, None),
        P(None, fsdp, None),
        P(),
    )
    out_specs = (
        P(replica, fsdp, None),
        P(replica, None, fsdp, None),
        P(fsdp, None),
        P(fsdp, None),
    )
    return jax.shard_map(shards, mesh=fine, in_specs=in_specs, out_specs=out_specs, check_vma=False)
```

time: 457 us -> 173 us (0.38)
  waiting for transfers between devices: 423 us -> 20 us
  blocking collectives: 0 us -> 74.1 us
  Pallas kernels: 0 us -> 38 us
  starting transfers between devices: 0.12 us -> 11.2 us
    psum x1 -> x0, waiting for transfers between devices: 200 us -> none  [shards(): total_delta = lax.psum(delta, 'replica')]
    reduce_scatter x1 -> x0, waiting for transfers between devices: 139 us -> none  [shards(): lax.psum_scatter((jnp.einsum('td,tk->dk', columns, upstream, preferred_el...]
    all_gather x1, waiting for transfers between devices: 84.3 us -> 0.01 us  [shards(): gathered = lax.all_gather(trained, ('x', 'zl', 'c'), axis=0, tiled=True)]
    all_to_all x0 -> x3, blocking collectives: none -> 74.1 us  [the longest x1 40.6 us: shards(): part = lax.all_to_all(part, 'x', 0, 0)]
    pallas_call x0 -> x2, Pallas kernels: none -> 38 us  [the longest x1 33 us: pick(): pl.pallas_call(pick_kernel, out_shape=jax.ShapeDtypeStruct((tokens, width...]
    all_to_all x0 -> x2, waiting for transfers between devices: none -> 18.9 us  [the longest x1 12.9 us: shards(): part = lax.all_to_all(part.reshape(SIDE, PIECE, features), 'zl', 0, 0)]
    all_to_all x0 -> x2, starting transfers between devices: none -> 6.8 us  [the longest x1 3.47 us: shards(): part = lax.all_to_all(part.reshape(SIDE, PIECE, features), 'zl', 0, 0)]
  transfers between devices with their start and end apart: 3 -> 5, of which waited for: 3 -> 3; matrix products, arithmetic and copies ran while one was open for 2% -> 4% of each run, Pallas kernels for 0% -> 22%
where the time goes in v1:
time: 173 us
  blocking collectives  74.1 us (43%)
  Pallas kernels  38 us (22%)
  waiting for transfers between devices  20 us (12%)
  between operations  14.8 us (9%)
  starting transfers between devices  11.2 us (6%)
  other arithmetic  5.84 us (3%)
  local copies, waits for them, and re-layouts  4.42 us (3%)
  matrix products  4.14 us (2%)
    all_to_all x1, blocking collectives, shards(): part = lax.all_to_all(part, 'x', 0, 0)  40.6 us
    pallas_call x1, Pallas kernels, pick(): pl.pallas_call(pick_kernel, out_shape=jax.ShapeDtypeStruct((tokens, width...  33 us
    all_to_all x1, blocking collectives, shards(): total = lax.all_to_all(total, 'zh', 0, 0)  24.8 us
    all_to_all x1, waiting for transfers between devices, shards(): part = lax.all_to_all(part.reshape(SIDE, PIECE, features), 'zl', 0, 0)  12.9 us
    all_to_all x1, blocking collectives, shards(): total = lax.all_to_all(delta.reshape(SIDE, quarter, features), 'y', 0, 0)  8.67 us
    all_to_all x1, waiting for transfers between devices, shards(): lax.all_to_all(average, 'y', 0, 0).reshape(PIECE, features)  5.93 us
    pallas_call x1, Pallas kernels, grad(): pl.pallas_call(grad_kernel, out_shape=jax.ShapeDtypeStruct((SIDE, rows, f...  5.01 us
    dot_general x1, matrix products, shards(): summed = jnp.dot(inputs, gathered, preferred_element_type=jnp.float32)  4.14 us
  transfers between devices with their start and end apart: 5, of which 3 were waited for; matrix products, arithmetic and copies ran while one was open for 4% of the time, Pallas kernels for 22%

profile of v1, /device:TPU:2, one launch (start us, length us, event | category | flops | bytes accessed | tf_op | source)
XLA Modules:
  0.0 172.6 jit_solution(8839662613925580763)
XLA Ops:
  7.2 0.0 copy-start.3
  7.2 0.0 all-gather.3.cloned.1.call-start
  7.2 1.7 slice.8
  8.9 0.0 all-gather.3.cloned.1.call-update
  8.9 33.0 %pick_columns.1 = bf16[256,2048]{1,0:T(8,128)(2,1)} custom-call(s32[1]{0:T(128)} %bitcast.6.core_ref, bf16[256,4096]{1,0:T(8,128)(2,1)} %bitcast.66), custom_call_target="tpu_custom_call" | custom-call | tf_op jit(solution)/shard_map/pick_columns/pallas_call | solution.py:38
  41.9 1.9 %collective-permute-start = (bf16[256,2048]{1,0:T(8,128)(2,1)}, bf16[256,2048]{1,0:T(8,128)(2,1)S(1)}, u32[]{:S(2)}, u32[]{:S(2)}) collective-permute-start(bf16[256,2048]{1,0:T(8,128)(2,1)} %pick_columns.1), channel_id=1, source_target_pairs={{0,1},{1,0},{2,3},{3,2},{4,5},{5,4},{6,7},{7,6},{8,9},{9,8},{10,11... | collective-permute-start | bytes 3145736 | tf_op jit(solution)/shard_map/ppermute | solution.py:106
  43.9 0.0 copy-done.3
  43.9 2.4 %collective-permute-start.1 = (bf16[256,512]{1,0:T(8,128)(2,1)S(1)}, bf16[256,512]{1,0:T(8,128)(2,1)S(1)}, u32[]{:S(2)}, u32[]{:S(2)}) collective-permute-start(bf16[256,512]{1,0:T(8,128)(2,1)S(1)} %bitcast.73), channel_id=1, source_target_pairs={{0,1},{1,0},{2,3},{3,2},{4,5},{5,4},{6,7},{7,6},{8,9},{9,8},{10,11... | collective-permute-start | bytes 786440 | tf_op jit(solution)/shard_map/ppermute | solution.py:105
  46.3 1.1 collective-permute-done.1.their_up_ref
  47.4 0.0 copy-start.4
  47.4 0.0 collective-permute-done.theirs_ref
  47.4 0.0 copy-start.2
  47.4 0.7 copy-done.4
  48.1 0.4 copy-done.2
  48.5 5.0 %gradient.1 = bf16[4,512,512]{2,1,0:T(8,128)(2,1)} custom-call(s32[1]{0:T(128)} %bitcast.5.core_ref, bf16[256,4096]{1,0:T(8,128)(2,1)} %bitcast.67, bf16[256,2048]{1,0:T(8,128)(2,1)} %copy-done.2, bf16[256,512]{1,0:T(8,128)(2,1)} %bitcast.72, bf16[256,512]{1,0:T(8,128)(2,1)} %copy-done.4), custom_call_target="tpu_custom_call" | custom-call | tf_op jit(solution)/shard_map/gradient/pallas_call | solution.py:73
  53.5 40.6 %all_to_all.25 = bf16[4,512,512]{2,1,0:T(8,128)(2,1)S(1)} all-to-all(bf16[4,512,512]{2,1,0:T(8,128)(2,1)} %gradient.1), channel_id=1, replica_groups=mesh['zh'=4,'y'=4,'x'=4,'zl'=4,'c'=2] {'x'}, dimensions={0} | all-to-all | bytes 4194304 | tf_op jit(solution)/shard_map/all_to_all | solution.py:109
  94.2 0.0 copy-start.1
  94.2 1.2 reduce_sum.42
  95.4 3.5 %all-to-all-start.1 = ((bf16[4,128,512]{2,1,0:T(8,128)(2,1)}), bf16[4,128,512]{2,1,0:T(8,128)(2,1)S(1)}, u32[]{:S(2)}, u32[]{:S(2)}) async-start(bf16[4,128,512]{2,1,0:T(8,128)(2,1)} %bitcast.8), calls=%async_computation.1 | async-start | bytes 1048576 | tf_op jit(solution)/shard_map/all_to_all | solution.py:111
  99.5 0.0 copy-done.1
  99.6 1.0 constant_dynamic-slice_fusion
  100.5 12.9 %all-to-all-done.1 = bf16[4,128,512]{2,1,0:T(8,128)(2,1)S(1)} async-done(((bf16[4,128,512]{2,1,0:T(8,128)(2,1)}), bf16[4,128,512]{2,1,0:T(8,128)(2,1)S(1)}, u32[]{:S(2)}, u32[]{:S(2)}) %all-to-all-start.1) | async-done | bytes 524320 | tf_op jit(solution)/shard_map/all_to_all | solution.py:111
  113.5 0.1 convert_reduce_fusion
  113.6 0.1 select_multiply_fusion
  113.6 0.1 subtract_convert_fusion
  113.7 8.7 %all_to_all.26 = bf16[4,32,512]{2,1,0:T(8,128)(2,1)S(1)} all-to-all(bf16[4,32,512]{2,1,0:T(8,128)(2,1)S(1)} %subtract_convert_fusion), channel_id=1, replica_groups=mesh['zh'=4,'y'=4,'x'=4,'zl'=4,'c'=2] {'y'}, dimensions={0} | all-to-all | bytes 262144 | tf_op jit(solution)/shard_map/all_to_all | solution.py:120
  122.4 24.8 %all_to_all.27 = bf16[4,32,512]{2,1,0:T(8,128)(2,1)S(1)} all-to-all(bf16[4,32,512]{2,1,0:T(8,128)(2,1)S(1)} %broadcast_in_dim.60), channel_id=1, replica_groups=mesh['zh'=4,'y'=4,'x'=4,'zl'=4,'c'=2] {'zh'}, dimensions={0} | all-to-all | bytes 262144 | tf_op jit(solution)/shard_map/all_to_all | solution.py:123
  147.3 0.7 broadcast_in_dim.61
  147.9 3.3 %all-to-all-start.4 = ((bf16[4,32,512]{2,1,0:T(8,128)(2,1)}), bf16[4,32,512]{2,1,0:T(8,128)(2,1)S(1)}, u32[]{:S(2)}, u32[]{:S(2)}) async-start(bf16[4,32,512]{2,1,0:T(8,128)(2,1)} %broadcast_in_dim.61), calls=%async_computation.4 | async-start | bytes 262144 | tf_op jit(solution)/shard_map/all_to_all | solution.py:126
  151.3 5.9 %all-to-all-done.4 = bf16[4,32,512]{2,1,0:T(8,128)(2,1)S(1)} async-done(((bf16[4,32,512]{2,1,0:T(8,128)(2,1)}), bf16[4,32,512]{2,1,0:T(8,128)(2,1)S(1)}, u32[]{:S(2)}, u32[]{:S(2)}) %all-to-all-start.4) | async-done | bytes 131104 | tf_op jit(solution)/shard_map/all_to_all | solution.py:126
  157.2 1.9 %fusion.13 = (f32[128,512]{1,0:T(8,128)}, f32[128,512]{1,0:T(8,128)}) fusion(bf16[4,32,512]{2,1,0:T(8,128)(2,1)S(1)} %all-to-all-done.4, f32[3,128,512]{2,1,0:T(8,128)} %param.10, s32[]{:T(128)S(6)} %select_n.34, f32[3,128,512]{2,1,0:T(8,128)} %param.9), kind=kLoop, calls=%fused_computation.12 | loop fusion | flops 458752 | bytes 1179652 | tf_op jit(solution)/shard_map/sub | solution.py:132
  159.1 0.0 copy-start
  159.1 1.3 fusion.19
  160.5 1.1 fusion.11
  161.6 0.0 all-gather.3.cloned.1.call-done
  161.6 0.0 copy-done
  161.6 4.1 %fusion.8 = bf16[1,256,512]{2,1,0:T(8,128)(2,1)} fusion(bf16[1,1,4096,512]{3,2,1,0:T(8,128)(2,1)} %all-gather.3.cloned.1.call-done, bf16[1,256,4096]{2,1,0:T(8,128)(2,1)S(1)} %copy-done), kind=kOutput, calls=%fused_computation.5 | convolution fusion | flops 1074003968 | bytes 6553600 | tf_op jit(solution)/shard_map/dot_general | solution.py:128
  (7 shorter events, 0.1 us)
Async XLA Ops:
  7.2 36.7 %copy-start.3 = (bf16[1,256,512]{2,1,0:T(8,128)(2,1)S(1)}, bf16[1,256,512]{2,1,0:T(8,128)(2,1)}, u32[]{:S(2)}) copy-start(bf16[1,256,512]{2,1,0:T(8,128)(2,1)} %param.7) | copy-start | bytes 786436
  7.2 154.4 %all-gather.3.cloned.1.call-start = ((), (), s32[]{:S(2)}) async-start(), calls=%async_computation.5 | async-start | bytes 4325376 | tf_op jit(solution)/shard_map/all_gather | solution.py:102
  41.9 5.5 %collective-permute-start = (bf16[256,2048]{1,0:T(8,128)(2,1)}, bf16[256,2048]{1,0:T(8,128)(2,1)S(1)}, u32[]{:S(2)}, u32[]{:S(2)}) collective-permute-start(bf16[256,2048]{1,0:T(8,128)(2,1)} %pick_columns.1), channel_id=1, source_target_pairs={{0,1},{1,0},{2,3},{3,2},{4,5},{5,4},{6,7},{7,6},{8,9},{9,8},{10,11... | collective-permute-start | bytes 3145736 | tf_op jit(solution)/shard_map/ppermute | solution.py:106
  43.9 3.6 %collective-permute-start.1 = (bf16[256,512]{1,0:T(8,128)(2,1)S(1)}, bf16[256,512]{1,0:T(8,128)(2,1)S(1)}, u32[]{:S(2)}, u32[]{:S(2)}) collective-permute-start(bf16[256,512]{1,0:T(8,128)(2,1)S(1)} %bitcast.73), channel_id=1, source_target_pairs={{0,1},{1,0},{2,3},{3,2},{4,5},{5,4},{6,7},{7,6},{8,9},{9,8},{10,11... | collective-permute-start | bytes 786440 | tf_op jit(solution)/shard_map/ppermute | solution.py:105
  47.4 0.7 copy-start.4
  47.4 1.1 copy-start.2
  94.2 5.4 %copy-start.1 = (f32[1,3,128,512]{3,2,1,0:T(8,128)S(1)}, f32[1,3,128,512]{3,2,1,0:T(8,128)}, u32[]{:S(2)}) copy-start(f32[1,3,128,512]{3,2,1,0:T(8,128)} %param.8) | copy-start | bytes 2359300
  95.4 18.1 %all-to-all-start.1 = ((bf16[4,128,512]{2,1,0:T(8,128)(2,1)}), bf16[4,128,512]{2,1,0:T(8,128)(2,1)S(1)}, u32[]{:S(2)}, u32[]{:S(2)}) async-start(bf16[4,128,512]{2,1,0:T(8,128)(2,1)} %bitcast.8), calls=%async_computation.1 | async-start | bytes 1048576 | tf_op jit(solution)/shard_map/all_to_all | solution.py:111
  147.9 9.3 %all-to-all-start.4 = ((bf16[4,32,512]{2,1,0:T(8,128)(2,1)}), bf16[4,32,512]{2,1,0:T(8,128)(2,1)S(1)}, u32[]{:S(2)}, u32[]{:S(2)}) async-start(bf16[4,32,512]{2,1,0:T(8,128)(2,1)} %broadcast_in_dim.61), calls=%async_computation.4 | async-start | bytes 262144 | tf_op jit(solution)/shard_map/all_to_all | solution.py:126
  159.1 2.5 %copy-start = (bf16[1,256,4096]{2,1,0:T(8,128)(2,1)S(1)}, bf16[1,256,4096]{2,1,0:T(8,128)(2,1)}, u32[]{:S(2)}) copy-start(bf16[1,256,4096]{2,1,0:T(8,128)(2,1)} %param.6) | copy-start | bytes 6291460
Sparse Core Ops, SparseCore 0:
  10.7 82.4 all-gather.2

commit v2 on v0

v2 whole, which is shorter than its diff:
```python
import jax
import jax.numpy as jnp
from jax import lax
from jax.experimental import pallas as pl
from jax.experimental.pallas import tpu as pltpu
from jax.sharding import Mesh, PartitionSpec as P

inner_rate = 0.25
outer_rate = 0.7
momentum_factor = 0.9
mixing = 0.5

SIDE = 4
CORES = 2
PIECE = 128
ROWS = SIDE * PIECE
QUARTER = PIECE // SIDE
SCALE = 4096 ** (-0.5)

VMEM_LIMIT = 56 << 20

bf16 = jnp.bfloat16
f32 = jnp.float32


def core_columns(ref, core, chunk=0):
    runs = []
    for run in range(SIDE):
        start = ((chunk * SIDE + run) * CORES + core) * PIECE
        runs.append(ref[:, pl.ds(pl.multiple_of(start, PIECE), PIECE)])
    return jnp.concatenate(runs, axis=1)


def grad_kernel(place_ref, inputs_ref, theirs_ref, up_ref, their_up_ref, out_ref):
    dims = (((0,), (0,)), ((), ()))
    core = place_ref[1]
    total = lax.dot_general(
        core_columns(inputs_ref, core), up_ref[...], dims, preferred_element_type=f32
    )
    total += lax.dot_general(
        core_columns(theirs_ref, core), their_up_ref[...], dims, preferred_element_type=f32
    )
    out_ref[0] = (total * SCALE).astype(bf16)


def grad(place, inputs, theirs, up, their_up):
    tokens = inputs.shape[0]
    features = up.shape[1]
    wide = pl.BlockSpec((tokens, CORES * ROWS), lambda i, place: (0, i))
    whole = pl.BlockSpec((tokens, features), lambda i, place: (0, 0))
    return pl.pallas_call(
        grad_kernel,
        out_shape=jax.ShapeDtypeStruct((SIDE, ROWS, features), bf16),
        grid_spec=pltpu.PrefetchScalarGridSpec(
            num_scalar_prefetch=1,
            grid=(SIDE,),
            in_specs=[wide, wide, whole, whole],
            out_specs=pl.BlockSpec((1, ROWS, features), lambda i, place: (i, 0, 0)),
        ),
        cost_estimate=pl.CostEstimate(flops=1 << 30, bytes_accessed=6 << 20, transcendentals=0),
        compiler_params=pltpu.CompilerParams(vmem_limit_bytes=VMEM_LIMIT),
        name="gradient",
    )(place, inputs, theirs, up, their_up)


def cast_kernel(after_ref, layer_ref, out_ref):
    out_ref[...] = layer_ref[0].astype(bf16)


def cast(layers, after):
    features = layers.shape[2]
    return pl.pallas_call(
        cast_kernel,
        out_shape=jax.ShapeDtypeStruct((PIECE, features), bf16),
        grid=(1,),
        in_specs=[
            pl.BlockSpec(memory_space=pl.ANY),
            pl.BlockSpec((1, PIECE, features), lambda i: (0, 0, 0)),
        ],
        out_specs=pl.BlockSpec((PIECE, features), lambda i: (0, 0)),
        cost_estimate=pl.CostEstimate(flops=0, bytes_accessed=1 << 20, transcendentals=0),
        name="cast_weights",
    )(after, layers)


def their_keys_kernel(place_ref, theirs_ref, *refs):
    total = 0.0
    for offset in range(SIDE):
        chunk = lax.rem(place_ref[0] + SIDE - offset, SIDE)
        columns = core_columns(theirs_ref, place_ref[1], chunk)
        total += jnp.dot(columns, refs[offset][...], preferred_element_type=f32)
    refs[-1][...] = (total * SCALE).astype(bf16)


def their_keys(place, theirs, weights):
    tokens = theirs.shape[0]
    features = weights[0].shape[1]
    return pl.pallas_call(
        their_keys_kernel,
        out_shape=jax.ShapeDtypeStruct((tokens, features), bf16),
        in_specs=[pl.BlockSpec(memory_space=pltpu.SMEM)]
        + [pl.BlockSpec(memory_space=pltpu.VMEM)] * (1 + SIDE),
        out_specs=pl.BlockSpec(memory_space=pltpu.VMEM),
        cost_estimate=pl.CostEstimate(flops=1 << 29, bytes_accessed=3 << 20, transcendentals=0),
        compiler_params=pltpu.CompilerParams(vmem_limit_bytes=VMEM_LIMIT),
        name="their_keys",
    )(place, theirs, *weights)


def own_keys_kernel(place_ref, inputs_ref, other_ref, *refs):
    total = 0.0
    for offset in range(SIDE):
        chunk = lax.rem(place_ref[0] + SIDE - offset, SIDE)
        columns = core_columns(inputs_ref, place_ref[1], chunk)
        total += jnp.dot(columns, refs[offset][...], preferred_element_type=f32)
    refs[-1][0] = (total * SCALE + other_ref[...].astype(f32)).astype(bf16)


def own_keys(place, inputs, weights, other):
    tokens = inputs.shape[0]
    features = weights[0].shape[1]
    return pl.pallas_call(
        own_keys_kernel,
        out_shape=jax.ShapeDtypeStruct((1, tokens, features), bf16),
        in_specs=[pl.BlockSpec(memory_space=pltpu.SMEM)]
        + [pl.BlockSpec(memory_space=pltpu.VMEM)] * (2 + SIDE),
        out_specs=pl.BlockSpec(memory_space=pltpu.VMEM),
        cost_estimate=pl.CostEstimate(flops=1 << 29, bytes_accessed=4 << 20, transcendentals=0),
        compiler_params=pltpu.CompilerParams(vmem_limit_bytes=VMEM_LIMIT),
        name="own_keys",
    )(place, inputs, other, *weights)


def update_kernel(parts_ref, layers_ref, out_ref):
    gradient = parts_ref[0].astype(f32)
    for other in range(1, parts_ref.shape[0]):
        gradient += parts_ref[other].astype(f32)
    out_ref[0, 0] = layers_ref[0, 0] - inner_rate * gradient


def update(parts, layers):
    rows, features = layers.shape[2:]
    steps = 2
    block = rows // steps
    layer = pl.BlockSpec((1, 1, block, features), lambda i: (0, 0, i, 0))
    return pl.pallas_call(
        update_kernel,
        out_shape=jax.ShapeDtypeStruct(layers.shape, f32),
        grid=(steps,),
        in_specs=[pl.BlockSpec((parts.shape[0], block, features), lambda i: (0, i, 0)), layer],
        out_specs=layer,
        input_output_aliases={1: 0},
        cost_estimate=pl.CostEstimate(flops=1 << 19, bytes_accessed=1 << 20, transcendentals=0),
        compiler_params=pltpu.CompilerParams(vmem_limit_bytes=VMEM_LIMIT),
        name="update",
    )(parts, layers)


def settle_kernel(
    chosen_ref, average_ref, layer_ref, outer_ref, moment_ref, layer_out, outer_out, moment_out
):
    average = average_ref[...].astype(f32)
    moment = momentum_factor * moment_ref[0] + average
    outer = outer_ref[0] - outer_rate * (average + momentum_factor * moment)
    moment_out[...] = moment
    outer_out[...] = outer
    layer_out[0, 0] = mixing * layer_ref[0, 0] + (1.0 - mixing) * outer


def settle(chosen, average, updated, outer_weight, outer_moment):
    rows, features = updated.shape[2:]
    steps = 2
    block = rows // steps
    picked = pl.BlockSpec((1, block, features), lambda i, chosen: (chosen[0], i, 0))
    layer = pl.BlockSpec((1, 1, block, features), lambda i, chosen: (0, chosen[0], i, 0))
    flat = pl.BlockSpec((block, features), lambda i, chosen: (i, 0))
    return pl.pallas_call(
        settle_kernel,
        out_shape=(
            jax.ShapeDtypeStruct(updated.shape, f32),
            jax.ShapeDtypeStruct((rows, features), f32),
            jax.ShapeDtypeStruct((rows, features), f32),
        ),
        grid_spec=pltpu.PrefetchScalarGridSpec(
            num_scalar_prefetch=1,
            grid=(steps,),
            in_specs=[flat, layer, picked, picked],
            out_specs=(layer, flat, flat),
        ),
        input_output_aliases={2: 0},
        cost_estimate=pl.CostEstimate(flops=1 << 20, bytes_accessed=2 << 20, transcendentals=0),
        compiler_params=pltpu.CompilerParams(vmem_limit_bytes=VMEM_LIMIT),
        name="settle",
    )(chosen, average, updated, outer_weight, outer_moment)


def sum_all(parts):
    terms = [parts[index].astype(f32) for index in range(parts.shape[0])]
    while len(terms) > 1:
        terms = [first + second for first, second in zip(terms[::2], terms[1::2])]
    return terms[0]


def spread(rows):
    return jnp.broadcast_to(rows.astype(bf16)[None], (SIDE,) + rows.shape)


def shift(offset):
    return [(source, (source + offset) % SIDE) for source in range(SIDE)]


swap = [(0, 1), (1, 0)]


def shards(activations, cotangent, local_weight, outer_weight, outer_moment, fragment_index):
    inputs = activations[0]
    upstream = cotangent[0]
    layers = local_weight[0]
    features = upstream.shape[1]
    chosen = fragment_index[0]
    place = jnp.stack([lax.axis_index(name) for name in ("x", "c")]).astype(jnp.int32)

    theirs = lax.ppermute(inputs, "c", swap)
    their_up = lax.ppermute(upstream, "c", swap)
    part = grad(place, inputs, theirs, upstream, their_up)
    rows = lax.all_gather(cast(layers, part), "zl", axis=0, tiled=True)
    pick = lambda array: lax.dynamic_index_in_dim(array, chosen, 0, keepdims=False)
    delta = pick(outer_weight) - pick(layers)
    part = lax.all_to_all(part, "x", 0, 0)
    part, rows, delta = lax.optimization_barrier((part, rows, delta))

    part = sum_all(part).astype(bf16).reshape(SIDE, PIECE, features)
    part = lax.all_to_all(part, "zl", 0, 0)
    weights = [rows] + [lax.ppermute(rows, "x", shift(offset)) for offset in (1, 2, 3)]

    mean = delta + jnp.where(chosen == 0, inner_rate, 0.0) * sum_all(part)
    mean = mean.astype(bf16).reshape(SIDE, QUARTER, features)
    mean = sum_all(lax.all_to_all(mean, "y", 0, 0)) * (1.0 / (SIDE * SIDE))
    mean, weights[1], weights[3] = lax.optimization_barrier((mean, weights[1], weights[3]))
    mean = sum_all(lax.all_to_all(spread(mean), "zh", 0, 0))
    mean = lax.all_to_all(spread(mean), "y", 0, 0).reshape(PIECE, features)

    updated = update(part, local_weight)
    other = lax.ppermute(their_keys(place, theirs, weights), "c", swap)
    keys = own_keys(place, inputs, weights, other)
    local_new, outer_new, moment_new = settle(
        fragment_index, mean, updated, outer_weight, outer_moment
    )
    return keys, local_new, outer_new, moment_new


def solution(mesh):
    fine = Mesh(
        mesh.devices.reshape(SIDE, SIDE, SIDE, SIDE, CORES), ("zh", "y", "x", "zl", "c")
    )
    replica = ("zh", "y")
    fsdp = ("x", "zl", "c")
    in_specs = (
        P(replica, fsdp, None),
        P(replica, fsdp, None),
        P(replica, None, fsdp, None),
        P(None, fsdp, None),
        P(None, fsdp, None),
        P(),
    )
    out_specs = (
        P(replica, fsdp, None),
        P(replica, None, fsdp, None),
        P(fsdp, None),
        P(fsdp, None),
    )
    return jax.shard_map(shards, mesh=fine, in_specs=in_specs, out_specs=out_specs, check_vma=False)
```

time: 457 us -> 121 us (0.26)
  the two profiles are of different devices: /device:TPU:2 before, /device:TPU:8 now
where the time goes in v2:
time: 121 us; the launch traced here: 120 us
  starting transfers between devices  48.6 us (40%)
  waiting for transfers between devices  23.7 us (20%)
  Pallas kernels  18.6 us (15%)
  blocking collectives  17.1 us (14%)
  local copies, waits for them, and re-layouts  6.71 us (6%)
  other arithmetic  3.55 us (3%)
  between operations  1.43 us (1%)
    all_gather x1, blocking collectives, shards(): rows = lax.all_gather(cast(layers, part), 'zl', axis=0, tiled=True)  17.1 us
    all_to_all x1, starting transfers between devices, shards(): mean = sum_all(lax.all_to_all(spread(mean), 'zh', 0, 0))  11 us
    ppermute x3, starting transfers between devices, shards(): lax.ppermute(rows, 'x', shift(offset))  9.6 us
    all_to_all x1, waiting for transfers between devices, shards(): mean = sum_all(lax.all_to_all(spread(mean), 'zh', 0, 0))  7.22 us
    all_to_all x1, starting transfers between devices, shards(): mean = sum_all(lax.all_to_all(mean, 'y', 0, 0)) * (1.0 / (SIDE * SIDE))  6.83 us
    all_to_all x1, waiting for transfers between devices, shards(): part = lax.all_to_all(part, 'zl', 0, 0)  6.59 us
    all_to_all x1, waiting for transfers between devices, shards(): part = lax.all_to_all(part, 'x', 0, 0)  6.21 us
    all_to_all x1, starting transfers between devices, shards(): part = lax.all_to_all(part, 'zl', 0, 0)  5.9 us
  transfers between devices with their start and end apart: 11, of which 5 were waited for; matrix products, arithmetic and copies ran while one was open for 3% of the time, Pallas kernels for 9%

profile of v2, /device:TPU:8, one launch (start us, length us, event | category | flops | bytes accessed | tf_op | source)
XLA Modules:
  0.0 119.7 jit_solution(14814304807200377174)
XLA Ops:
  0.6 1.1 copy.16.layers_ref
  1.8 1.9 %collective-permute-start = (bf16[256,4096]{1,0:T(8,128)(2,1)}, bf16[256,4096]{1,0:T(8,128)(2,1)S(1)}, u32[]{:S(2)}, u32[]{:S(2)}) collective-permute-start(bf16[256,4096]{1,0:T(8,128)(2,1)} %bitcast.26), channel_id=1, source_target_pairs={{0,1},{1,0},{2,3},{3,2},{4,5},{5,4},{6,7},{7,6},{8,9},{9,8},{10,11... | collective-permute-start | bytes 6291464 | tf_op jit(solution)/shard_map/ppermute | solution.py:223
  3.7 2.4 %collective-permute-start.1 = (bf16[256,512]{1,0:T(8,128)(2,1)}, bf16[256,512]{1,0:T(8,128)(2,1)S(1)}, u32[]{:S(2)}, u32[]{:S(2)}) collective-permute-start(bf16[256,512]{1,0:T(8,128)(2,1)} %bitcast.30), channel_id=1, source_target_pairs={{0,1},{1,0},{2,3},{3,2},{4,5},{5,4},{6,7},{7,6},{8,9},{9,8},{10,11... | collective-permute-start | bytes 786440 | tf_op jit(solution)/shard_map/ppermute | solution.py:224
  6.1 0.6 pad_add_fusion.place_ref
  6.7 1.7 %collective-permute-done.1.their_up_ref = bf16[256,512]{1,0:T(8,128)(2,1)S(1)} collective-permute-done((bf16[256,512]{1,0:T(8,128)(2,1)}, bf16[256,512]{1,0:T(8,128)(2,1)S(1)}, u32[]{:S(2)}, u32[]{:S(2)}) %collective-permute-start.1) | collective-permute-done | bytes 262176 | tf_op jit(solution)/shard_map/ppermute | solution.py:224
  8.4 0.0 collective-permute-done.theirs_ref
  8.4 0.7 copy-done.9
  9.1 1.3 %copy-done.1 = bf16[256,4096]{1,0:T(8,128)(2,1)} copy-done((bf16[256,4096]{1,0:T(8,128)(2,1)}, bf16[256,4096]{1,0:T(8,128)(2,1)S(1)}, u32[]{:S(2)}) %copy-start.1) | copy-done | bytes 2097176
  10.4 5.9 %gradient.1.after_ref = bf16[4,512,512]{2,1,0:T(8,128)(2,1)} custom-call(s32[2]{0:T(128)} %pad_add_fusion.place_ref, bf16[256,4096]{1,0:T(8,128)(2,1)} %bitcast.27, bf16[256,4096]{1,0:T(8,128)(2,1)} %copy-done.1, bf16[256,512]{1,0:T(8,128)(2,1)} %bitcast.31, bf16[256,512]{1,0:T(8,128)(2,1)} %copy-done.9), custom_call_target="tpu_custom_call" | custom-call | flops 1073741824 | bytes 6291456 | tf_op jit(solution)/shard_map/gradient/pallas_call | solution.py:51
  16.3 4.3 %all-to-all-start = ((bf16[4,512,512]{2,1,0:T(8,128)(2,1)}), bf16[4,512,512]{2,1,0:T(8,128)(2,1)S(1)}, u32[]{:S(2)}, u32[]{:S(2)}) async-start(bf16[4,512,512]{2,1,0:T(8,128)(2,1)} %gradient.1.after_ref), calls=%async_computation | async-start | bytes 4194304 | tf_op jit(solution)/shard_map/all_to_all | solution.py:229
  21.2 0.0 copy-done
  21.2 1.0 bitcast_subtract_fusion
  22.2 1.6 %cast_weights.1 = bf16[128,512]{1,0:T(8,128)(2,1)} custom-call(bf16[4,512,512]{2,1,0:T(8,128)(2,1)} %gradient.1.after_ref, f32[3,128,512]{2,1,0:T(8,128)} %bitcast.25), custom_call_target="tpu_custom_call" | custom-call | bytes 1048576 | tf_op jit(solution)/shard_map/cast_weights/pallas_call | solution.py:72
  23.9 17.1 %all_gather.3.refs_0_ = bf16[512,512]{1,0:T(8,128)(2,1)S(1)} all-gather(bf16[128,512]{1,0:T(8,128)(2,1)} %cast_weights.1), channel_id=1, replica_groups=mesh['zh'=4,'y'=4,'x'=4,'zl'=4,'c'=2] {'zl'}, dimensions={0}, use_global_device_ids=true | all-gather | bytes 655360 | tf_op jit(solution)/shard_map/all_gather | solution.py:226
  41.0 6.2 %all-to-all-done = bf16[4,512,512]{2,1,0:T(8,128)(2,1)S(1)} async-done(((bf16[4,512,512]{2,1,0:T(8,128)(2,1)}), bf16[4,512,512]{2,1,0:T(8,128)(2,1)S(1)}, u32[]{:S(2)}, u32[]{:S(2)}) %all-to-all-start) | async-done | bytes 2097184 | tf_op jit(solution)/shard_map/all_to_all | solution.py:229
  47.2 1.1 add_convert_fusion
  48.3 5.9 %all-to-all-start.1 = ((bf16[4,128,512]{2,1,0:T(8,128)(2,1)}), bf16[4,128,512]{2,1,0:T(8,128)(2,1)S(1)}, u32[]{:S(2)}, u32[]{:S(2)}) async-start(bf16[4,128,512]{2,1,0:T(8,128)(2,1)} %bitcast.8), calls=%async_computation.1 | async-start | bytes 1048576 | tf_op jit(solution)/shard_map/all_to_all | solution.py:233
  54.2 2.5 %collective-permute-start.2 = (bf16[512,512]{1,0:T(8,128)(2,1)S(1)}, bf16[512,512]{1,0:T(8,128)(2,1)S(1)}, u32[]{:S(2)}, u32[]{:S(2)}) collective-permute-start(bf16[512,512]{1,0:T(8,128)(2,1)S(1)} %all_gather.3.refs_0_), channel_id=1, source_target_pairs={{0,8},{8,16},{16,24},{24,0},{1,9},{9,17},{17,25},{25,1},{2,10},{10... | collective-permute-start | bytes 1572872 | tf_op jit(solution)/shard_map/ppermute | solution.py:234
  56.7 4.6 %collective-permute-start.3 = (bf16[512,512]{1,0:T(8,128)(2,1)S(1)}, bf16[512,512]{1,0:T(8,128)(2,1)S(1)}, u32[]{:S(2)}, u32[]{:S(2)}) collective-permute-start(bf16[512,512]{1,0:T(8,128)(2,1)S(1)} %all_gather.3.refs_0_), channel_id=1, source_target_pairs={{0,24},{8,0},{16,8},{24,16},{1,25},{9,1},{17,9},{25,17},{2,26},{10... | collective-permute-start | bytes 1572872 | tf_op jit(solution)/shard_map/ppermute | solution.py:234
  61.2 6.6 %all-to-all-done.1.parts_ref = bf16[4,128,512]{2,1,0:T(8,128)(2,1)S(1)} async-done(((bf16[4,128,512]{2,1,0:T(8,128)(2,1)}), bf16[4,128,512]{2,1,0:T(8,128)(2,1)S(1)}, u32[]{:S(2)}, u32[]{:S(2)}) %all-to-all-start.1) | async-done | bytes 524320 | tf_op jit(solution)/shard_map/all_to_all | solution.py:233
  67.8 0.8 fusion
  68.7 6.8 %all-to-all-start.2 = ((bf16[4,32,512]{2,1,0:T(8,128)(2,1)}), bf16[4,32,512]{2,1,0:T(8,128)(2,1)S(1)}, u32[]{:S(2)}, u32[]{:S(2)}) async-start(bf16[4,32,512]{2,1,0:T(8,128)(2,1)} %bitcast.10), calls=%async_computation.2 | async-start | bytes 262144 | tf_op jit(solution)/shard_map/all_to_all | solution.py:238
  75.5 0.0 copy-done.2
  75.5 2.6 %collective-permute-start.4 = (bf16[512,512]{1,0:T(8,128)(2,1)S(1)}, bf16[512,512]{1,0:T(8,128)(2,1)S(1)}, u32[]{:S(2)}, u32[]{:S(2)}) collective-permute-start(bf16[512,512]{1,0:T(8,128)(2,1)S(1)} %all_gather.3.refs_0_), channel_id=1, source_target_pairs={{0,16},{8,24},{16,0},{24,8},{1,17},{9,25},{17,1},{25,9},{2,18},{10... | collective-permute-start | bytes 1572872 | tf_op jit(solution)/shard_map/ppermute | solution.py:234
  78.1 2.0 %all-to-all-done.2 = bf16[4,32,512]{2,1,0:T(8,128)(2,1)S(1)} async-done(((bf16[4,32,512]{2,1,0:T(8,128)(2,1)}), bf16[4,32,512]{2,1,0:T(8,128)(2,1)S(1)}, u32[]{:S(2)}, u32[]{:S(2)}) %all-to-all-start.2) | async-done | bytes 131104 | tf_op jit(solution)/shard_map/all_to_all | solution.py:238
  80.0 0.0 collective-permute-done.2.refs_1_
  80.0 0.0 copy-start.4
  80.1 0.0 collective-permute-done.3.refs_3_
  80.1 0.0 copy-start.5
  80.1 0.7 broadcast_in_dim.6
  80.8 11.0 %all-to-all-start.3 = ((bf16[4,32,512]{2,1,0:T(8,128)(2,1)}), bf16[4,32,512]{2,1,0:T(8,128)(2,1)S(1)}, u32[]{:S(2)}, u32[]{:S(2)}) async-start(bf16[4,32,512]{2,1,0:T(8,128)(2,1)} %broadcast_in_dim.6), calls=%async_computation.3 | async-start | bytes 262144 | tf_op jit(solution)/shard_map/all_to_all | solution.py:240
  91.8 0.0 collective-permute-done.4.refs_2_
  91.8 0.0 copy-done.4
  91.8 0.0 copy-done.5
  91.8 0.0 copy-start.6
  91.8 0.8 copy-done.6
  92.6 3.6 %their_keys.1 = bf16[256,512]{1,0:T(8,128)(2,1)} custom-call(s32[2]{0:T(128)} %pad_add_fusion.place_ref, bf16[256,4096]{1,0:T(8,128)(2,1)} %copy-done.1, bf16[512,512]{1,0:T(8,128)(2,1)} %copy-done.2, bf16[512,512]{1,0:T(8,128)(2,1)} %copy-done.4, bf16[512,512]{1,0:T(8,128)(2,1)} %copy-done.6, bf16[512,512]{1,0:T(8,128)(2,1)} %copy-done.5), custom_call_target="tpu_custom_call" | custom-call | flops 536870912 | bytes 3145728 | tf_op jit(solution)/shard_map/their_keys/pallas_call | solution.py:98
  96.2 1.9 %collective-permute-start.5 = (bf16[256,512]{1,0:T(8,128)(2,1)}, bf16[256,512]{1,0:T(8,128)(2,1)S(1)}, u32[]{:S(2)}, u32[]{:S(2)}) collective-permute-start(bf16[256,512]{1,0:T(8,128)(2,1)} %their_keys.1), channel_id=1, source_target_pairs={{0,1},{1,0},{2,3},{3,2},{4,5},{5,4},{6,7},{7,6},{8,9},{9,8},{10,11... | collective-permute-start | bytes 786440 | tf_op jit(solution)/shard_map/ppermute | solution.py:244
  98.1 7.2 %all-to-all-done.3 = bf16[4,32,512]{2,1,0:T(8,128)(2,1)S(1)} async-done(((bf16[4,32,512]{2,1,0:T(8,128)(2,1)}), bf16[4,32,512]{2,1,0:T(8,128)(2,1)S(1)}, u32[]{:S(2)}, u32[]{:S(2)}) %all-to-all-start.3) | async-done | bytes 131104 | tf_op jit(solution)/shard_map/all_to_all | solution.py:240
  105.4 0.7 broadcast_in_dim.16
  106.0 4.8 %all-to-all-start.4 = ((bf16[4,32,512]{2,1,0:T(8,128)(2,1)}), bf16[4,32,512]{2,1,0:T(8,128)(2,1)S(1)}, u32[]{:S(2)}, u32[]{:S(2)}) async-start(bf16[4,32,512]{2,1,0:T(8,128)(2,1)} %broadcast_in_dim.16), calls=%async_computation.4 | async-start | bytes 262144 | tf_op jit(solution)/shard_map/all_to_all | solution.py:241
  110.8 1.8 %update.1.layer_ref = f32[1,3,128,512]{3,2,1,0:T(8,128)} custom-call(bf16[4,128,512]{2,1,0:T(8,128)(2,1)} %copy-done.3, f32[1,3,128,512]{3,2,1,0:T(8,128)} %copy-done), custom_call_target="tpu_custom_call", output_to_operand_aliasing={{}: (1, {})} | custom-call | flops 524288 | bytes 1048576 | tf_op jit(solution)/shard_map/update/pallas_call | solution.py:146
  112.6 0.0 collective-permute-done.5.other_ref
  112.6 0.7 copy-done.8
  113.3 3.7 %own_keys.1 = bf16[1,256,512]{2,1,0:T(8,128)(2,1)} custom-call(s32[2]{0:T(128)} %pad_add_fusion.place_ref, bf16[256,4096]{1,0:T(8,128)(2,1)} %bitcast.28, bf16[256,512]{1,0:T(8,128)(2,1)} %copy-done.8, bf16[512,512]{1,0:T(8,128)(2,1)} %copy-done.2, bf16[512,512]{1,0:T(8,128)(2,1)} %copy-done.4, bf16[512,512]{1,0:T(8,128)(2,1)} %copy-done.6, ...), custom_call_target="tpu_custom_call" | custom-call | flops 536870912 | bytes 4194304 | tf_op jit(solution)/shard_map/own_keys/pallas_call | solution.py:122
  117.0 0.0 all-to-all-done.4
  117.0 0.7 copy-done.7
  117.6 2.0 %settle.1 = (f32[1,3,128,512]{3,2,1,0:T(8,128)}, f32[128,512]{1,0:T(8,128)}, f32[128,512]{1,0:T(8,128)}) custom-call(s32[1]{0:T(128)} %copy.15.chosen_ref, bf16[128,512]{1,0:T(8,128)(2,1)} %bitcast.29, f32[1,3,128,512]{3,2,1,0:T(8,128)} %update.1.layer_ref, f32[3,128,512]{2,1,0:T(8,128)} %outer_ref.1, ...), custom_call_target="tpu_custom_call", output_to_operand_aliasing={{0}: (2, {})} | custom-call | flops 1048576 | bytes 2097152 | tf_op jit(solution)/shard_map/settle/pallas_call | solution.py:177
  (10 shorter events, 0.1 us)
Async XLA Ops:
  1.8 19.5 %copy-start = (f32[1,3,128,512]{3,2,1,0:T(8,128)}, f32[1,3,128,512]{3,2,1,0:T(8,128)S(1)}, u32[]{:S(2)}) copy-start(f32[1,3,128,512]{3,2,1,0:T(8,128)S(1)} %copy.16.layers_ref) | copy-start | bytes 2359300
  1.8 6.6 %collective-permute-start = (bf16[256,4096]{1,0:T(8,128)(2,1)}, bf16[256,4096]{1,0:T(8,128)(2,1)S(1)}, u32[]{:S(2)}, u32[]{:S(2)}) collective-permute-start(bf16[256,4096]{1,0:T(8,128)(2,1)} %bitcast.26), channel_id=1, source_target_pairs={{0,1},{1,0},{2,3},{3,2},{4,5},{5,4},{6,7},{7,6},{8,9},{9,8},{10,11... | collective-permute-start | bytes 6291464 | tf_op jit(solution)/shard_map/ppermute | solution.py:223
  3.7 4.7 %collective-permute-start.1 = (bf16[256,512]{1,0:T(8,128)(2,1)}, bf16[256,512]{1,0:T(8,128)(2,1)S(1)}, u32[]{:S(2)}, u32[]{:S(2)}) collective-permute-start(bf16[256,512]{1,0:T(8,128)(2,1)} %bitcast.30), channel_id=1, source_target_pairs={{0,1},{1,0},{2,3},{3,2},{4,5},{5,4},{6,7},{7,6},{8,9},{9,8},{10,11... | collective-permute-start | bytes 786440 | tf_op jit(solution)/shard_map/ppermute | solution.py:224
  8.4 0.7 copy-start.9
  9.1 1.3 %copy-start.1 = (bf16[256,4096]{1,0:T(8,128)(2,1)}, bf16[256,4096]{1,0:T(8,128)(2,1)S(1)}, u32[]{:S(2)}) copy-start(bf16[256,4096]{1,0:T(8,128)(2,1)S(1)} %collective-permute-done.theirs_ref) | copy-start | bytes 6291460
  16.3 30.9 %all-to-all-start = ((bf16[4,512,512]{2,1,0:T(8,128)(2,1)}), bf16[4,512,512]{2,1,0:T(8,128)(2,1)S(1)}, u32[]{:S(2)}, u32[]{:S(2)}) async-start(bf16[4,512,512]{2,1,0:T(8,128)(2,1)} %gradient.1.after_ref), calls=%async_computation | async-start | bytes 4194304 | tf_op jit(solution)/shard_map/all_to_all | solution.py:229
  41.0 34.5 %copy-start.2 = (bf16[512,512]{1,0:T(8,128)(2,1)}, bf16[512,512]{1,0:T(8,128)(2,1)S(1)}, u32[]{:S(2)}) copy-start(bf16[512,512]{1,0:T(8,128)(2,1)S(1)} %all_gather.3.refs_0_) | copy-start | bytes 1572868
  48.3 19.5 %all-to-all-start.1 = ((bf16[4,128,512]{2,1,0:T(8,128)(2,1)}), bf16[4,128,512]{2,1,0:T(8,128)(2,1)S(1)}, u32[]{:S(2)}, u32[]{:S(2)}) async-start(bf16[4,128,512]{2,1,0:T(8,128)(2,1)} %bitcast.8), calls=%async_computation.1 | async-start | bytes 1048576 | tf_op jit(solution)/shard_map/all_to_all | solution.py:233
  54.2 25.9 %collective-permute-start.2 = (bf16[512,512]{1,0:T(8,128)(2,1)S(1)}, bf16[512,512]{1,0:T(8,128)(2,1)S(1)}, u32[]{:S(2)}, u32[]{:S(2)}) collective-permute-start(bf16[512,512]{1,0:T(8,128)(2,1)S(1)} %all_gather.3.refs_0_), channel_id=1, source_target_pairs={{0,8},{8,16},{16,24},{24,0},{1,9},{9,17},{17,25},{25,1},{2,10},{10... | collective-permute-start | bytes 1572872 | tf_op jit(solution)/shard_map/ppermute | solution.py:234
  56.7 23.4 %collective-permute-start.3 = (bf16[512,512]{1,0:T(8,128)(2,1)S(1)}, bf16[512,512]{1,0:T(8,128)(2,1)S(1)}, u32[]{:S(2)}, u32[]{:S(2)}) collective-permute-start(bf16[512,512]{1,0:T(8,128)(2,1)S(1)} %all_gather.3.refs_0_), channel_id=1, source_target_pairs={{0,24},{8,0},{16,8},{24,16},{1,25},{9,1},{17,9},{25,17},{2,26},{10... | collective-permute-start | bytes 1572872 | tf_op jit(solution)/shard_map/ppermute | solution.py:234
  67.8 28.4 %copy-start.3 = (bf16[4,128,512]{2,1,0:T(8,128)(2,1)}, bf16[4,128,512]{2,1,0:T(8,128)(2,1)S(1)}, u32[]{:S(2)}) copy-start(bf16[4,128,512]{2,1,0:T(8,128)(2,1)S(1)} %all-to-all-done.1.parts_ref) | copy-start | bytes 1572868
  68.7 11.3 %all-to-all-start.2 = ((bf16[4,32,512]{2,1,0:T(8,128)(2,1)}), bf16[4,32,512]{2,1,0:T(8,128)(2,1)S(1)}, u32[]{:S(2)}, u32[]{:S(2)}) async-start(bf16[4,32,512]{2,1,0:T(8,128)(2,1)} %bitcast.10), calls=%async_computation.2 | async-start | bytes 262144 | tf_op jit(solution)/shard_map/all_to_all | solution.py:238
  75.5 16.3 %collective-permute-start.4 = (bf16[512,512]{1,0:T(8,128)(2,1)S(1)}, bf16[512,512]{1,0:T(8,128)(2,1)S(1)}, u32[]{:S(2)}, u32[]{:S(2)}) collective-permute-start(bf16[512,512]{1,0:T(8,128)(2,1)S(1)} %all_gather.3.refs_0_), channel_id=1, source_target_pairs={{0,16},{8,24},{16,0},{24,8},{1,17},{9,25},{17,1},{25,9},{2,18},{10... | collective-permute-start | bytes 1572872 | tf_op jit(solution)/shard_map/ppermute | solution.py:234
  80.0 11.8 %copy-start.4 = (bf16[512,512]{1,0:T(8,128)(2,1)}, bf16[512,512]{1,0:T(8,128)(2,1)S(1)}, u32[]{:S(2)}) copy-start(bf16[512,512]{1,0:T(8,128)(2,1)S(1)} %collective-permute-done.2.refs_1_) | copy-start | bytes 1572868
  80.1 11.7 %copy-start.5 = (bf16[512,512]{1,0:T(8,128)(2,1)}, bf16[512,512]{1,0:T(8,128)(2,1)S(1)}, u32[]{:S(2)}) copy-start(bf16[512,512]{1,0:T(8,128)(2,1)S(1)} %collective-permute-done.3.refs_3_) | copy-start | bytes 1572868
  80.8 24.5 %all-to-all-start.3 = ((bf16[4,32,512]{2,1,0:T(8,128)(2,1)}), bf16[4,32,512]{2,1,0:T(8,128)(2,1)S(1)}, u32[]{:S(2)}, u32[]{:S(2)}) async-start(bf16[4,32,512]{2,1,0:T(8,128)(2,1)} %broadcast_in_dim.6), calls=%async_computation.3 | async-start | bytes 262144 | tf_op jit(solution)/shard_map/all_to_all | solution.py:240
  91.8 0.8 copy-start.6
  96.2 16.4 %collective-permute-start.5 = (bf16[256,512]{1,0:T(8,128)(2,1)}, bf16[256,512]{1,0:T(8,128)(2,1)S(1)}, u32[]{:S(2)}, u32[]{:S(2)}) collective-permute-start(bf16[256,512]{1,0:T(8,128)(2,1)} %their_keys.1), channel_id=1, source_target_pairs={{0,1},{1,0},{2,3},{3,2},{4,5},{5,4},{6,7},{7,6},{8,9},{9,8},{10,11... | collective-permute-start | bytes 786440 | tf_op jit(solution)/shard_map/ppermute | solution.py:244
  106.0 10.9 %all-to-all-start.4 = ((bf16[4,32,512]{2,1,0:T(8,128)(2,1)}), bf16[4,32,512]{2,1,0:T(8,128)(2,1)S(1)}, u32[]{:S(2)}, u32[]{:S(2)}) async-start(bf16[4,32,512]{2,1,0:T(8,128)(2,1)} %broadcast_in_dim.16), calls=%async_computation.4 | async-start | bytes 262144 | tf_op jit(solution)/shard_map/all_to_all | solution.py:241
  112.6 0.7 copy-start.8
  117.0 0.7 copy-start.7

commit v3 on v2

--- a/solution.py
+++ b/solution.py
@@ -18,6 +18,7 @@
 SCALE = 4096 ** (-0.5)
 
 VMEM_LIMIT = 56 << 20
+GRAD_VMEM_LIMIT = 60 << 20
 
 bf16 = jnp.bfloat16
 f32 = jnp.float32
@@ -31,34 +32,53 @@
     return jnp.concatenate(runs, axis=1)
 
 
-def grad_kernel(place_ref, inputs_ref, theirs_ref, up_ref, their_up_ref, out_ref):
-    dims = (((0,), (0,)), ((), ()))
-    core = place_ref[1]
-    total = lax.dot_general(
-        core_columns(inputs_ref, core), up_ref[...], dims, preferred_element_type=f32
-    )
-    total += lax.dot_general(
-        core_columns(theirs_ref, core), their_up_ref[...], dims, preferred_element_type=f32
-    )
-    out_ref[0] = (total * SCALE).astype(bf16)
+def grad_kernel(
+    place_ref, inputs_hbm, theirs_hbm, up_hbm, their_up_hbm, out_hbm, inputs, ups, out, in_sems, out_sems
+):
+    tokens = inputs_hbm.shape[0]
+    copies = [
+        pltpu.make_async_copy(inputs_hbm, inputs.at[:tokens], in_sems.at[0]),
+        pltpu.make_async_copy(theirs_hbm, inputs.at[tokens:], in_sems.at[1]),
+        pltpu.make_async_copy(up_hbm, ups.at[:tokens], in_sems.at[2]),
+        pltpu.make_async_copy(their_up_hbm, ups.at[tokens:], in_sems.at[3]),
+    ]
+    for copy in copies:
+        copy.start()
+    for copy in copies:
+        copy.wait()
+    stores = []
+    for chunk in range(SIDE):
+        total = lax.dot_general(
+            core_columns(inputs, place_ref[1], chunk),
+            ups[...],
+            (((0,), (0,)), ((), ())),
+            preferred_element_type=f32,
+        )
+        out[chunk] = (total * SCALE).astype(bf16)
+        stores.append(pltpu.make_async_copy(out.at[chunk], out_hbm.at[chunk], out_sems.at[chunk]))
+        stores[-1].start()
+    for store in stores:
+        store.wait()
 
 
 def grad(place, inputs, theirs, up, their_up):
-    tokens = inputs.shape[0]
+    tokens, width = inputs.shape
     features = up.shape[1]
-    wide = pl.BlockSpec((tokens, CORES * ROWS), lambda i, place: (0, i))
-    whole = pl.BlockSpec((tokens, features), lambda i, place: (0, 0))
+    anywhere = pl.BlockSpec(memory_space=pl.ANY)
     return pl.pallas_call(
         grad_kernel,
         out_shape=jax.ShapeDtypeStruct((SIDE, ROWS, features), bf16),
-        grid_spec=pltpu.PrefetchScalarGridSpec(
-            num_scalar_prefetch=1,
-            grid=(SIDE,),
-            in_specs=[wide, wide, whole, whole],
-            out_specs=pl.BlockSpec((1, ROWS, features), lambda i, place: (i, 0, 0)),
-        ),
+        in_specs=[pl.BlockSpec(memory_space=pltpu.SMEM)] + [anywhere] * 4,
+        out_specs=anywhere,
+        scratch_shapes=[
+            pltpu.VMEM((2 * tokens, width), bf16),
+            pltpu.VMEM((2 * tokens, features), bf16),
+            pltpu.VMEM((SIDE, ROWS, features), bf16),
+            pltpu.SemaphoreType.DMA((4,)),
+            pltpu.SemaphoreType.DMA((SIDE,)),
+        ],
         cost_estimate=pl.CostEstimate(flops=1 << 30, bytes_accessed=6 << 20, transcendentals=0),
-        compiler_params=pltpu.CompilerParams(vmem_limit_bytes=VMEM_LIMIT),
+        compiler_params=pltpu.CompilerParams(vmem_limit_bytes=GRAD_VMEM_LIMIT),
         name="gradient",
     )(place, inputs, theirs, up, their_up)
 
@@ -83,7 +103,7 @@
     )(after, layers)
 
 
-def their_keys_kernel(place_ref, theirs_ref, *refs):
+def their_keys_kernel(place_ref, after_ref, theirs_ref, *refs):
     total = 0.0
     for offset in range(SIDE):
         chunk = lax.rem(place_ref[0] + SIDE - offset, SIDE)
@@ -92,19 +112,19 @@
     refs[-1][...] = (total * SCALE).astype(bf16)
 
 
-def their_keys(place, theirs, weights):
+def their_keys(place, theirs, weights, after):
     tokens = theirs.shape[0]
     features = weights[0].shape[1]
     return pl.pallas_call(
         their_keys_kernel,
         out_shape=jax.ShapeDtypeStruct((tokens, features), bf16),
-        in_specs=[pl.BlockSpec(memory_space=pltpu.SMEM)]
+        in_specs=[pl.BlockSpec(memory_space=pltpu.SMEM), pl.BlockSpec(memory_space=pl.ANY)]
         + [pl.BlockSpec(memory_space=pltpu.VMEM)] * (1 + SIDE),
         out_specs=pl.BlockSpec(memory_space=pltpu.VMEM),
         cost_estimate=pl.CostEstimate(flops=1 << 29, bytes_accessed=3 << 20, transcendentals=0),
         compiler_params=pltpu.CompilerParams(vmem_limit_bytes=VMEM_LIMIT),
         name="their_keys",
-    )(place, theirs, *weights)
+    )(place, after, theirs, *weights)
 
 
 def own_keys_kernel(place_ref, inputs_ref, other_ref, *refs):
@@ -133,27 +153,28 @@
 
 def update_kernel(parts_ref, layers_ref, out_ref):
     gradient = parts_ref[0].astype(f32)
-    for other in range(1, parts_ref.shape[0]):
+    for other in range(1, SIDE):
         gradient += parts_ref[other].astype(f32)
     out_ref[0, 0] = layers_ref[0, 0] - inner_rate * gradient
-
-
-def update(parts, layers):
-    rows, features = layers.shape[2:]
+    for layer in range(1, layers_ref.shape[1]):
+        out_ref[0, layer] = layers_ref[0, layer]
+
+
+def update(parts, local_weight):
+    count, rows, features = local_weight.shape[1:]
     steps = 2
     block = rows // steps
-    layer = pl.BlockSpec((1, 1, block, features), lambda i: (0, 0, i, 0))
+    layers = pl.BlockSpec((1, count, block, features), lambda i: (0, 0, i, 0))
     return pl.pallas_call(
         update_kernel,
-        out_shape=jax.ShapeDtypeStruct(layers.shape, f32),
+        out_shape=jax.ShapeDtypeStruct(local_weight.shape, f32),
         grid=(steps,),
-        in_specs=[pl.BlockSpec((parts.shape[0], block, features), lambda i: (0, i, 0)), layer],
-        out_specs=layer,
-        input_output_aliases={1: 0},
-        cost_estimate=pl.CostEstimate(flops=1 << 19, bytes_accessed=1 << 20, transcendentals=0),
+        in_specs=[pl.BlockSpec((SIDE, block, features), lambda i: (0, i, 0)), layers],
+        out_specs=layers,
+        cost_estimate=pl.CostEstimate(flops=1 << 19, bytes_accessed=2 << 20, transcendentals=0),
         compiler_params=pltpu.CompilerParams(vmem_limit_bytes=VMEM_LIMIT),
         name="update",
-    )(parts, layers)
+    )(parts, local_weight)
 
 
 def settle_kernel(
@@ -241,7 +262,7 @@
     mean = lax.all_to_all(spread(mean), "y", 0, 0).reshape(PIECE, features)
 
     updated = update(part, local_weight)
-    other = lax.ppermute(their_keys(place, theirs, weights), "c", swap)
+    other = lax.ppermute(their_keys(place, theirs, weights, updated), "c", swap)
     keys = own_keys(place, inputs, weights, other)
     local_new, outer_new, moment_new = settle(
         fragment_index, mean, updated, outer_weight, outer_moment

time: 121 us -> 117 us (0.967)
  the two profiles are of different devices: /device:TPU:8 before, /device:TPU:2 now
where the time goes in v3:
time: 117 us; the launch traced here: 116 us
  starting transfers between devices  46.1 us (39%)
  waiting for transfers between devices  24.9 us (21%)
  Pallas kernels  18.1 us (15%)
  blocking collectives  16.5 us (14%)
  local copies, waits for them, and re-layouts  5.55 us (5%)
  other arithmetic  3.62 us (3%)
  between operations  1.48 us (1%)
    all_gather x1, blocking collectives, shards(): rows = lax.all_gather(cast(layers, part), 'zl', axis=0, tiled=True)  16.5 us
    all_to_all x1, starting transfers between devices, shards(): mean = sum_all(lax.all_to_all(spread(mean), 'zh', 0, 0))  11 us
    all_to_all x1, starting transfers between devices, shards(): part = lax.all_to_all(part, 'x', 0, 0)  9.49 us
    ppermute x3, starting transfers between devices, shards(): lax.ppermute(rows, 'x', shift(offset))  9.21 us
    all_to_all x1, waiting for transfers between devices, shards(): part = lax.all_to_all(part, 'zl', 0, 0)  8.35 us
    all_to_all x1, waiting for transfers between devices, shards(): part = lax.all_to_all(part, 'x', 0, 0)  5.63 us
    all_to_all x1, waiting for transfers between devices, shards(): mean = sum_all(lax.all_to_all(spread(mean), 'zh', 0, 0))  5.14 us
    pallas_call x1, Pallas kernels, grad(): pl.pallas_call(grad_kernel, out_shape=jax.ShapeDtypeStruct((SIDE, ROWS, f...  5.12 us
  transfers between devices with their start and end apart: 11, of which 6 were waited for; matrix products, arithmetic and copies ran while one was open for 3% of the time, Pallas kernels for 9%

profile of v3, /device:TPU:2, one launch (start us, length us, event | category | flops | bytes accessed | tf_op | source)
XLA Modules:
  0.0 116.2 jit_solution(1283922167049342400)
XLA Ops:
  0.6 1.9 %collective-permute-start = (bf16[256,4096]{1,0:T(8,128)(2,1)}, bf16[256,4096]{1,0:T(8,128)(2,1)S(1)}, u32[]{:S(2)}, u32[]{:S(2)}) collective-permute-start(bf16[256,4096]{1,0:T(8,128)(2,1)} %bitcast.25), channel_id=1, source_target_pairs={{0,1},{1,0},{2,3},{3,2},{4,5},{5,4},{6,7},{7,6},{8,9},{9,8},{10,11... | collective-permute-start | bytes 6291464 | tf_op jit(solution)/shard_map/ppermute | solution.py:244
  2.6 2.4 %collective-permute-start.1 = (bf16[256,512]{1,0:T(8,128)(2,1)}, bf16[256,512]{1,0:T(8,128)(2,1)S(1)}, u32[]{:S(2)}, u32[]{:S(2)}) collective-permute-start(bf16[256,512]{1,0:T(8,128)(2,1)} %bitcast.30), channel_id=1, source_target_pairs={{0,1},{1,0},{2,3},{3,2},{4,5},{5,4},{6,7},{7,6},{8,9},{9,8},{10,11... | collective-permute-start | bytes 786440 | tf_op jit(solution)/shard_map/ppermute | solution.py:245
  5.0 0.6 pad_add_fusion.place_ref
  5.6 1.7 %collective-permute-done.1.their_up_hbm = bf16[256,512]{1,0:T(8,128)(2,1)S(1)} collective-permute-done((bf16[256,512]{1,0:T(8,128)(2,1)}, bf16[256,512]{1,0:T(8,128)(2,1)S(1)}, u32[]{:S(2)}, u32[]{:S(2)}) %collective-permute-start.1) | collective-permute-done | bytes 262176 | tf_op jit(solution)/shard_map/ppermute | solution.py:245
  7.3 0.0 collective-permute-done.theirs_hbm.theirs_ref
  7.3 0.7 copy-done.8
  8.0 1.3 %copy-done = bf16[256,4096]{1,0:T(8,128)(2,1)} copy-done((bf16[256,4096]{1,0:T(8,128)(2,1)}, bf16[256,4096]{1,0:T(8,128)(2,1)S(1)}, u32[]{:S(2)}) %copy-start) | copy-done | bytes 2097176
  9.3 5.1 %gradient.1.after_ref = bf16[4,512,512]{2,1,0:T(8,128)(2,1)} custom-call(s32[2]{0:T(128)} %pad_add_fusion.place_ref, bf16[256,4096]{1,0:T(8,128)(2,1)} %bitcast.26, bf16[256,4096]{1,0:T(8,128)(2,1)} %copy-done, bf16[256,512]{1,0:T(8,128)(2,1)} %bitcast.31, bf16[256,512]{1,0:T(8,128)(2,1)} %copy-done.8), custom_call_target="tpu_custom_call" | custom-call | flops 1073741824 | bytes 6291456 | tf_op jit(solution)/shard_map/gradient/pallas_call | solution.py:68
  14.4 9.5 %all-to-all-start = ((bf16[4,512,512]{2,1,0:T(8,128)(2,1)}), bf16[4,512,512]{2,1,0:T(8,128)(2,1)S(1)}, u32[]{:S(2)}, u32[]{:S(2)}) async-start(bf16[4,512,512]{2,1,0:T(8,128)(2,1)} %gradient.1.after_ref), calls=%async_computation | async-start | bytes 4194304 | tf_op jit(solution)/shard_map/all_to_all | solution.py:250
  24.6 1.1 bitcast_subtract_fusion
  25.6 1.6 %cast_weights.1 = bf16[128,512]{1,0:T(8,128)(2,1)} custom-call(bf16[4,512,512]{2,1,0:T(8,128)(2,1)} %gradient.1.after_ref, f32[3,128,512]{2,1,0:T(8,128)} %bitcast.28), custom_call_target="tpu_custom_call" | custom-call | bytes 1048576 | tf_op jit(solution)/shard_map/cast_weights/pallas_call | solution.py:92
  27.3 16.5 %all_gather.3.refs_0_ = bf16[512,512]{1,0:T(8,128)(2,1)S(1)} all-gather(bf16[128,512]{1,0:T(8,128)(2,1)} %cast_weights.1), channel_id=1, replica_groups=mesh['zh'=4,'y'=4,'x'=4,'zl'=4,'c'=2] {'zl'}, dimensions={0}, use_global_device_ids=true | all-gather | bytes 655360 | tf_op jit(solution)/shard_map/all_gather | solution.py:247
  43.8 5.6 %all-to-all-done = bf16[4,512,512]{2,1,0:T(8,128)(2,1)S(1)} async-done(((bf16[4,512,512]{2,1,0:T(8,128)(2,1)}), bf16[4,512,512]{2,1,0:T(8,128)(2,1)S(1)}, u32[]{:S(2)}, u32[]{:S(2)}) %all-to-all-start) | async-done | bytes 2097184 | tf_op jit(solution)/shard_map/all_to_all | solution.py:250
  49.4 1.1 add_convert_fusion
  50.5 3.5 %all-to-all-start.1 = ((bf16[4,128,512]{2,1,0:T(8,128)(2,1)}), bf16[4,128,512]{2,1,0:T(8,128)(2,1)S(1)}, u32[]{:S(2)}, u32[]{:S(2)}) async-start(bf16[4,128,512]{2,1,0:T(8,128)(2,1)} %bitcast.8), calls=%async_computation.1 | async-start | bytes 1048576 | tf_op jit(solution)/shard_map/all_to_all | solution.py:254
  53.9 1.9 %collective-permute-start.2 = (bf16[512,512]{1,0:T(8,128)(2,1)S(1)}, bf16[512,512]{1,0:T(8,128)(2,1)S(1)}, u32[]{:S(2)}, u32[]{:S(2)}) collective-permute-start(bf16[512,512]{1,0:T(8,128)(2,1)S(1)} %all_gather.3.refs_0_), channel_id=1, source_target_pairs={{0,8},{8,16},{16,24},{24,0},{1,9},{9,17},{17,25},{25,1},{2,10},{10... | collective-permute-start | bytes 1572872 | tf_op jit(solution)/shard_map/ppermute | solution.py:255
  55.9 3.9 %collective-permute-start.3 = (bf16[512,512]{1,0:T(8,128)(2,1)S(1)}, bf16[512,512]{1,0:T(8,128)(2,1)S(1)}, u32[]{:S(2)}, u32[]{:S(2)}) collective-permute-start(bf16[512,512]{1,0:T(8,128)(2,1)S(1)} %all_gather.3.refs_0_), channel_id=1, source_target_pairs={{0,24},{8,0},{16,8},{24,16},{1,25},{9,1},{17,9},{25,17},{2,26},{10... | collective-permute-start | bytes 1572872 | tf_op jit(solution)/shard_map/ppermute | solution.py:255
  59.8 8.3 %all-to-all-done.1.parts_ref = bf16[4,128,512]{2,1,0:T(8,128)(2,1)S(1)} async-done(((bf16[4,128,512]{2,1,0:T(8,128)(2,1)}), bf16[4,128,512]{2,1,0:T(8,128)(2,1)S(1)}, u32[]{:S(2)}, u32[]{:S(2)}) %all-to-all-start.1) | async-done | bytes 524320 | tf_op jit(solution)/shard_map/all_to_all | solution.py:254
  68.2 0.8 fusion
  69.0 3.3 %all-to-all-start.2 = ((bf16[4,32,512]{2,1,0:T(8,128)(2,1)}), bf16[4,32,512]{2,1,0:T(8,128)(2,1)S(1)}, u32[]{:S(2)}, u32[]{:S(2)}) async-start(bf16[4,32,512]{2,1,0:T(8,128)(2,1)} %bitcast.10), calls=%async_computation.2 | async-start | bytes 262144 | tf_op jit(solution)/shard_map/all_to_all | solution.py:259
  72.3 0.0 copy-done.1
  72.3 3.4 %collective-permute-start.4 = (bf16[512,512]{1,0:T(8,128)(2,1)S(1)}, bf16[512,512]{1,0:T(8,128)(2,1)S(1)}, u32[]{:S(2)}, u32[]{:S(2)}) collective-permute-start(bf16[512,512]{1,0:T(8,128)(2,1)S(1)} %all_gather.3.refs_0_), channel_id=1, source_target_pairs={{0,16},{8,24},{16,0},{24,8},{1,17},{9,25},{17,1},{25,9},{2,18},{10... | collective-permute-start | bytes 1572872 | tf_op jit(solution)/shard_map/ppermute | solution.py:255
  75.7 2.6 %all-to-all-done.2 = bf16[4,32,512]{2,1,0:T(8,128)(2,1)S(1)} async-done(((bf16[4,32,512]{2,1,0:T(8,128)(2,1)}), bf16[4,32,512]{2,1,0:T(8,128)(2,1)S(1)}, u32[]{:S(2)}, u32[]{:S(2)}) %all-to-all-start.2) | async-done | bytes 131104 | tf_op jit(solution)/shard_map/all_to_all | solution.py:259
  78.3 0.0 collective-permute-done.2.refs_1_
  78.3 0.0 copy-start.3
  78.3 0.0 collective-permute-done.3.refs_3_
  78.3 0.0 copy-start.4
  78.3 0.7 broadcast_in_dim.6
  79.0 11.0 %all-to-all-start.3 = ((bf16[4,32,512]{2,1,0:T(8,128)(2,1)}), bf16[4,32,512]{2,1,0:T(8,128)(2,1)S(1)}, u32[]{:S(2)}, u32[]{:S(2)}) async-start(bf16[4,32,512]{2,1,0:T(8,128)(2,1)} %broadcast_in_dim.6), calls=%async_computation.3 | async-start | bytes 262144 | tf_op jit(solution)/shard_map/all_to_all | solution.py:261
  90.1 0.0 copy-done.2
  90.1 2.1 %update.1.after_ref.layer_ref = f32[1,3,128,512]{3,2,1,0:T(8,128)} custom-call(bf16[4,128,512]{2,1,0:T(8,128)(2,1)} %copy-done.2, f32[1,3,128,512]{3,2,1,0:T(8,128)} %layers_ref.1), custom_call_target="tpu_custom_call" | custom-call | flops 524288 | bytes 2097152 | tf_op jit(solution)/shard_map/update/pallas_call | solution.py:168
  92.1 0.0 collective-permute-done.4.refs_2_
  92.2 0.0 copy-done.3
  92.2 0.0 copy-done.4
  92.2 0.0 copy-start.5
  92.2 0.8 copy-done.5
  93.0 3.6 %their_keys.1 = bf16[256,512]{1,0:T(8,128)(2,1)} custom-call(s32[2]{0:T(128)} %pad_add_fusion.place_ref, f32[1,3,128,512]{3,2,1,0:T(8,128)} %update.1.after_ref.layer_ref, bf16[256,4096]{1,0:T(8,128)(2,1)} %copy-done, bf16[512,512]{1,0:T(8,128)(2,1)} %copy-done.1, bf16[512,512]{1,0:T(8,128)(2,1)} %copy-done.3, bf16[512,512]{1,0:T(8,128)(2,1)} %copy-done.5, ...), custom_call_target="tpu_custom_call" | custom-call | flops 536870912 | bytes 3145728 | tf_op jit(solution)/shard_map/their_keys/pallas_call | solution.py:118
  96.5 1.9 %collective-permute-start.5 = (bf16[256,512]{1,0:T(8,128)(2,1)}, bf16[256,512]{1,0:T(8,128)(2,1)S(1)}, u32[]{:S(2)}, u32[]{:S(2)}) collective-permute-start(bf16[256,512]{1,0:T(8,128)(2,1)} %their_keys.1), channel_id=1, source_target_pairs={{0,1},{1,0},{2,3},{3,2},{4,5},{5,4},{6,7},{7,6},{8,9},{9,8},{10,11... | collective-permute-start | bytes 786440 | tf_op jit(solution)/shard_map/ppermute | solution.py:265
  98.4 5.1 %all-to-all-done.3 = bf16[4,32,512]{2,1,0:T(8,128)(2,1)S(1)} async-done(((bf16[4,32,512]{2,1,0:T(8,128)(2,1)}), bf16[4,32,512]{2,1,0:T(8,128)(2,1)S(1)}, u32[]{:S(2)}, u32[]{:S(2)}) %all-to-all-start.3) | async-done | bytes 131104 | tf_op jit(solution)/shard_map/all_to_all | solution.py:261
  103.6 0.7 broadcast_in_dim.16
  104.3 3.3 %all-to-all-start.4 = ((bf16[4,32,512]{2,1,0:T(8,128)(2,1)}), bf16[4,32,512]{2,1,0:T(8,128)(2,1)S(1)}, u32[]{:S(2)}, u32[]{:S(2)}) async-start(bf16[4,32,512]{2,1,0:T(8,128)(2,1)} %broadcast_in_dim.16), calls=%async_computation.4 | async-start | bytes 262144 | tf_op jit(solution)/shard_map/all_to_all | solution.py:262
  107.6 0.0 collective-permute-done.5.other_ref
  107.6 0.0 copy-start.7
  107.6 0.7 copy-done.7
  108.3 3.7 %own_keys.1 = bf16[1,256,512]{2,1,0:T(8,128)(2,1)} custom-call(s32[2]{0:T(128)} %pad_add_fusion.place_ref, bf16[256,4096]{1,0:T(8,128)(2,1)} %bitcast.27, bf16[256,512]{1,0:T(8,128)(2,1)} %copy-done.7, bf16[512,512]{1,0:T(8,128)(2,1)} %copy-done.1, bf16[512,512]{1,0:T(8,128)(2,1)} %copy-done.3, bf16[512,512]{1,0:T(8,128)(2,1)} %copy-done.5, ...), custom_call_target="tpu_custom_call" | custom-call | flops 536870912 | bytes 4194304 | tf_op jit(solution)/shard_map/own_keys/pallas_call | solution.py:142
  112.0 1.6 %all-to-all-done.4 = bf16[4,32,512]{2,1,0:T(8,128)(2,1)S(1)} async-done(((bf16[4,32,512]{2,1,0:T(8,128)(2,1)}), bf16[4,32,512]{2,1,0:T(8,128)(2,1)S(1)}, u32[]{:S(2)}, u32[]{:S(2)}) %all-to-all-start.4) | async-done | bytes 131104 | tf_op jit(solution)/shard_map/all_to_all | solution.py:262
  113.6 0.6 copy-done.6
  114.2 2.0 %settle.1 = (f32[1,3,128,512]{3,2,1,0:T(8,128)}, f32[128,512]{1,0:T(8,128)}, f32[128,512]{1,0:T(8,128)}) custom-call(s32[1]{0:T(128)} %copy.12.chosen_ref, bf16[128,512]{1,0:T(8,128)(2,1)} %bitcast.29, f32[1,3,128,512]{3,2,1,0:T(8,128)} %update.1.after_ref.layer_ref, f32[3,128,512]{2,1,0:T(8,128)} %outer_ref.1, ...), custom_call_target="tpu_custom_call", output_to_operand_aliasing={{0}: (2, {})} | custom-call | flops 1048576 | bytes 2097152 | tf_op jit(solution)/shard_map/settle/pallas_call | solution.py:198
  (7 shorter events, 0.1 us)
Async XLA Ops:
  0.6 6.6 %collective-permute-start = (bf16[256,4096]{1,0:T(8,128)(2,1)}, bf16[256,4096]{1,0:T(8,128)(2,1)S(1)}, u32[]{:S(2)}, u32[]{:S(2)}) collective-permute-start(bf16[256,4096]{1,0:T(8,128)(2,1)} %bitcast.25), channel_id=1, source_target_pairs={{0,1},{1,0},{2,3},{3,2},{4,5},{5,4},{6,7},{7,6},{8,9},{9,8},{10,11... | collective-permute-start | bytes 6291464 | tf_op jit(solution)/shard_map/ppermute | solution.py:244
  2.6 4.7 %collective-permute-start.1 = (bf16[256,512]{1,0:T(8,128)(2,1)}, bf16[256,512]{1,0:T(8,128)(2,1)S(1)}, u32[]{:S(2)}, u32[]{:S(2)}) collective-permute-start(bf16[256,512]{1,0:T(8,128)(2,1)} %bitcast.30), channel_id=1, source_target_pairs={{0,1},{1,0},{2,3},{3,2},{4,5},{5,4},{6,7},{7,6},{8,9},{9,8},{10,11... | collective-permute-start | bytes 786440 | tf_op jit(solution)/shard_map/ppermute | solution.py:245
  7.3 0.7 copy-start.8
  8.0 1.3 %copy-start = (bf16[256,4096]{1,0:T(8,128)(2,1)}, bf16[256,4096]{1,0:T(8,128)(2,1)S(1)}, u32[]{:S(2)}) copy-start(bf16[256,4096]{1,0:T(8,128)(2,1)S(1)} %collective-permute-done.theirs_hbm.theirs_ref) | copy-start | bytes 6291460
  14.4 35.0 %all-to-all-start = ((bf16[4,512,512]{2,1,0:T(8,128)(2,1)}), bf16[4,512,512]{2,1,0:T(8,128)(2,1)S(1)}, u32[]{:S(2)}, u32[]{:S(2)}) async-start(bf16[4,512,512]{2,1,0:T(8,128)(2,1)} %gradient.1.after_ref), calls=%async_computation | async-start | bytes 4194304 | tf_op jit(solution)/shard_map/all_to_all | solution.py:250
  43.8 28.6 %copy-start.1 = (bf16[512,512]{1,0:T(8,128)(2,1)}, bf16[512,512]{1,0:T(8,128)(2,1)S(1)}, u32[]{:S(2)}) copy-start(bf16[512,512]{1,0:T(8,128)(2,1)S(1)} %all_gather.3.refs_0_) | copy-start | bytes 1572868
  50.5 17.7 %all-to-all-start.1 = ((bf16[4,128,512]{2,1,0:T(8,128)(2,1)}), bf16[4,128,512]{2,1,0:T(8,128)(2,1)S(1)}, u32[]{:S(2)}, u32[]{:S(2)}) async-start(bf16[4,128,512]{2,1,0:T(8,128)(2,1)} %bitcast.8), calls=%async_computation.1 | async-start | bytes 1048576 | tf_op jit(solution)/shard_map/all_to_all | solution.py:254
  53.9 24.3 %collective-permute-start.2 = (bf16[512,512]{1,0:T(8,128)(2,1)S(1)}, bf16[512,512]{1,0:T(8,128)(2,1)S(1)}, u32[]{:S(2)}, u32[]{:S(2)}) collective-permute-start(bf16[512,512]{1,0:T(8,128)(2,1)S(1)} %all_gather.3.refs_0_), channel_id=1, source_target_pairs={{0,8},{8,16},{16,24},{24,0},{1,9},{9,17},{17,25},{25,1},{2,10},{10... | collective-permute-start | bytes 1572872 | tf_op jit(solution)/shard_map/ppermute | solution.py:255
  55.9 22.4 %collective-permute-start.3 = (bf16[512,512]{1,0:T(8,128)(2,1)S(1)}, bf16[512,512]{1,0:T(8,128)(2,1)S(1)}, u32[]{:S(2)}, u32[]{:S(2)}) collective-permute-start(bf16[512,512]{1,0:T(8,128)(2,1)S(1)} %all_gather.3.refs_0_), channel_id=1, source_target_pairs={{0,24},{8,0},{16,8},{24,16},{1,25},{9,1},{17,9},{25,17},{2,26},{10... | collective-permute-start | bytes 1572872 | tf_op jit(solution)/shard_map/ppermute | solution.py:255
  68.1 21.9 %copy-start.2 = (bf16[4,128,512]{2,1,0:T(8,128)(2,1)}, bf16[4,128,512]{2,1,0:T(8,128)(2,1)S(1)}, u32[]{:S(2)}) copy-start(bf16[4,128,512]{2,1,0:T(8,128)(2,1)S(1)} %all-to-all-done.1.parts_ref) | copy-start | bytes 1572868
  69.0 9.3 %all-to-all-start.2 = ((bf16[4,32,512]{2,1,0:T(8,128)(2,1)}), bf16[4,32,512]{2,1,0:T(8,128)(2,1)S(1)}, u32[]{:S(2)}, u32[]{:S(2)}) async-start(bf16[4,32,512]{2,1,0:T(8,128)(2,1)} %bitcast.10), calls=%async_computation.2 | async-start | bytes 262144 | tf_op jit(solution)/shard_map/all_to_all | solution.py:259
  72.3 19.8 %collective-permute-start.4 = (bf16[512,512]{1,0:T(8,128)(2,1)S(1)}, bf16[512,512]{1,0:T(8,128)(2,1)S(1)}, u32[]{:S(2)}, u32[]{:S(2)}) collective-permute-start(bf16[512,512]{1,0:T(8,128)(2,1)S(1)} %all_gather.3.refs_0_), channel_id=1, source_target_pairs={{0,16},{8,24},{16,0},{24,8},{1,17},{9,25},{17,1},{25,9},{2,18},{10... | collective-permute-start | bytes 1572872 | tf_op jit(solution)/shard_map/ppermute | solution.py:255
  78.3 13.9 %copy-start.3 = (bf16[512,512]{1,0:T(8,128)(2,1)}, bf16[512,512]{1,0:T(8,128)(2,1)S(1)}, u32[]{:S(2)}) copy-start(bf16[512,512]{1,0:T(8,128)(2,1)S(1)} %collective-permute-done.2.refs_1_) | copy-start | bytes 1572868
  78.3 13.9 %copy-start.4 = (bf16[512,512]{1,0:T(8,128)(2,1)}, bf16[512,512]{1,0:T(8,128)(2,1)S(1)}, u32[]{:S(2)}) copy-start(bf16[512,512]{1,0:T(8,128)(2,1)S(1)} %collective-permute-done.3.refs_3_) | copy-start | bytes 1572868
  79.0 24.6 %all-to-all-start.3 = ((bf16[4,32,512]{2,1,0:T(8,128)(2,1)}), bf16[4,32,512]{2,1,0:T(8,128)(2,1)S(1)}, u32[]{:S(2)}, u32[]{:S(2)}) async-start(bf16[4,32,512]{2,1,0:T(8,128)(2,1)} %broadcast_in_dim.6), calls=%async_computation.3 | async-start | bytes 262144 | tf_op jit(solution)/shard_map/all_to_all | solution.py:261
  92.2 0.8 copy-start.5
  96.5 11.1 %collective-permute-start.5 = (bf16[256,512]{1,0:T(8,128)(2,1)}, bf16[256,512]{1,0:T(8,128)(2,1)S(1)}, u32[]{:S(2)}, u32[]{:S(2)}) collective-permute-start(bf16[256,512]{1,0:T(8,128)(2,1)} %their_keys.1), channel_id=1, source_target_pairs={{0,1},{1,0},{2,3},{3,2},{4,5},{5,4},{6,7},{7,6},{8,9},{9,8},{10,11... | collective-permute-start | bytes 786440 | tf_op jit(solution)/shard_map/ppermute | solution.py:265
  104.3 9.3 %all-to-all-start.4 = ((bf16[4,32,512]{2,1,0:T(8,128)(2,1)}), bf16[4,32,512]{2,1,0:T(8,128)(2,1)S(1)}, u32[]{:S(2)}, u32[]{:S(2)}) async-start(bf16[4,32,512]{2,1,0:T(8,128)(2,1)} %broadcast_in_dim.16), calls=%async_computation.4 | async-start | bytes 262144 | tf_op jit(solution)/shard_map/all_to_all | solution.py:262
  107.6 0.7 copy-start.7
  113.6 0.6 copy-start.6

commit v4 on v3

--- a/solution.py
+++ b/solution.py
@@ -17,8 +17,8 @@
 QUARTER = PIECE // SIDE
 SCALE = 4096 ** (-0.5)
 
-VMEM_LIMIT = 56 << 20
-GRAD_VMEM_LIMIT = 60 << 20
+VMEM_LIMIT = 12 << 20
+GRAD_VMEM_LIMIT = 62 << 20
 
 bf16 = jnp.bfloat16
 f32 = jnp.float32
@@ -103,64 +103,73 @@
     )(after, layers)
 
 
-def their_keys_kernel(place_ref, after_ref, theirs_ref, *refs):
-    total = 0.0
-    for offset in range(SIDE):
+def keys_kernel(
+    place_ref, inputs_hbm, theirs_hbm, w0_hbm, w1_hbm, w2_hbm, w3_hbm, own_ref, other_ref, inputs, theirs, weights, sems
+):
+    sources = (w0_hbm, w1_hbm, w2_hbm, w3_hbm)
+    offsets = (0, 1, 3, 2)
+    loads = [
+        pltpu.make_async_copy(inputs_hbm, inputs, sems.at[SIDE]),
+        pltpu.make_async_copy(theirs_hbm, theirs, sems.at[SIDE + 1]),
+    ]
+    rows = [
+        pltpu.make_async_copy(sources[offset], weights.at[offset], sems.at[offset])
+        for offset in range(SIDE)
+    ]
+    rows[0].start()
+    for load in loads:
+        load.start()
+    for offset in offsets[1:]:
+        rows[offset].start()
+    for load in loads:
+        load.wait()
+    own = 0.0
+    other = 0.0
+    for offset in offsets:
         chunk = lax.rem(place_ref[0] + SIDE - offset, SIDE)
-        columns = core_columns(theirs_ref, place_ref[1], chunk)
-        total += jnp.dot(columns, refs[offset][...], preferred_element_type=f32)
-    refs[-1][...] = (total * SCALE).astype(bf16)
-
-
-def their_keys(place, theirs, weights, after):
-    tokens = theirs.shape[0]
-    features = weights[0].shape[1]
-    return pl.pallas_call(
-        their_keys_kernel,
-        out_shape=jax.ShapeDtypeStruct((tokens, features), bf16),
-        in_specs=[pl.BlockSpec(memory_space=pltpu.SMEM), pl.BlockSpec(memory_space=pl.ANY)]
-        + [pl.BlockSpec(memory_space=pltpu.VMEM)] * (1 + SIDE),
-        out_specs=pl.BlockSpec(memory_space=pltpu.VMEM),
-        cost_estimate=pl.CostEstimate(flops=1 << 29, bytes_accessed=3 << 20, transcendentals=0),
-        compiler_params=pltpu.CompilerParams(vmem_limit_bytes=VMEM_LIMIT),
-        name="their_keys",
-    )(place, after, theirs, *weights)
-
-
-def own_keys_kernel(place_ref, inputs_ref, other_ref, *refs):
-    total = 0.0
-    for offset in range(SIDE):
-        chunk = lax.rem(place_ref[0] + SIDE - offset, SIDE)
-        columns = core_columns(inputs_ref, place_ref[1], chunk)
-        total += jnp.dot(columns, refs[offset][...], preferred_element_type=f32)
-    refs[-1][0] = (total * SCALE + other_ref[...].astype(f32)).astype(bf16)
-
-
-def own_keys(place, inputs, weights, other):
-    tokens = inputs.shape[0]
-    features = weights[0].shape[1]
-    return pl.pallas_call(
-        own_keys_kernel,
-        out_shape=jax.ShapeDtypeStruct((1, tokens, features), bf16),
-        in_specs=[pl.BlockSpec(memory_space=pltpu.SMEM)]
-        + [pl.BlockSpec(memory_space=pltpu.VMEM)] * (2 + SIDE),
-        out_specs=pl.BlockSpec(memory_space=pltpu.VMEM),
-        cost_estimate=pl.CostEstimate(flops=1 << 29, bytes_accessed=4 << 20, transcendentals=0),
-        compiler_params=pltpu.CompilerParams(vmem_limit_bytes=VMEM_LIMIT),
-        name="own_keys",
-    )(place, inputs, other, *weights)
-
-
-def update_kernel(parts_ref, layers_ref, out_ref):
-    gradient = parts_ref[0].astype(f32)
-    for other in range(1, SIDE):
-        gradient += parts_ref[other].astype(f32)
-    out_ref[0, 0] = layers_ref[0, 0] - inner_rate * gradient
+        rows[offset].wait()
+        own += jnp.dot(
+            core_columns(inputs, place_ref[1], chunk), weights[offset], preferred_element_type=f32
+        )
+        other += jnp.dot(
+            core_columns(theirs, place_ref[1], chunk), weights[offset], preferred_element_type=f32
+        )
+    own_ref[...] = own * SCALE
+    other_ref[...] = (other * SCALE).astype(bf16)
+
+
+def half_keys(place, inputs, theirs, weights):
+    tokens, width = inputs.shape
+    rows, features = weights[0].shape
+    anywhere = pl.BlockSpec(memory_space=pl.ANY)
+    whole = pl.BlockSpec(memory_space=pltpu.VMEM)
+    return pl.pallas_call(
+        keys_kernel,
+        out_shape=(
+            jax.ShapeDtypeStruct((tokens, features), f32),
+            jax.ShapeDtypeStruct((tokens, features), bf16),
+        ),
+        in_specs=[pl.BlockSpec(memory_space=pltpu.SMEM)] + [anywhere] * (2 + SIDE),
+        out_specs=(whole, whole),
+        scratch_shapes=[
+            pltpu.VMEM((tokens, width), bf16),
+            pltpu.VMEM((tokens, width), bf16),
+            pltpu.VMEM((SIDE, rows, features), bf16),
+            pltpu.SemaphoreType.DMA((SIDE + 2,)),
+        ],
+        cost_estimate=pl.CostEstimate(flops=1 << 30, bytes_accessed=7 << 20, transcendentals=0),
+        compiler_params=pltpu.CompilerParams(vmem_limit_bytes=GRAD_VMEM_LIMIT),
+        name="half_keys",
+    )(place, inputs, theirs, *weights)
+
+
+def update_kernel(gradient_ref, layers_ref, out_ref):
+    out_ref[0, 0] = layers_ref[0, 0] - inner_rate * gradient_ref[...]
     for layer in range(1, layers_ref.shape[1]):
         out_ref[0, layer] = layers_ref[0, layer]
 
 
-def update(parts, local_weight):
+def update(gradient, local_weight):
     count, rows, features = local_weight.shape[1:]
     steps = 2
     block = rows // steps
@@ -169,32 +178,60 @@
         update_kernel,
         out_shape=jax.ShapeDtypeStruct(local_weight.shape, f32),
         grid=(steps,),
-        in_specs=[pl.BlockSpec((SIDE, block, features), lambda i: (0, i, 0)), layers],
+        in_specs=[pl.BlockSpec((block, features), lambda i: (i, 0)), layers],
         out_specs=layers,
         cost_estimate=pl.CostEstimate(flops=1 << 19, bytes_accessed=2 << 20, transcendentals=0),
         compiler_params=pltpu.CompilerParams(vmem_limit_bytes=VMEM_LIMIT),
         name="update",
-    )(parts, local_weight)
+    )(gradient, local_weight)
 
 
 def settle_kernel(
-    chosen_ref, average_ref, layer_ref, outer_ref, moment_ref, layer_out, outer_out, moment_out
+    chosen_ref,
+    average_hbm,
+    layers_hbm,
+    outer_hbm,
+    moment_hbm,
+    layers_out,
+    outer_out,
+    moment_out,
+    average,
+    olds,
+    news,
+    in_sems,
+    out_sems,
 ):
-    average = average_ref[...].astype(f32)
-    moment = momentum_factor * moment_ref[0] + average
-    outer = outer_ref[0] - outer_rate * (average + momentum_factor * moment)
-    moment_out[...] = moment
-    outer_out[...] = outer
-    layer_out[0, 0] = mixing * layer_ref[0, 0] + (1.0 - mixing) * outer
+    chosen = chosen_ref[0]
+    loads = [
+        pltpu.make_async_copy(moment_hbm.at[chosen], olds.at[0], in_sems.at[0]),
+        pltpu.make_async_copy(average_hbm, average, in_sems.at[1]),
+        pltpu.make_async_copy(outer_hbm.at[chosen], olds.at[1], in_sems.at[2]),
+        pltpu.make_async_copy(layers_hbm.at[0, chosen], olds.at[2], in_sems.at[3]),
+    ]
+    stores = [
+        pltpu.make_async_copy(news.at[0], moment_out, out_sems.at[0]),
+        pltpu.make_async_copy(news.at[1], outer_out, out_sems.at[1]),
+        pltpu.make_async_copy(news.at[2], layers_out.at[0, chosen], out_sems.at[2]),
+    ]
+    for load in loads:
+        load.start()
+    loads[0].wait()
+    loads[1].wait()
+    news[0] = momentum_factor * olds[0] + average[...].astype(f32)
+    stores[0].start()
+    loads[2].wait()
+    news[1] = olds[1] - outer_rate * (average[...].astype(f32) + momentum_factor * news[0])
+    stores[1].start()
+    loads[3].wait()
+    news[2] = mixing * olds[2] + (1.0 - mixing) * news[1]
+    stores[2].start()
+    for store in stores:
+        store.wait()
 
 
 def settle(chosen, average, updated, outer_weight, outer_moment):
     rows, features = updated.shape[2:]
-    steps = 2
-    block = rows // steps
-    picked = pl.BlockSpec((1, block, features), lambda i, chosen: (chosen[0], i, 0))
-    layer = pl.BlockSpec((1, 1, block, features), lambda i, chosen: (0, chosen[0], i, 0))
-    flat = pl.BlockSpec((block, features), lambda i, chosen: (i, 0))
+    anywhere = pl.BlockSpec(memory_space=pl.ANY)
     return pl.pallas_call(
         settle_kernel,
         out_shape=(
@@ -202,12 +239,15 @@
             jax.ShapeDtypeStruct((rows, features), f32),
             jax.ShapeDtypeStruct((rows, features), f32),
         ),
-        grid_spec=pltpu.PrefetchScalarGridSpec(
-            num_scalar_prefetch=1,
-            grid=(steps,),
-            in_specs=[flat, layer, picked, picked],
-            out_specs=(layer, flat, flat),
-        ),
+        in_specs=[pl.BlockSpec(memory_space=pltpu.SMEM)] + [anywhere] * 4,
+        out_specs=(anywhere,) * 3,
+        scratch_shapes=[
+            pltpu.VMEM((rows, features), average.dtype),
+            pltpu.VMEM((3, rows, features), f32),
+            pltpu.VMEM((3, rows, features), f32),
+            pltpu.SemaphoreType.DMA((4,)),
+            pltpu.SemaphoreType.DMA((3,)),
+        ],
         input_output_aliases={2: 0},
         cost_estimate=pl.CostEstimate(flops=1 << 20, bytes_accessed=2 << 20, transcendentals=0),
         compiler_params=pltpu.CompilerParams(vmem_limit_bytes=VMEM_LIMIT),
@@ -233,20 +273,18 @@
 swap = [(0, 1), (1, 0)]
 
 
-def shards(activations, cotangent, local_weight, outer_weight, outer_moment, fragment_index):
+def trained_step(activations, cotangent, local_weight, outer_weight, outer_moment, fragment_index):
     inputs = activations[0]
     upstream = cotangent[0]
     layers = local_weight[0]
     features = upstream.shape[1]
-    chosen = fragment_index[0]
     place = jnp.stack([lax.axis_index(name) for name in ("x", "c")]).astype(jnp.int32)
 
     theirs = lax.ppermute(inputs, "c", swap)
     their_up = lax.ppermute(upstream, "c", swap)
     part = grad(place, inputs, theirs, upstream, their_up)
     rows = lax.all_gather(cast(layers, part), "zl", axis=0, tiled=True)
-    pick = lambda array: lax.dynamic_index_in_dim(array, chosen, 0, keepdims=False)
-    delta = pick(outer_weight) - pick(layers)
+    delta = outer_weight[0] - layers[0]
     part = lax.all_to_all(part, "x", 0, 0)
     part, rows, delta = lax.optimization_barrier((part, rows, delta))
 
@@ -254,20 +292,79 @@
     part = lax.all_to_all(part, "zl", 0, 0)
     weights = [rows] + [lax.ppermute(rows, "x", shift(offset)) for offset in (1, 2, 3)]
 
-    mean = delta + jnp.where(chosen == 0, inner_rate, 0.0) * sum_all(part)
+    gradient = sum_all(part)
+    mean = delta + inner_rate * gradient
     mean = mean.astype(bf16).reshape(SIDE, QUARTER, features)
     mean = sum_all(lax.all_to_all(mean, "y", 0, 0)) * (1.0 / (SIDE * SIDE))
     mean, weights[1], weights[3] = lax.optimization_barrier((mean, weights[1], weights[3]))
     mean = sum_all(lax.all_to_all(spread(mean), "zh", 0, 0))
+    mean, gradient = lax.optimization_barrier((mean, gradient))
     mean = lax.all_to_all(spread(mean), "y", 0, 0).reshape(PIECE, features)
 
-    updated = update(part, local_weight)
-    other = lax.ppermute(their_keys(place, theirs, weights, updated), "c", swap)
-    keys = own_keys(place, inputs, weights, other)
+    own, other = half_keys(place, inputs, theirs, weights)
+    other = lax.ppermute(other, "c", swap)
+    keys = (own + other.astype(f32)).astype(bf16)[None]
+    updated = update(gradient, local_weight)
     local_new, outer_new, moment_new = settle(
         fragment_index, mean, updated, outer_weight, outer_moment
     )
     return keys, local_new, outer_new, moment_new
+
+
+def flip(mask):
+    return [(source, source ^ mask) for source in range(SIDE)]
+
+
+def other_step(activations, cotangent, local_weight, outer_weight, outer_moment, fragment_index):
+    inputs = activations[0]
+    upstream = cotangent[0]
+    layers = local_weight[0]
+    features = upstream.shape[1]
+    place = jnp.stack([lax.axis_index(name) for name in ("x", "c")]).astype(jnp.int32)
+
+    theirs = lax.ppermute(inputs, "c", swap)
+    their_up = lax.ppermute(upstream, "c", swap)
+    part = grad(place, inputs, theirs, upstream, their_up)
+    rows = lax.all_gather(cast(layers, part), "zl", axis=0, tiled=True)
+    pick = lambda array: lax.dynamic_index_in_dim(array, fragment_index[0], 0, keepdims=False)
+    delta = (pick(outer_weight) - pick(layers)).astype(bf16).reshape(SIDE, QUARTER, features)
+    part = lax.all_to_all(part, "x", 0, 0)
+    part, rows, delta = lax.optimization_barrier((part, rows, delta))
+    weights = [rows] + [lax.ppermute(rows, "x", shift(offset)) for offset in (1, 2, 3)]
+
+    mean = sum_all(lax.all_to_all(delta, "y", 0, 0)) * (1.0 / (SIDE * SIDE))
+    part = sum_all(part).astype(bf16).reshape(SIDE, PIECE, features)
+    mean = sum_all(lax.all_to_all(spread(mean), "zh", 0, 0))
+    mean = lax.all_to_all(spread(mean), "y", 0, 0).reshape(PIECE, features)
+
+    along = lax.axis_index("zl")
+    chunk = lambda mask: lax.dynamic_index_in_dim(part, along ^ mask, 0, keepdims=False)
+    gradient = sum_all(
+        jnp.stack([chunk(0)] + [lax.ppermute(chunk(mask), "zl", flip(mask)) for mask in (1, 2, 3)])
+    )
+
+    own, other = half_keys(place, inputs, theirs, weights)
+    other = lax.ppermute(other, "c", swap)
+    keys = (own + other.astype(f32)).astype(bf16)[None]
+    updated = update(gradient, local_weight)
+    local_new, outer_new, moment_new = settle(
+        fragment_index, mean, updated, outer_weight, outer_moment
+    )
+    return keys, local_new, outer_new, moment_new
+
+
+def shards(activations, cotangent, local_weight, outer_weight, outer_moment, fragment_index):
+    return lax.cond(
+        fragment_index[0] == 0,
+        trained_step,
+        other_step,
+        activations,
+        cotangent,
+        local_weight,
+        outer_weight,
+        outer_moment,
+        fragment_index,
+    )
 
 
 def solution(mesh):

time: 117 us -> 111 us (0.949)
  the two profiles are of different devices: /device:TPU:2 before, /device:TPU:1 now
where the time goes in v4:
time: 111 us; the launch traced here: 110 us
  starting transfers between devices  56.3 us (51%)
  Pallas kernels  14.9 us (13%)
  blocking collectives  13.8 us (12%)
  waiting for transfers between devices  13.5 us (12%)
  other arithmetic  5.05 us (5%)
  local copies, waits for them, and re-layouts  2.94 us (3%)
  loops' own time  2.26 us (2%)
  between operations  1.28 us (1%)
    all_gather x1, blocking collectives, other_step(): rows = lax.all_gather(cast(layers, part), 'zl', axis=0, tiled=True)  13.8 us
    all_to_all x1, starting transfers between devices, other_step(): mean = sum_all(lax.all_to_all(spread(mean), 'zh', 0, 0))  10.3 us
    ppermute x3, starting transfers between devices, other_step(): lax.ppermute(chunk(mask), 'zl', flip(mask))  9.26 us
    all_to_all x1, waiting for transfers between devices, other_step(): part = lax.all_to_all(part, 'x', 0, 0)  8.99 us
    ppermute x1, starting transfers between devices, other_step(): theirs = lax.ppermute(inputs, 'c', swap)  8.79 us
    ppermute x3, starting transfers between devices, other_step(): lax.ppermute(rows, 'x', shift(offset))  8.42 us
    pallas_call x1, Pallas kernels, half_keys(): pl.pallas_call(keys_kernel, out_shape=(jax.ShapeDtypeStruct((tokens, feat...  5.42 us
    ppermute x1, starting transfers between devices, other_step(): other = lax.ppermute(other, 'c', swap)  5.17 us
  transfers between devices with their start and end apart: 13, of which 3 were waited for; matrix products, arithmetic and copies ran while one was open for 6% of the time, Pallas kernels for 9%

profile of v4, /device:TPU:1, one launch (start us, length us, event | category | flops | bytes accessed | tf_op | source)
XLA Modules:
  0.0 109.9 jit_solution(947811979664018371)
XLA Ops:
  1.3 108.6 %conditional.1 = (f32[1,3,128,512]{3,2,1,0:T(8,128)}, f32[128,512]{1,0:T(8,128)}, f32[128,512]{1,0:T(8,128)}, bf16[1,256,512]{2,1,0:T(8,128)(2,1)}) conditional(s32[]{:T(128)} %bitcast.32, (bf16[1,256,4096]{2,1,0:T(8,128)(2,1)}, bf16[1,256,512]{2,1,0:T(8,128)(2,1)}, f32[1,3,128,512]{3,2,1,0:T(8,128)}, s32[1]{0:T(128)}, f32[3,128,512]{2,1,0:T(8,128)}, ...), branch_computations={%region_0.1_spmd, %region_1.2_spmd} | conditional | flops 2152546304 | bytes 69731344 | solution.py:357
  1.3 8.8 %collective-permute-start = (bf16[256,4096]{1,0:T(8,128)(2,1)}, bf16[256,4096]{1,0:T(8,128)(2,1)}, u32[]{:S(2)}, u32[]{:S(2)}) collective-permute-start(bf16[256,4096]{1,0:T(8,128)(2,1)} %bitcast.49), channel_id=1, source_target_pairs={{0,1},{1,0},{2,3},{3,2},{4,5},{5,4},{6,7},{7,6},{8,9},{9,8},{10,11... | collective-permute-start | bytes 6291464 | tf_op jit(solution)/shard_map/cond/branch_0_fun/ppermute | solution.py:325
  10.1 1.9 %collective-permute-start.1 = (bf16[256,512]{1,0:T(8,128)(2,1)}, bf16[256,512]{1,0:T(8,128)(2,1)S(1)}, u32[]{:S(2)}, u32[]{:S(2)}) collective-permute-start(bf16[256,512]{1,0:T(8,128)(2,1)} %bitcast.59), channel_id=1, source_target_pairs={{0,1},{1,0},{2,3},{3,2},{4,5},{5,4},{6,7},{7,6},{8,9},{9,8},{10,11... | collective-permute-start | bytes 786440 | tf_op jit(solution)/shard_map/cond/branch_0_fun/ppermute | solution.py:326
  12.0 0.7 pad_add_fusion.place_ref
  12.7 1.8 %collective-permute-done.1.their_up_hbm = bf16[256,512]{1,0:T(8,128)(2,1)S(1)} collective-permute-done((bf16[256,512]{1,0:T(8,128)(2,1)}, bf16[256,512]{1,0:T(8,128)(2,1)S(1)}, u32[]{:S(2)}, u32[]{:S(2)}) %collective-permute-start.1) | collective-permute-done | bytes 262176 | tf_op jit(solution)/shard_map/cond/branch_0_fun/ppermute | solution.py:326
  14.4 0.0 collective-permute-done.theirs_hbm
  14.4 0.7 copy-done.11
  15.1 5.1 %gradient.2.after_ref = bf16[4,512,512]{2,1,0:T(8,128)(2,1)} custom-call(s32[2]{0:T(128)} %pad_add_fusion.place_ref, bf16[256,4096]{1,0:T(8,128)(2,1)} %bitcast.50, bf16[256,4096]{1,0:T(8,128)(2,1)} %collective-permute-done.theirs_hbm, bf16[256,512]{1,0:T(8,128)(2,1)} %bitcast.60, bf16[256,512]{1,0:T(8,128)(2,1)} %copy-done.11), custom_call_target="tpu_custom_call" | custom-call | flops 1073741824 | bytes 6291456 | tf_op jit(solution)/shard_map/cond/branch_0_fun/gradient/pallas_call | solution.py:68
  20.3 0.0 copy-start.2
  20.3 0.0 copy-start
  20.3 4.6 %all-to-all-start = ((bf16[4,512,512]{2,1,0:T(8,128)(2,1)}), bf16[4,512,512]{2,1,0:T(8,128)(2,1)}, u32[]{:S(2)}, u32[]{:S(2)}) async-start(bf16[4,512,512]{2,1,0:T(8,128)(2,1)} %gradient.2.after_ref), calls=%async_computation | async-start | bytes 4194304 | tf_op jit(solution)/shard_map/cond/branch_0_fun/all_to_all | solution.py:331
  26.9 0.0 copy-done
  26.9 0.7 subtract_convert_fusion
  27.6 0.7 cast_weights.2
  28.3 13.8 %all_gather.4.w0_hbm = bf16[512,512]{1,0:T(8,128)(2,1)S(1)} all-gather(bf16[128,512]{1,0:T(8,128)(2,1)} %cast_weights.2), channel_id=1, replica_groups=mesh['zh'=4,'y'=4,'x'=4,'zl'=4,'c'=2] {'zl'}, dimensions={0}, use_global_device_ids=true | all-gather | bytes 655360 | tf_op jit(solution)/shard_map/cond/branch_0_fun/all_gather | solution.py:328
  42.1 9.0 %all-to-all-done = bf16[4,512,512]{2,1,0:T(8,128)(2,1)} async-done(((bf16[4,512,512]{2,1,0:T(8,128)(2,1)}), bf16[4,512,512]{2,1,0:T(8,128)(2,1)}, u32[]{:S(2)}, u32[]{:S(2)}) %all-to-all-start) | async-done | bytes 2097184 | tf_op jit(solution)/shard_map/cond/branch_0_fun/all_to_all | solution.py:331
  51.0 3.3 %all-to-all-start.1 = ((bf16[4,32,512]{2,1,0:T(8,128)(2,1)}), bf16[4,32,512]{2,1,0:T(8,128)(2,1)S(1)}, u32[]{:S(2)}, u32[]{:S(2)}) async-start(bf16[4,32,512]{2,1,0:T(8,128)(2,1)} %subtract_convert_fusion), calls=%async_computation.1 | async-start | bytes 262144 | tf_op jit(solution)/shard_map/cond/branch_0_fun/all_to_all | solution.py:335
  54.4 2.2 %collective-permute-start.2 = (bf16[512,512]{1,0:T(8,128)(2,1)S(1)}, bf16[512,512]{1,0:T(8,128)(2,1)}, u32[]{:S(2)}, u32[]{:S(2)}) collective-permute-start(bf16[512,512]{1,0:T(8,128)(2,1)S(1)} %all_gather.4.w0_hbm), channel_id=1, source_target_pairs={{0,8},{8,16},{16,24},{24,0},{1,9},{9,17},{17,25},{25,1},{2,10},{10... | collective-permute-start | bytes 1572872 | tf_op jit(solution)/shard_map/cond/branch_0_fun/ppermute | solution.py:333
  56.6 3.7 %collective-permute-start.3 = (bf16[512,512]{1,0:T(8,128)(2,1)S(1)}, bf16[512,512]{1,0:T(8,128)(2,1)}, u32[]{:S(2)}, u32[]{:S(2)}) collective-permute-start(bf16[512,512]{1,0:T(8,128)(2,1)S(1)} %all_gather.4.w0_hbm), channel_id=1, source_target_pairs={{0,16},{8,24},{16,0},{24,8},{1,17},{9,25},{17,1},{25,9},{2,18},{10... | collective-permute-start | bytes 1572872 | tf_op jit(solution)/shard_map/cond/branch_0_fun/ppermute | solution.py:333
  60.3 2.5 %collective-permute-start.4 = (bf16[512,512]{1,0:T(8,128)(2,1)S(1)}, bf16[512,512]{1,0:T(8,128)(2,1)}, u32[]{:S(2)}, u32[]{:S(2)}) collective-permute-start(bf16[512,512]{1,0:T(8,128)(2,1)S(1)} %all_gather.4.w0_hbm), channel_id=1, source_target_pairs={{0,24},{8,0},{16,8},{24,16},{1,25},{9,1},{17,9},{25,17},{2,26},{10... | collective-permute-start | bytes 1572872 | tf_op jit(solution)/shard_map/cond/branch_0_fun/ppermute | solution.py:333
  62.8 0.0 all-to-all-done.1
  62.9 0.7 broadcast_in_dim.19
  63.5 10.3 %all-to-all-start.2 = ((bf16[4,32,512]{2,1,0:T(8,128)(2,1)}), bf16[4,32,512]{2,1,0:T(8,128)(2,1)S(1)}, u32[]{:S(2)}, u32[]{:S(2)}) async-start(bf16[4,32,512]{2,1,0:T(8,128)(2,1)} %broadcast_in_dim.19), calls=%async_computation.2 | async-start | bytes 262144 | tf_op jit(solution)/shard_map/cond/branch_0_fun/all_to_all | solution.py:337
  73.8 1.8 %add_convert_fusion = bf16[1,512,512]{2,1,0:T(8,128)(2,1)S(1)} fusion(bf16[4,512,512]{2,1,0:T(8,128)(2,1)} %all-to-all-done), kind=kLoop, calls=%fused_computation | loop fusion | flops 2097152 | bytes 2621440 | tf_op jit(solution)/shard_map/cond/branch_0_fun/convert_element_type | solution.py:336
  75.6 0.0 copy-start.8
  75.6 0.8 dynamic-slice_bitcast_fusion.2
  76.4 3.5 %collective-permute-start.8 = (bf16[128,512]{1,0:T(8,128)(2,1)}, bf16[128,512]{1,0:T(8,128)(2,1)S(1)}, u32[]{:S(2)}, u32[]{:S(2)}) collective-permute-start(bf16[128,512]{1,0:T(8,128)(2,1)} %get-tuple-element.65), channel_id=1, source_target_pairs={{0,6},{2,4},{4,2},{6,0},{1,7},{3,5},{5,3},{7,1},{8,14},{10,12},{12... | collective-permute-start | bytes 393224 | tf_op jit(solution)/shard_map/cond/branch_0_fun/ppermute | solution.py:343
  80.0 2.2 %collective-permute-start.7 = (bf16[128,512]{1,0:T(8,128)(2,1)}, bf16[128,512]{1,0:T(8,128)(2,1)}, u32[]{:S(2)}, u32[]{:S(2)}) collective-permute-start(bf16[128,512]{1,0:T(8,128)(2,1)} %get-tuple-element.66), channel_id=1, source_target_pairs={{0,4},{2,6},{4,0},{6,2},{1,5},{3,7},{5,1},{7,3},{8,12},{10,14},{12... | collective-permute-start | bytes 393224 | tf_op jit(solution)/shard_map/cond/branch_0_fun/ppermute | solution.py:343
  82.2 0.0 collective-permute-done.2.w1_hbm
  82.2 3.6 %collective-permute-start.6 = (bf16[128,512]{1,0:T(8,128)(2,1)S(1)}, bf16[128,512]{1,0:T(8,128)(2,1)}, u32[]{:S(2)}, u32[]{:S(2)}) collective-permute-start(bf16[128,512]{1,0:T(8,128)(2,1)S(1)} %get-tuple-element.64), channel_id=1, source_target_pairs={{0,2},{2,0},{4,6},{6,4},{1,3},{3,1},{5,7},{7,5},{8,10},{10,8},{12,... | collective-permute-start | bytes 393224 | tf_op jit(solution)/shard_map/cond/branch_0_fun/ppermute | solution.py:343
  85.7 0.0 collective-permute-done.3.w2_hbm
  85.8 0.0 collective-permute-done.4.w3_hbm
  85.8 5.4 %half_keys.2 = (f32[256,512]{1,0:T(8,128)}, bf16[256,512]{1,0:T(8,128)(2,1)}) custom-call(s32[2]{0:T(128)} %pad_add_fusion.place_ref, bf16[256,4096]{1,0:T(8,128)(2,1)} %bitcast.51, bf16[256,4096]{1,0:T(8,128)(2,1)} %collective-permute-done.theirs_hbm, bf16[512,512]{1,0:T(8,128)(2,1)} %copy-done.6, bf16[512,512]{1,0:T(8,128)(2,1)} %collective-permute-done.2.w1_hbm, ...), custom_call_target="tpu_custom_call" | custom-call | flops 1073741824 | bytes 7340032 | tf_op jit(solution)/shard_map/cond/branch_0_fun/half_keys/pallas_call | solution.py:146
  91.2 0.0 copy-start.4
  91.2 5.2 %collective-permute-start.5 = (bf16[256,512]{1,0:T(8,128)(2,1)}, bf16[256,512]{1,0:T(8,128)(2,1)S(1)}, u32[]{:S(2)}, u32[]{:S(2)}) collective-permute-start(bf16[256,512]{1,0:T(8,128)(2,1)} %get-tuple-element.31), channel_id=1, source_target_pairs={{0,1},{1,0},{2,3},{3,2},{4,5},{5,4},{6,7},{7,6},{8,9},{9,8},{10,11... | collective-permute-start | bytes 786440 | tf_op jit(solution)/shard_map/cond/branch_0_fun/ppermute | solution.py:347
  96.4 0.0 all-to-all-done.2
  96.4 0.7 broadcast_in_dim.21
  97.1 4.5 %all-to-all-start.3 = ((bf16[4,32,512]{2,1,0:T(8,128)(2,1)}), bf16[4,32,512]{2,1,0:T(8,128)(2,1)S(1)}, u32[]{:S(2)}, u32[]{:S(2)}) async-start(bf16[4,32,512]{2,1,0:T(8,128)(2,1)} %broadcast_in_dim.21), calls=%async_computation.3 | async-start | bytes 262144 | tf_op jit(solution)/shard_map/cond/branch_0_fun/all_to_all | solution.py:338
  101.6 0.0 collective-permute-done.8
  101.6 0.0 collective-permute-done.7
  101.6 0.0 collective-permute-done.6
  101.6 1.1 %fusion.1.gradient_ref = f32[128,512]{1,0:T(8,128)S(1)} fusion(bf16[128,512]{1,0:T(8,128)(2,1)S(1)} %collective-permute-done.8, bf16[128,512]{1,0:T(8,128)(2,1)} %collective-permute-done.7, bf16[128,512]{1,0:T(8,128)(2,1)} %collective-permute-done.6, bf16[4,128,512]{2,1,0:T(8,128)(2,1)} %bitcast.58, s32[]{:T(128)S(6)} %select_n.14), kind=kLoop, calls=%fused_computation.4 | loop fusion | flops 458752 | bytes 786436 | tf_op jit(solution)/shard_map/cond/branch_0_fun/add | solution.py:261
  102.7 1.0 update.2.layers_hbm
  103.7 2.7 %all-to-all-done.3 = bf16[4,32,512]{2,1,0:T(8,128)(2,1)S(1)} async-done(((bf16[4,32,512]{2,1,0:T(8,128)(2,1)}), bf16[4,32,512]{2,1,0:T(8,128)(2,1)S(1)}, u32[]{:S(2)}, u32[]{:S(2)}) %all-to-all-start.3) | async-done | bytes 131104 | tf_op jit(solution)/shard_map/cond/branch_0_fun/all_to_all | solution.py:338
  106.5 0.0 copy-done.4
  106.5 2.7 %settle.2 = (f32[1,3,128,512]{3,2,1,0:T(8,128)}, f32[128,512]{1,0:T(8,128)}, f32[128,512]{1,0:T(8,128)}) custom-call(s32[1]{0:T(128)} %get-tuple-element.28.chosen_ref, bf16[128,512]{1,0:T(8,128)(2,1)S(1)} %bitcast.47, f32[1,3,128,512]{3,2,1,0:T(8,128)} %update.2.layers_hbm, f32[3,128,512]{2,1,0:T(8,128)S(1)} %copy-done.2, ...), custom_call_target="tpu_custom_call", output_to_operand_aliasing={{0}: (2, {})} | custom-call | flops 1048576 | bytes 2097152 | tf_op jit(solution)/shard_map/cond/branch_0_fun/settle/pallas_call | solution.py:235
  109.1 0.0 collective-permute-done.5
  109.2 0.8 fusion
  (11 shorter events, 0.1 us)
Async XLA Ops:
  1.3 13.2 %collective-permute-start = (bf16[256,4096]{1,0:T(8,128)(2,1)}, bf16[256,4096]{1,0:T(8,128)(2,1)}, u32[]{:S(2)}, u32[]{:S(2)}) collective-permute-start(bf16[256,4096]{1,0:T(8,128)(2,1)} %bitcast.49), channel_id=1, source_target_pairs={{0,1},{1,0},{2,3},{3,2},{4,5},{5,4},{6,7},{7,6},{8,9},{9,8},{10,11... | collective-permute-start | bytes 6291464 | tf_op jit(solution)/shard_map/cond/branch_0_fun/ppermute | solution.py:325
  10.1 4.3 %collective-permute-start.1 = (bf16[256,512]{1,0:T(8,128)(2,1)}, bf16[256,512]{1,0:T(8,128)(2,1)S(1)}, u32[]{:S(2)}, u32[]{:S(2)}) collective-permute-start(bf16[256,512]{1,0:T(8,128)(2,1)} %bitcast.59), channel_id=1, source_target_pairs={{0,1},{1,0},{2,3},{3,2},{4,5},{5,4},{6,7},{7,6},{8,9},{9,8},{10,11... | collective-permute-start | bytes 786440 | tf_op jit(solution)/shard_map/cond/branch_0_fun/ppermute | solution.py:326
  14.4 0.7 copy-start.11
  20.3 6.6 %copy-start.2 = (f32[3,128,512]{2,1,0:T(8,128)S(1)}, f32[3,128,512]{2,1,0:T(8,128)}, u32[]{:S(2)}) copy-start(f32[3,128,512]{2,1,0:T(8,128)} %get-tuple-element.27.outer_hbm) | copy-start | bytes 2359300 | tf_op jit(solution)/shard_map/cond
  20.3 6.6 %copy-start = (f32[1,3,128,512]{3,2,1,0:T(8,128)S(1)}, f32[1,3,128,512]{3,2,1,0:T(8,128)}, u32[]{:S(2)}) copy-start(f32[1,3,128,512]{3,2,1,0:T(8,128)} %get-tuple-element.26.layers_ref) | copy-start | bytes 2359300 | tf_op jit(solution)/shard_map/cond
  20.3 30.7 %all-to-all-start = ((bf16[4,512,512]{2,1,0:T(8,128)(2,1)}), bf16[4,512,512]{2,1,0:T(8,128)(2,1)}, u32[]{:S(2)}, u32[]{:S(2)}) async-start(bf16[4,512,512]{2,1,0:T(8,128)(2,1)} %gradient.2.after_ref), calls=%async_computation | async-start | bytes 4194304 | tf_op jit(solution)/shard_map/cond/branch_0_fun/all_to_all | solution.py:331
  42.0 34.4 %copy-start.6 = (bf16[512,512]{1,0:T(8,128)(2,1)}, bf16[512,512]{1,0:T(8,128)(2,1)S(1)}, u32[]{:S(2)}) copy-start(bf16[512,512]{1,0:T(8,128)(2,1)S(1)} %all_gather.4.w0_hbm) | copy-start | bytes 1572868 | tf_op jit(solution)/shard_map/cond
  51.0 11.8 %all-to-all-start.1 = ((bf16[4,32,512]{2,1,0:T(8,128)(2,1)}), bf16[4,32,512]{2,1,0:T(8,128)(2,1)S(1)}, u32[]{:S(2)}, u32[]{:S(2)}) async-start(bf16[4,32,512]{2,1,0:T(8,128)(2,1)} %subtract_convert_fusion), calls=%async_computation.1 | async-start | bytes 262144 | tf_op jit(solution)/shard_map/cond/branch_0_fun/all_to_all | solution.py:335
  54.4 27.8 %collective-permute-start.2 = (bf16[512,512]{1,0:T(8,128)(2,1)S(1)}, bf16[512,512]{1,0:T(8,128)(2,1)}, u32[]{:S(2)}, u32[]{:S(2)}) collective-permute-start(bf16[512,512]{1,0:T(8,128)(2,1)S(1)} %all_gather.4.w0_hbm), channel_id=1, source_target_pairs={{0,8},{8,16},{16,24},{24,0},{1,9},{9,17},{17,25},{25,1},{2,10},{10... | collective-permute-start | bytes 1572872 | tf_op jit(solution)/shard_map/cond/branch_0_fun/ppermute | solution.py:333
  56.6 29.1 %collective-permute-start.3 = (bf16[512,512]{1,0:T(8,128)(2,1)S(1)}, bf16[512,512]{1,0:T(8,128)(2,1)}, u32[]{:S(2)}, u32[]{:S(2)}) collective-permute-start(bf16[512,512]{1,0:T(8,128)(2,1)S(1)} %all_gather.4.w0_hbm), channel_id=1, source_target_pairs={{0,16},{8,24},{16,0},{24,8},{1,17},{9,25},{17,1},{25,9},{2,18},{10... | collective-permute-start | bytes 1572872 | tf_op jit(solution)/shard_map/cond/branch_0_fun/ppermute | solution.py:333
  60.3 25.5 %collective-permute-start.4 = (bf16[512,512]{1,0:T(8,128)(2,1)S(1)}, bf16[512,512]{1,0:T(8,128)(2,1)}, u32[]{:S(2)}, u32[]{:S(2)}) collective-permute-start(bf16[512,512]{1,0:T(8,128)(2,1)S(1)} %all_gather.4.w0_hbm), channel_id=1, source_target_pairs={{0,24},{8,0},{16,8},{24,16},{1,25},{9,1},{17,9},{25,17},{2,26},{10... | collective-permute-start | bytes 1572872 | tf_op jit(solution)/shard_map/cond/branch_0_fun/ppermute | solution.py:333
  63.5 32.8 %all-to-all-start.2 = ((bf16[4,32,512]{2,1,0:T(8,128)(2,1)}), bf16[4,32,512]{2,1,0:T(8,128)(2,1)S(1)}, u32[]{:S(2)}, u32[]{:S(2)}) async-start(bf16[4,32,512]{2,1,0:T(8,128)(2,1)} %broadcast_in_dim.19), calls=%async_computation.2 | async-start | bytes 262144 | tf_op jit(solution)/shard_map/cond/branch_0_fun/all_to_all | solution.py:337
  75.6 10.2 %copy-start.8 = (bf16[1,512,512]{2,1,0:T(8,128)(2,1)}, bf16[1,512,512]{2,1,0:T(8,128)(2,1)S(1)}, u32[]{:S(2)}) copy-start(bf16[1,512,512]{2,1,0:T(8,128)(2,1)S(1)} %add_convert_fusion) | copy-start | bytes 1572868 | tf_op jit(solution)/shard_map/cond
  76.4 25.2 %collective-permute-start.8 = (bf16[128,512]{1,0:T(8,128)(2,1)}, bf16[128,512]{1,0:T(8,128)(2,1)S(1)}, u32[]{:S(2)}, u32[]{:S(2)}) collective-permute-start(bf16[128,512]{1,0:T(8,128)(2,1)} %get-tuple-element.65), channel_id=1, source_target_pairs={{0,6},{2,4},{4,2},{6,0},{1,7},{3,5},{5,3},{7,1},{8,14},{10,12},{12... | collective-permute-start | bytes 393224 | tf_op jit(solution)/shard_map/cond/branch_0_fun/ppermute | solution.py:343
  80.0 21.6 %collective-permute-start.7 = (bf16[128,512]{1,0:T(8,128)(2,1)}, bf16[128,512]{1,0:T(8,128)(2,1)}, u32[]{:S(2)}, u32[]{:S(2)}) collective-permute-start(bf16[128,512]{1,0:T(8,128)(2,1)} %get-tuple-element.66), channel_id=1, source_target_pairs={{0,4},{2,6},{4,0},{6,2},{1,5},{3,7},{5,1},{7,3},{8,12},{10,14},{12... | collective-permute-start | bytes 393224 | tf_op jit(solution)/shard_map/cond/branch_0_fun/ppermute | solution.py:343
  82.2 19.4 %collective-permute-start.6 = (bf16[128,512]{1,0:T(8,128)(2,1)S(1)}, bf16[128,512]{1,0:T(8,128)(2,1)}, u32[]{:S(2)}, u32[]{:S(2)}) collective-permute-start(bf16[128,512]{1,0:T(8,128)(2,1)S(1)} %get-tuple-element.64), channel_id=1, source_target_pairs={{0,2},{2,0},{4,6},{6,4},{1,3},{3,1},{5,7},{7,5},{8,10},{10,8},{12,... | collective-permute-start | bytes 393224 | tf_op jit(solution)/shard_map/cond/branch_0_fun/ppermute | solution.py:343
  91.2 15.3 %copy-start.4 = (f32[3,128,512]{2,1,0:T(8,128)S(1)}, f32[3,128,512]{2,1,0:T(8,128)}, u32[]{:S(2)}) copy-start(f32[3,128,512]{2,1,0:T(8,128)} %get-tuple-element.34.moment_hbm) | copy-start | bytes 2359300 | tf_op jit(solution)/shard_map/cond
  91.2 17.9 %collective-permute-start.5 = (bf16[256,512]{1,0:T(8,128)(2,1)}, bf16[256,512]{1,0:T(8,128)(2,1)S(1)}, u32[]{:S(2)}, u32[]{:S(2)}) collective-permute-start(bf16[256,512]{1,0:T(8,128)(2,1)} %get-tuple-element.31), channel_id=1, source_target_pairs={{0,1},{1,0},{2,3},{3,2},{4,5},{5,4},{6,7},{7,6},{8,9},{9,8},{10,11... | collective-permute-start | bytes 786440 | tf_op jit(solution)/shard_map/cond/branch_0_fun/ppermute | solution.py:347
  97.1 9.4 %all-to-all-start.3 = ((bf16[4,32,512]{2,1,0:T(8,128)(2,1)}), bf16[4,32,512]{2,1,0:T(8,128)(2,1)S(1)}, u32[]{:S(2)}, u32[]{:S(2)}) async-start(bf16[4,32,512]{2,1,0:T(8,128)(2,1)} %broadcast_in_dim.21), calls=%async_computation.3 | async-start | bytes 262144 | tf_op jit(solution)/shard_map/cond/branch_0_fun/all_to_all | solution.py:338
  103.7 5.4 %copy-start.9 = (f32[256,512]{1,0:T(8,128)S(1)}, f32[256,512]{1,0:T(8,128)}, u32[]{:S(2)}) copy-start(f32[256,512]{1,0:T(8,128)} %get-tuple-element.30) | copy-start | bytes 1572868 | tf_op jit(solution)/shard_map/cond

commit v5 on v4

--- a/solution.py
+++ b/solution.py
@@ -19,6 +19,7 @@
 
 VMEM_LIMIT = 12 << 20
 GRAD_VMEM_LIMIT = 62 << 20
+KEYS_VMEM_LIMIT = 24 << 20
 
 bf16 = jnp.bfloat16
 f32 = jnp.float32
@@ -158,32 +159,38 @@
             pltpu.SemaphoreType.DMA((SIDE + 2,)),
         ],
         cost_estimate=pl.CostEstimate(flops=1 << 30, bytes_accessed=7 << 20, transcendentals=0),
-        compiler_params=pltpu.CompilerParams(vmem_limit_bytes=GRAD_VMEM_LIMIT),
+        compiler_params=pltpu.CompilerParams(vmem_limit_bytes=KEYS_VMEM_LIMIT),
         name="half_keys",
     )(place, inputs, theirs, *weights)
 
 
-def update_kernel(gradient_ref, layers_ref, out_ref):
+def update_kernel(gradient_ref, layers_ref, own_ref, other_ref, out_ref, keys_ref):
     out_ref[0, 0] = layers_ref[0, 0] - inner_rate * gradient_ref[...]
     for layer in range(1, layers_ref.shape[1]):
         out_ref[0, layer] = layers_ref[0, layer]
-
-
-def update(gradient, local_weight):
+    keys_ref[0] = (own_ref[...] + other_ref[...].astype(f32)).astype(bf16)
+
+
+def update(gradient, local_weight, own, other):
     count, rows, features = local_weight.shape[1:]
+    tokens = own.shape[0]
     steps = 2
     block = rows // steps
     layers = pl.BlockSpec((1, count, block, features), lambda i: (0, 0, i, 0))
+    half = pl.BlockSpec((tokens // steps, features), lambda i: (i, 0))
     return pl.pallas_call(
         update_kernel,
-        out_shape=jax.ShapeDtypeStruct(local_weight.shape, f32),
+        out_shape=(
+            jax.ShapeDtypeStruct(local_weight.shape, f32),
+            jax.ShapeDtypeStruct((1, tokens, features), bf16),
+        ),
         grid=(steps,),
-        in_specs=[pl.BlockSpec((block, features), lambda i: (i, 0)), layers],
-        out_specs=layers,
-        cost_estimate=pl.CostEstimate(flops=1 << 19, bytes_accessed=2 << 20, transcendentals=0),
+        in_specs=[pl.BlockSpec((block, features), lambda i: (i, 0)), layers, half, half],
+        out_specs=(layers, pl.BlockSpec((1, tokens // steps, features), lambda i: (0, i, 0))),
+        cost_estimate=pl.CostEstimate(flops=1 << 19, bytes_accessed=3 << 20, transcendentals=0),
         compiler_params=pltpu.CompilerParams(vmem_limit_bytes=VMEM_LIMIT),
         name="update",
-    )(gradient, local_weight)
+    )(gradient, local_weight, own, other)
 
 
 def settle_kernel(
@@ -303,8 +310,7 @@
 
     own, other = half_keys(place, inputs, theirs, weights)
     other = lax.ppermute(other, "c", swap)
-    keys = (own + other.astype(f32)).astype(bf16)[None]
-    updated = update(gradient, local_weight)
+    updated, keys = update(gradient, local_weight, own, other)
     local_new, outer_new, moment_new = settle(
         fragment_index, mean, updated, outer_weight, outer_moment
     )
@@ -345,8 +351,7 @@
 
     own, other = half_keys(place, inputs, theirs, weights)
     other = lax.ppermute(other, "c", swap)
-    keys = (own + other.astype(f32)).astype(bf16)[None]
-    updated = update(gradient, local_weight)
+    updated, keys = update(gradient, local_weight, own, other)
     local_new, outer_new, moment_new = settle(
         fragment_index, mean, updated, outer_weight, outer_moment
     )

time: 111 us -> 117 us (1.054)
  the two profiles are of different devices: /device:TPU:1 before, /device:TPU:2 now
where the time goes in v5:
time: 117 us; the launch traced here: 116 us
  starting transfers between devices  46.5 us (40%)
  waiting for transfers between devices  31.1 us (27%)
  blocking collectives  16.5 us (14%)
  Pallas kernels  14.6 us (12%)
  other arithmetic  3.42 us (3%)
  local copies, waits for them, and re-layouts  2.92 us (2%)
  between operations  1.28 us (1%)
    all_gather x1, blocking collectives, trained_step(): rows = lax.all_gather(cast(layers, part), 'zl', axis=0, tiled=True)  16.5 us
    all_to_all x1, starting transfers between devices, trained_step(): mean = sum_all(lax.all_to_all(spread(mean), 'zh', 0, 0))  11 us
    all_to_all x1, starting transfers between devices, trained_step(): part = lax.all_to_all(part, 'x', 0, 0)  9.62 us
    ppermute x3, starting transfers between devices, trained_step(): lax.ppermute(rows, 'x', shift(offset))  9.21 us
    all_to_all x1, waiting for transfers between devices, trained_step(): part = lax.all_to_all(part, 'zl', 0, 0)  8.36 us
    all_to_all x1, waiting for transfers between devices, trained_step(): part = lax.all_to_all(part, 'x', 0, 0)  7.32 us
    all_to_all x1, waiting for transfers between devices, trained_step(): mean = sum_all(lax.all_to_all(spread(mean), 'zh', 0, 0))  7.05 us
    pallas_call x1, Pallas kernels, grad(): pl.pallas_call(grad_kernel, out_shape=jax.ShapeDtypeStruct((SIDE, ROWS, f...  5.14 us
  transfers between devices with their start and end apart: 11, of which 6 were waited for; matrix products, arithmetic and copies ran while one was open for 3% of the time, Pallas kernels for 6%

profile of v5, /device:TPU:2, one launch (start us, length us, event | category | flops | bytes accessed | tf_op | source)
XLA Modules:
  0.0 116.4 jit_solution(1088356269025357967)
XLA Ops:
  1.3 115.1 %conditional.1 = (bf16[1,256,512]{2,1,0:T(8,128)(2,1)}, f32[1,3,128,512]{3,2,1,0:T(8,128)}, f32[128,512]{1,0:T(8,128)}, f32[128,512]{1,0:T(8,128)}) conditional(s32[]{:T(128)} %bitcast.30, (bf16[1,256,4096]{2,1,0:T(8,128)(2,1)}, bf16[1,256,512]{2,1,0:T(8,128)(2,1)}, f32[1,3,128,512]{3,2,1,0:T(8,128)}, s32[1]{0:T(128)}, f32[3,128,512]{2,1,0:T(8,128)}, ...), branch_computations={%region_0.1_spmd, %region_1.2_spmd} | conditional | flops 2152153088 | bytes 80217128 | solution.py:362
  1.3 1.9 %collective-permute-start.9 = (bf16[256,4096]{1,0:T(8,128)(2,1)}, bf16[256,4096]{1,0:T(8,128)(2,1)}, u32[]{:S(2)}, u32[]{:S(2)}) collective-permute-start(bf16[256,4096]{1,0:T(8,128)(2,1)} %bitcast.48), channel_id=1, source_target_pairs={{0,1},{1,0},{2,3},{3,2},{4,5},{5,4},{6,7},{7,6},{8,9},{9,8},{10,11... | collective-permute-start | bytes 6291464 | tf_op jit(solution)/shard_map/cond/branch_1_fun/ppermute | solution.py:290
  3.2 2.4 %collective-permute-start.10 = (bf16[256,512]{1,0:T(8,128)(2,1)}, bf16[256,512]{1,0:T(8,128)(2,1)S(1)}, u32[]{:S(2)}, u32[]{:S(2)}) collective-permute-start(bf16[256,512]{1,0:T(8,128)(2,1)} %bitcast.57), channel_id=1, source_target_pairs={{0,1},{1,0},{2,3},{3,2},{4,5},{5,4},{6,7},{7,6},{8,9},{9,8},{10,11... | collective-permute-start | bytes 786440 | tf_op jit(solution)/shard_map/cond/branch_1_fun/ppermute | solution.py:291
  5.6 0.6 pad_add_fusion.1.place_ref
  6.2 1.7 %collective-permute-done.10.their_up_hbm = bf16[256,512]{1,0:T(8,128)(2,1)S(1)} collective-permute-done((bf16[256,512]{1,0:T(8,128)(2,1)}, bf16[256,512]{1,0:T(8,128)(2,1)S(1)}, u32[]{:S(2)}, u32[]{:S(2)}) %collective-permute-start.10) | collective-permute-done | bytes 262176 | tf_op jit(solution)/shard_map/cond/branch_1_fun/ppermute | solution.py:291
  7.9 0.0 copy-start.10
  7.9 0.0 collective-permute-done.9.theirs_hbm
  7.9 0.7 copy-done.10
  8.6 5.1 %gradient.3.after_ref = bf16[4,512,512]{2,1,0:T(8,128)(2,1)} custom-call(s32[2]{0:T(128)} %pad_add_fusion.1.place_ref, bf16[256,4096]{1,0:T(8,128)(2,1)} %bitcast.49, bf16[256,4096]{1,0:T(8,128)(2,1)} %collective-permute-done.9.theirs_hbm, bf16[256,512]{1,0:T(8,128)(2,1)} %bitcast.58, bf16[256,512]{1,0:T(8,128)(2,1)} %copy-done.10), custom_call_target="tpu_custom_call" | custom-call | flops 1073741824 | bytes 6291456 | tf_op jit(solution)/shard_map/cond/branch_1_fun/gradient/pallas_call | solution.py:69
  13.8 0.0 copy-start.4
  13.8 9.6 %all-to-all-start.4 = ((bf16[4,512,512]{2,1,0:T(8,128)(2,1)}), bf16[4,512,512]{2,1,0:T(8,128)(2,1)S(1)}, u32[]{:S(2)}, u32[]{:S(2)}) async-start(bf16[4,512,512]{2,1,0:T(8,128)(2,1)} %gradient.3.after_ref), calls=%async_computation.4 | async-start | bytes 4194304 | tf_op jit(solution)/shard_map/cond/branch_1_fun/all_to_all | solution.py:295
  23.4 0.0 copy-done.4
  23.4 1.0 bitcast_subtract_fusion
  24.4 0.7 cast_weights.3
  25.1 16.5 %all_gather.5.w0_hbm = bf16[512,512]{1,0:T(8,128)(2,1)S(1)} all-gather(bf16[128,512]{1,0:T(8,128)(2,1)} %cast_weights.3), channel_id=1, replica_groups=mesh['zh'=4,'y'=4,'x'=4,'zl'=4,'c'=2] {'zl'}, dimensions={0}, use_global_device_ids=true | all-gather | bytes 655360 | tf_op jit(solution)/shard_map/cond/branch_1_fun/all_gather | solution.py:293
  41.6 7.3 %all-to-all-done.4 = bf16[4,512,512]{2,1,0:T(8,128)(2,1)S(1)} async-done(((bf16[4,512,512]{2,1,0:T(8,128)(2,1)}), bf16[4,512,512]{2,1,0:T(8,128)(2,1)S(1)}, u32[]{:S(2)}, u32[]{:S(2)}) %all-to-all-start.4) | async-done | bytes 2097184 | tf_op jit(solution)/shard_map/cond/branch_1_fun/all_to_all | solution.py:295
  48.9 1.1 add_convert_fusion.2
  50.0 0.0 copy-start.1
  50.0 3.6 %all-to-all-start.5 = ((bf16[4,128,512]{2,1,0:T(8,128)(2,1)}), bf16[4,128,512]{2,1,0:T(8,128)(2,1)S(1)}, u32[]{:S(2)}, u32[]{:S(2)}) async-start(bf16[4,128,512]{2,1,0:T(8,128)(2,1)} %bitcast.24), calls=%async_computation.5 | async-start | bytes 1048576 | tf_op jit(solution)/shard_map/cond/branch_1_fun/all_to_all | solution.py:299
  53.6 1.9 %collective-permute-start.11 = (bf16[512,512]{1,0:T(8,128)(2,1)S(1)}, bf16[512,512]{1,0:T(8,128)(2,1)S(1)}, u32[]{:S(2)}, u32[]{:S(2)}) collective-permute-start(bf16[512,512]{1,0:T(8,128)(2,1)S(1)} %all_gather.5.w0_hbm), channel_id=1, source_target_pairs={{0,8},{8,16},{16,24},{24,0},{1,9},{9,17},{17,25},{25,1},{2,10},{10... | collective-permute-start | bytes 1572872 | tf_op jit(solution)/shard_map/cond/branch_1_fun/ppermute | solution.py:300
  55.5 3.9 %collective-permute-start.12 = (bf16[512,512]{1,0:T(8,128)(2,1)S(1)}, bf16[512,512]{1,0:T(8,128)(2,1)S(1)}, u32[]{:S(2)}, u32[]{:S(2)}) collective-permute-start(bf16[512,512]{1,0:T(8,128)(2,1)S(1)} %all_gather.5.w0_hbm), channel_id=1, source_target_pairs={{0,24},{8,0},{16,8},{24,16},{1,25},{9,1},{17,9},{25,17},{2,26},{10... | collective-permute-start | bytes 1572872 | tf_op jit(solution)/shard_map/cond/branch_1_fun/ppermute | solution.py:300
  59.4 8.4 %all-to-all-done.5 = bf16[4,128,512]{2,1,0:T(8,128)(2,1)S(1)} async-done(((bf16[4,128,512]{2,1,0:T(8,128)(2,1)}), bf16[4,128,512]{2,1,0:T(8,128)(2,1)S(1)}, u32[]{:S(2)}, u32[]{:S(2)}) %all-to-all-start.5) | async-done | bytes 524320 | tf_op jit(solution)/shard_map/cond/branch_1_fun/all_to_all | solution.py:299
  67.8 0.7 add_convert_fusion.3
  68.5 3.3 %all-to-all-start.6 = ((bf16[4,32,512]{2,1,0:T(8,128)(2,1)}), bf16[4,32,512]{2,1,0:T(8,128)(2,1)S(1)}, u32[]{:S(2)}, u32[]{:S(2)}) async-start(bf16[4,32,512]{2,1,0:T(8,128)(2,1)} %bitcast.26), calls=%async_computation.6 | async-start | bytes 262144 | tf_op jit(solution)/shard_map/cond/branch_1_fun/all_to_all | solution.py:305
  71.9 3.4 %collective-permute-start.13 = (bf16[512,512]{1,0:T(8,128)(2,1)S(1)}, bf16[512,512]{1,0:T(8,128)(2,1)S(1)}, u32[]{:S(2)}, u32[]{:S(2)}) collective-permute-start(bf16[512,512]{1,0:T(8,128)(2,1)S(1)} %all_gather.5.w0_hbm), channel_id=1, source_target_pairs={{0,16},{8,24},{16,0},{24,8},{1,17},{9,25},{17,1},{25,9},{2,18},{10... | collective-permute-start | bytes 1572872 | tf_op jit(solution)/shard_map/cond/branch_1_fun/ppermute | solution.py:300
  75.2 2.6 %all-to-all-done.6 = bf16[4,32,512]{2,1,0:T(8,128)(2,1)S(1)} async-done(((bf16[4,32,512]{2,1,0:T(8,128)(2,1)}), bf16[4,32,512]{2,1,0:T(8,128)(2,1)S(1)}, u32[]{:S(2)}, u32[]{:S(2)}) %all-to-all-start.6) | async-done | bytes 131104 | tf_op jit(solution)/shard_map/cond/branch_1_fun/all_to_all | solution.py:305
  77.8 0.0 collective-permute-done.11.w1_hbm
  77.8 0.0 collective-permute-done.12.w3_hbm
  77.8 0.7 broadcast_in_dim.18
  78.5 11.0 %all-to-all-start.7 = ((bf16[4,32,512]{2,1,0:T(8,128)(2,1)}), bf16[4,32,512]{2,1,0:T(8,128)(2,1)S(1)}, u32[]{:S(2)}, u32[]{:S(2)}) async-start(bf16[4,32,512]{2,1,0:T(8,128)(2,1)} %broadcast_in_dim.18), calls=%async_computation.7 | async-start | bytes 262144 | tf_op jit(solution)/shard_map/cond/branch_1_fun/all_to_all | solution.py:307
  89.5 0.0 collective-permute-done.13.w2_hbm
  89.5 0.0 copy-done.1
  89.5 4.4 %half_keys.3 = (f32[256,512]{1,0:T(8,128)S(1)}, bf16[256,512]{1,0:T(8,128)(2,1)S(1)}) custom-call(s32[2]{0:T(128)S(1)} %copy-done.1, bf16[256,4096]{1,0:T(8,128)(2,1)} %bitcast.50, bf16[256,4096]{1,0:T(8,128)(2,1)} %collective-permute-done.9.theirs_hbm, bf16[512,512]{1,0:T(8,128)(2,1)S(1)} %all_gather.5.w0_hbm, ...), custom_call_target="tpu_custom_call" | custom-call | flops 1073741824 | bytes 7340032 | tf_op jit(solution)/shard_map/cond/branch_1_fun/half_keys/pallas_call | solution.py:147
  93.9 0.0 copy-start.7
  94.0 2.1 %collective-permute-start.14 = (bf16[256,512]{1,0:T(8,128)(2,1)S(1)}, bf16[256,512]{1,0:T(8,128)(2,1)S(1)}, u32[]{:S(2)}, u32[]{:S(2)}) collective-permute-start(bf16[256,512]{1,0:T(8,128)(2,1)S(1)} %get-tuple-element.52), channel_id=1, source_target_pairs={{0,1},{1,0},{2,3},{3,2},{4,5},{5,4},{6,7},{7,6},{8,9},{9,8},{10,11... | collective-permute-start | bytes 786440 | tf_op jit(solution)/shard_map/cond/branch_1_fun/ppermute | solution.py:312
  96.0 7.0 %all-to-all-done.7 = bf16[4,32,512]{2,1,0:T(8,128)(2,1)S(1)} async-done(((bf16[4,32,512]{2,1,0:T(8,128)(2,1)}), bf16[4,32,512]{2,1,0:T(8,128)(2,1)S(1)}, u32[]{:S(2)}, u32[]{:S(2)}) %all-to-all-start.7) | async-done | bytes 131104 | tf_op jit(solution)/shard_map/cond/branch_1_fun/all_to_all | solution.py:307
  103.1 0.7 broadcast_in_dim.19
  103.8 3.3 %all-to-all-start.8 = ((bf16[4,32,512]{2,1,0:T(8,128)(2,1)}), bf16[4,32,512]{2,1,0:T(8,128)(2,1)S(1)}, u32[]{:S(2)}, u32[]{:S(2)}) async-start(bf16[4,32,512]{2,1,0:T(8,128)(2,1)} %broadcast_in_dim.19), calls=%async_computation.8 | async-start | bytes 262144 | tf_op jit(solution)/shard_map/cond/branch_1_fun/all_to_all | solution.py:309
  107.1 0.0 collective-permute-done.14.other_ref
  107.1 1.9 %update.3 = (f32[1,3,128,512]{3,2,1,0:T(8,128)S(1)}, bf16[1,256,512]{2,1,0:T(8,128)(2,1)}) custom-call(f32[128,512]{1,0:T(8,128)S(1)} %get-tuple-element.48.gradient_ref, f32[1,3,128,512]{3,2,1,0:T(8,128)} %get-tuple-element.42.layers_ref, f32[256,512]{1,0:T(8,128)S(1)} %get-tuple-element.51.own_ref, bf16[256,512]{1,0:T(8,128)(2,1)S(1)} %collective-permute-done.14.other_ref), custom_call_target="tpu_custom_call" | custom-call | flops 524288 | bytes 3145728 | tf_op jit(solution)/shard_map/cond/branch_1_fun/update/pallas_call | solution.py:181
  109.0 4.1 %all-to-all-done.8 = bf16[4,32,512]{2,1,0:T(8,128)(2,1)S(1)} async-done(((bf16[4,32,512]{2,1,0:T(8,128)(2,1)}), bf16[4,32,512]{2,1,0:T(8,128)(2,1)S(1)}, u32[]{:S(2)}, u32[]{:S(2)}) %all-to-all-start.8) | async-done | bytes 131104 | tf_op jit(solution)/shard_map/cond/branch_1_fun/all_to_all | solution.py:309
  113.0 0.0 copy-done.7
  113.0 2.5 %settle.3 = (f32[1,3,128,512]{3,2,1,0:T(8,128)S(1)}, f32[128,512]{1,0:T(8,128)}, f32[128,512]{1,0:T(8,128)}) custom-call(s32[1]{0:T(128)} %get-tuple-element.54.chosen_ref, bf16[128,512]{1,0:T(8,128)(2,1)S(1)} %bitcast.44, f32[1,3,128,512]{3,2,1,0:T(8,128)S(1)} %get-tuple-element.56.layers_hbm, ...), custom_call_target="tpu_custom_call", output_to_operand_aliasing={{0}: (2, {})} | custom-call | flops 1048576 | bytes 2097152 | tf_op jit(solution)/shard_map/cond/branch_1_fun/settle/pallas_call | solution.py:242
  115.5 0.0 copy-start.9
  115.5 0.9 copy-done.9
  (2 shorter events, 0.0 us)
Async XLA Ops:
  1.3 6.6 %collective-permute-start.9 = (bf16[256,4096]{1,0:T(8,128)(2,1)}, bf16[256,4096]{1,0:T(8,128)(2,1)}, u32[]{:S(2)}, u32[]{:S(2)}) collective-permute-start(bf16[256,4096]{1,0:T(8,128)(2,1)} %bitcast.48), channel_id=1, source_target_pairs={{0,1},{1,0},{2,3},{3,2},{4,5},{5,4},{6,7},{7,6},{8,9},{9,8},{10,11... | collective-permute-start | bytes 6291464 | tf_op jit(solution)/shard_map/cond/branch_1_fun/ppermute | solution.py:290
  3.2 4.7 %collective-permute-start.10 = (bf16[256,512]{1,0:T(8,128)(2,1)}, bf16[256,512]{1,0:T(8,128)(2,1)S(1)}, u32[]{:S(2)}, u32[]{:S(2)}) collective-permute-start(bf16[256,512]{1,0:T(8,128)(2,1)} %bitcast.57), channel_id=1, source_target_pairs={{0,1},{1,0},{2,3},{3,2},{4,5},{5,4},{6,7},{7,6},{8,9},{9,8},{10,11... | collective-permute-start | bytes 786440 | tf_op jit(solution)/shard_map/cond/branch_1_fun/ppermute | solution.py:291
  7.9 0.7 copy-start.10
  13.8 9.6 %copy-start.4 = (f32[1,3,128,512]{3,2,1,0:T(8,128)S(1)}, f32[1,3,128,512]{3,2,1,0:T(8,128)}, u32[]{:S(2)}) copy-start(f32[1,3,128,512]{3,2,1,0:T(8,128)} %get-tuple-element.42.layers_ref) | copy-start | bytes 2359300 | tf_op jit(solution)/shard_map/cond
  13.8 35.1 %all-to-all-start.4 = ((bf16[4,512,512]{2,1,0:T(8,128)(2,1)}), bf16[4,512,512]{2,1,0:T(8,128)(2,1)S(1)}, u32[]{:S(2)}, u32[]{:S(2)}) async-start(bf16[4,512,512]{2,1,0:T(8,128)(2,1)} %gradient.3.after_ref), calls=%async_computation.4 | async-start | bytes 4194304 | tf_op jit(solution)/shard_map/cond/branch_1_fun/all_to_all | solution.py:295
  50.0 39.6 %copy-start.1 = (s32[2]{0:T(128)S(1)}, s32[2]{0:T(128)}, u32[]{:S(2)}) copy-start(s32[2]{0:T(128)} %pad_add_fusion.1.place_ref) | copy-start | bytes 28 | tf_op jit(solution)/shard_map/cond
  50.0 17.8 %all-to-all-start.5 = ((bf16[4,128,512]{2,1,0:T(8,128)(2,1)}), bf16[4,128,512]{2,1,0:T(8,128)(2,1)S(1)}, u32[]{:S(2)}, u32[]{:S(2)}) async-start(bf16[4,128,512]{2,1,0:T(8,128)(2,1)} %bitcast.24), calls=%async_computation.5 | async-start | bytes 1048576 | tf_op jit(solution)/shard_map/cond/branch_1_fun/all_to_all | solution.py:299
  53.6 24.3 %collective-permute-start.11 = (bf16[512,512]{1,0:T(8,128)(2,1)S(1)}, bf16[512,512]{1,0:T(8,128)(2,1)S(1)}, u32[]{:S(2)}, u32[]{:S(2)}) collective-permute-start(bf16[512,512]{1,0:T(8,128)(2,1)S(1)} %all_gather.5.w0_hbm), channel_id=1, source_target_pairs={{0,8},{8,16},{16,24},{24,0},{1,9},{9,17},{17,25},{25,1},{2,10},{10... | collective-permute-start | bytes 1572872 | tf_op jit(solution)/shard_map/cond/branch_1_fun/ppermute | solution.py:300
  55.5 22.3 %collective-permute-start.12 = (bf16[512,512]{1,0:T(8,128)(2,1)S(1)}, bf16[512,512]{1,0:T(8,128)(2,1)S(1)}, u32[]{:S(2)}, u32[]{:S(2)}) collective-permute-start(bf16[512,512]{1,0:T(8,128)(2,1)S(1)} %all_gather.5.w0_hbm), channel_id=1, source_target_pairs={{0,24},{8,0},{16,8},{24,16},{1,25},{9,1},{17,9},{25,17},{2,26},{10... | collective-permute-start | bytes 1572872 | tf_op jit(solution)/shard_map/cond/branch_1_fun/ppermute | solution.py:300
  68.5 9.3 %all-to-all-start.6 = ((bf16[4,32,512]{2,1,0:T(8,128)(2,1)}), bf16[4,32,512]{2,1,0:T(8,128)(2,1)S(1)}, u32[]{:S(2)}, u32[]{:S(2)}) async-start(bf16[4,32,512]{2,1,0:T(8,128)(2,1)} %bitcast.26), calls=%async_computation.6 | async-start | bytes 262144 | tf_op jit(solution)/shard_map/cond/branch_1_fun/all_to_all | solution.py:305
  71.9 17.7 %collective-permute-start.13 = (bf16[512,512]{1,0:T(8,128)(2,1)S(1)}, bf16[512,512]{1,0:T(8,128)(2,1)S(1)}, u32[]{:S(2)}, u32[]{:S(2)}) collective-permute-start(bf16[512,512]{1,0:T(8,128)(2,1)S(1)} %all_gather.5.w0_hbm), channel_id=1, source_target_pairs={{0,16},{8,24},{16,0},{24,8},{1,17},{9,25},{17,1},{25,9},{2,18},{10... | collective-permute-start | bytes 1572872 | tf_op jit(solution)/shard_map/cond/branch_1_fun/ppermute | solution.py:300
  78.5 24.6 %all-to-all-start.7 = ((bf16[4,32,512]{2,1,0:T(8,128)(2,1)}), bf16[4,32,512]{2,1,0:T(8,128)(2,1)S(1)}, u32[]{:S(2)}, u32[]{:S(2)}) async-start(bf16[4,32,512]{2,1,0:T(8,128)(2,1)} %broadcast_in_dim.18), calls=%async_computation.7 | async-start | bytes 262144 | tf_op jit(solution)/shard_map/cond/branch_1_fun/all_to_all | solution.py:307
  93.9 19.1 %copy-start.7 = (f32[3,128,512]{2,1,0:T(8,128)S(1)}, f32[3,128,512]{2,1,0:T(8,128)}, u32[]{:S(2)}) copy-start(f32[3,128,512]{2,1,0:T(8,128)} %get-tuple-element.43.outer_hbm) | copy-start | bytes 2359300 | tf_op jit(solution)/shard_map/cond
  94.0 13.1 %collective-permute-start.14 = (bf16[256,512]{1,0:T(8,128)(2,1)S(1)}, bf16[256,512]{1,0:T(8,128)(2,1)S(1)}, u32[]{:S(2)}, u32[]{:S(2)}) collective-permute-start(bf16[256,512]{1,0:T(8,128)(2,1)S(1)} %get-tuple-element.52), channel_id=1, source_target_pairs={{0,1},{1,0},{2,3},{3,2},{4,5},{5,4},{6,7},{7,6},{8,9},{9,8},{10,11... | collective-permute-start | bytes 786440 | tf_op jit(solution)/shard_map/cond/branch_1_fun/ppermute | solution.py:312
  103.8 9.3 %all-to-all-start.8 = ((bf16[4,32,512]{2,1,0:T(8,128)(2,1)}), bf16[4,32,512]{2,1,0:T(8,128)(2,1)S(1)}, u32[]{:S(2)}, u32[]{:S(2)}) async-start(bf16[4,32,512]{2,1,0:T(8,128)(2,1)} %broadcast_in_dim.19), calls=%async_computation.8 | async-start | bytes 262144 | tf_op jit(solution)/shard_map/cond/branch_1_fun/all_to_all | solution.py:309
  115.5 0.9 copy-start.9

commit v6 on v5

--- a/solution.py
+++ b/solution.py
@@ -164,14 +164,18 @@
     )(place, inputs, theirs, *weights)
 
 
-def update_kernel(gradient_ref, layers_ref, own_ref, other_ref, out_ref, keys_ref):
-    out_ref[0, 0] = layers_ref[0, 0] - inner_rate * gradient_ref[...]
+def update_kernel(layers_ref, own_ref, other_ref, *refs):
+    out_ref, keys_ref = refs[-2:]
+    terms = [ref[...].astype(f32) for ref in refs[:-2]]
+    while len(terms) > 1:
+        terms = [first + second for first, second in zip(terms[::2], terms[1::2])]
+    out_ref[0, 0] = layers_ref[0, 0] - inner_rate * terms[0]
     for layer in range(1, layers_ref.shape[1]):
         out_ref[0, layer] = layers_ref[0, layer]
     keys_ref[0] = (own_ref[...] + other_ref[...].astype(f32)).astype(bf16)
 
 
-def update(gradient, local_weight, own, other):
+def update(pieces, local_weight, own, other):
     count, rows, features = local_weight.shape[1:]
     tokens = own.shape[0]
     steps = 2
@@ -185,12 +189,13 @@
             jax.ShapeDtypeStruct((1, tokens, features), bf16),
         ),
         grid=(steps,),
-        in_specs=[pl.BlockSpec((block, features), lambda i: (i, 0)), layers, half, half],
+        in_specs=[layers, half, half]
+        + [pl.BlockSpec((block, features), lambda i: (i, 0))] * len(pieces),
         out_specs=(layers, pl.BlockSpec((1, tokens // steps, features), lambda i: (0, i, 0))),
         cost_estimate=pl.CostEstimate(flops=1 << 19, bytes_accessed=3 << 20, transcendentals=0),
         compiler_params=pltpu.CompilerParams(vmem_limit_bytes=VMEM_LIMIT),
         name="update",
-    )(gradient, local_weight, own, other)
+    )(local_weight, own, other, *pieces)
 
 
 def settle_kernel(
@@ -310,7 +315,7 @@
 
     own, other = half_keys(place, inputs, theirs, weights)
     other = lax.ppermute(other, "c", swap)
-    updated, keys = update(gradient, local_weight, own, other)
+    updated, keys = update([gradient], local_weight, own, other)
     local_new, outer_new, moment_new = settle(
         fragment_index, mean, updated, outer_weight, outer_moment
     )
@@ -345,13 +350,11 @@
 
     along = lax.axis_index("zl")
     chunk = lambda mask: lax.dynamic_index_in_dim(part, along ^ mask, 0, keepdims=False)
-    gradient = sum_all(
-        jnp.stack([chunk(0)] + [lax.ppermute(chunk(mask), "zl", flip(mask)) for mask in (1, 2, 3)])
-    )
+    pieces = [chunk(0)] + [lax.ppermute(chunk(mask), "zl", flip(mask)) for mask in (1, 2, 3)]
 
     own, other = half_keys(place, inputs, theirs, weights)
     other = lax.ppermute(other, "c", swap)
-    updated, keys = update(gradient, local_weight, own, other)
+    updated, keys = update(pieces, local_weight, own, other)
     local_new, outer_new, moment_new = settle(
         fragment_index, mean, updated, outer_weight, outer_moment
     )

time: 117 us -> 108 us (0.923)
  waiting for transfers between devices: 31.1 us -> 10.3 us
  starting transfers between devices: 46.5 us -> 55.4 us
  loops' own time: 0.19 us -> 2.24 us
    all_to_all x5 -> x4, waiting for transfers between devices: 29.3 us -> 8.56 us  [the longest x1 4.66 us: other_step(): part = lax.all_to_all(part, 'x', 0, 0)]
    ppermute x6 -> x9, starting transfers between devices: 15.6 us -> 26.3 us  [the longest x3 10.1 us: other_step(): lax.ppermute(chunk(mask), 'zl', flip(mask))]
    another operation x1, loops' own time: 0.19 us -> 2.24 us  [shards(): lax.cond(fragment_index[0] == 0, trained_step, other_step, activations, c...]
    all_to_all x5 -> x4, starting transfers between devices: 30.9 us -> 29.1 us  [the longest x1 11.4 us: other_step(): mean = sum_all(lax.all_to_all(spread(mean), 'zh', 0, 0))]
  transfers between devices with their start and end apart: 11 -> 13, of which waited for: 6 -> 3; matrix products, arithmetic and copies ran while one was open for 3% -> 6% of each run, Pallas kernels for 6% -> 6%
where the time goes in v6:
time: 108 us; the launch traced here: 107 us
  starting transfers between devices  55.4 us (51%)
  blocking collectives  16.5 us (15%)
  Pallas kernels  14.3 us (13%)
  waiting for transfers between devices  10.3 us (10%)
  local copies, waits for them, and re-layouts  3.81 us (4%)
  other arithmetic  3.28 us (3%)
  loops' own time  2.24 us (2%)
  between operations  1.28 us (1%)
    all_gather x1, blocking collectives, other_step(): rows = lax.all_gather(cast(layers, part), 'zl', axis=0, tiled=True)  16.5 us
    all_to_all x1, starting transfers between devices, other_step(): mean = sum_all(lax.all_to_all(spread(mean), 'zh', 0, 0))  11.4 us
    ppermute x3, starting transfers between devices, other_step(): lax.ppermute(chunk(mask), 'zl', flip(mask))  10.1 us
    ppermute x3, starting transfers between devices, other_step(): lax.ppermute(rows, 'x', shift(offset))  9.81 us
    all_to_all x1, starting transfers between devices, other_step(): part = lax.all_to_all(part, 'x', 0, 0)  9.64 us
    pallas_call x1, Pallas kernels, grad(): pl.pallas_call(grad_kernel, out_shape=jax.ShapeDtypeStruct((SIDE, ROWS, f...  5.12 us
    all_to_all x1, starting transfers between devices, other_step(): mean = lax.all_to_all(spread(mean), 'y', 0, 0).reshape(PIECE, features)  4.8 us
    all_to_all x1, waiting for transfers between devices, other_step(): part = lax.all_to_all(part, 'x', 0, 0)  4.66 us
  transfers between devices with their start and end apart: 13, of which 3 were waited for; matrix products, arithmetic and copies ran while one was open for 6% of the time, Pallas kernels for 6%

profile of v6, /device:TPU:2, one launch (start us, length us, event | category | flops | bytes accessed | tf_op | source)
XLA Modules:
  0.0 107.1 jit_solution(4895015909595907870)
XLA Ops:
  1.3 105.8 %conditional.1 = (bf16[1,256,512]{2,1,0:T(8,128)(2,1)}, f32[1,3,128,512]{3,2,1,0:T(8,128)}, f32[128,512]{1,0:T(8,128)}, f32[128,512]{1,0:T(8,128)}) conditional(s32[]{:T(128)} %bitcast.29, (bf16[1,256,4096]{2,1,0:T(8,128)(2,1)}, bf16[1,256,512]{2,1,0:T(8,128)(2,1)}, f32[1,3,128,512]{3,2,1,0:T(8,128)}, s32[1]{0:T(128)}, f32[3,128,512]{2,1,0:T(8,128)}, ...), branch_computations={%region_0.1_spmd, %region_1.2_spmd} | conditional | flops 2152153088 | bytes 76547080 | solution.py:365
  1.3 1.9 %collective-permute-start = (bf16[256,4096]{1,0:T(8,128)(2,1)}, bf16[256,4096]{1,0:T(8,128)(2,1)}, u32[]{:S(2)}, u32[]{:S(2)}) collective-permute-start(bf16[256,4096]{1,0:T(8,128)(2,1)} %bitcast.44), channel_id=1, source_target_pairs={{0,1},{1,0},{2,3},{3,2},{4,5},{5,4},{6,7},{7,6},{8,9},{9,8},{10,11... | collective-permute-start | bytes 6291464 | tf_op jit(solution)/shard_map/cond/branch_0_fun/ppermute | solution.py:336
  3.2 2.4 %collective-permute-start.1 = (bf16[256,512]{1,0:T(8,128)(2,1)}, bf16[256,512]{1,0:T(8,128)(2,1)S(1)}, u32[]{:S(2)}, u32[]{:S(2)}) collective-permute-start(bf16[256,512]{1,0:T(8,128)(2,1)} %bitcast.53), channel_id=1, source_target_pairs={{0,1},{1,0},{2,3},{3,2},{4,5},{5,4},{6,7},{7,6},{8,9},{9,8},{10,11... | collective-permute-start | bytes 786440 | tf_op jit(solution)/shard_map/cond/branch_0_fun/ppermute | solution.py:337
  5.6 0.6 pad_add_fusion.place_ref
  6.3 1.7 %collective-permute-done.1.their_up_hbm = bf16[256,512]{1,0:T(8,128)(2,1)S(1)} collective-permute-done((bf16[256,512]{1,0:T(8,128)(2,1)}, bf16[256,512]{1,0:T(8,128)(2,1)S(1)}, u32[]{:S(2)}, u32[]{:S(2)}) %collective-permute-start.1) | collective-permute-done | bytes 262176 | tf_op jit(solution)/shard_map/cond/branch_0_fun/ppermute | solution.py:337
  7.9 0.0 collective-permute-done.theirs_hbm
  7.9 0.7 copy-done.10
  8.6 5.1 %gradient.2.after_ref = bf16[4,512,512]{2,1,0:T(8,128)(2,1)} custom-call(s32[2]{0:T(128)} %pad_add_fusion.place_ref, bf16[256,4096]{1,0:T(8,128)(2,1)} %bitcast.45, bf16[256,4096]{1,0:T(8,128)(2,1)} %collective-permute-done.theirs_hbm, bf16[256,512]{1,0:T(8,128)(2,1)} %bitcast.54, bf16[256,512]{1,0:T(8,128)(2,1)} %copy-done.10), custom_call_target="tpu_custom_call" | custom-call | flops 1073741824 | bytes 6291456 | tf_op jit(solution)/shard_map/cond/branch_0_fun/gradient/pallas_call | solution.py:69
  13.8 0.0 copy-start.3
  13.8 9.6 %all-to-all-start = ((bf16[4,512,512]{2,1,0:T(8,128)(2,1)}), bf16[4,512,512]{2,1,0:T(8,128)(2,1)S(1)}, u32[]{:S(2)}, u32[]{:S(2)}) async-start(bf16[4,512,512]{2,1,0:T(8,128)(2,1)} %gradient.2.after_ref), calls=%async_computation | async-start | bytes 4194304 | tf_op jit(solution)/shard_map/cond/branch_0_fun/all_to_all | solution.py:342
  25.4 1.0 constant_dynamic-slice_fusion.1
  26.3 0.0 copy-done.3
  26.4 0.7 subtract_convert_fusion
  27.1 0.7 cast_weights.2
  27.7 16.5 %all_gather.4.w0_hbm = bf16[512,512]{1,0:T(8,128)(2,1)S(1)} all-gather(bf16[128,512]{1,0:T(8,128)(2,1)} %cast_weights.2), channel_id=1, replica_groups=mesh['zh'=4,'y'=4,'x'=4,'zl'=4,'c'=2] {'zl'}, dimensions={0}, use_global_device_ids=true | all-gather | bytes 655360 | tf_op jit(solution)/shard_map/cond/branch_0_fun/all_gather | solution.py:339
  44.2 4.7 %all-to-all-done = bf16[4,512,512]{2,1,0:T(8,128)(2,1)S(1)} async-done(((bf16[4,512,512]{2,1,0:T(8,128)(2,1)}), bf16[4,512,512]{2,1,0:T(8,128)(2,1)S(1)}, u32[]{:S(2)}, u32[]{:S(2)}) %all-to-all-start) | async-done | bytes 2097184 | tf_op jit(solution)/shard_map/cond/branch_0_fun/all_to_all | solution.py:342
  48.9 3.3 %all-to-all-start.1 = ((bf16[4,32,512]{2,1,0:T(8,128)(2,1)}), bf16[4,32,512]{2,1,0:T(8,128)(2,1)S(1)}, u32[]{:S(2)}, u32[]{:S(2)}) async-start(bf16[4,32,512]{2,1,0:T(8,128)(2,1)} %subtract_convert_fusion), calls=%async_computation.1 | async-start | bytes 262144 | tf_op jit(solution)/shard_map/cond/branch_0_fun/all_to_all | solution.py:346
  52.2 0.0 copy-done.5
  52.2 0.0 copy-start
  52.3 3.4 %collective-permute-start.4 = (bf16[512,512]{1,0:T(8,128)(2,1)S(1)}, bf16[512,512]{1,0:T(8,128)(2,1)S(1)}, u32[]{:S(2)}, u32[]{:S(2)}) collective-permute-start(bf16[512,512]{1,0:T(8,128)(2,1)S(1)} %all_gather.4.w0_hbm), channel_id=1, source_target_pairs={{0,24},{8,0},{16,8},{24,16},{1,25},{9,1},{17,9},{25,17},{2,26},{10... | collective-permute-start | bytes 1572872 | tf_op jit(solution)/shard_map/cond/branch_0_fun/ppermute | solution.py:344
  55.6 1.9 %collective-permute-start.3 = (bf16[512,512]{1,0:T(8,128)(2,1)S(1)}, bf16[512,512]{1,0:T(8,128)(2,1)S(1)}, u32[]{:S(2)}, u32[]{:S(2)}) collective-permute-start(bf16[512,512]{1,0:T(8,128)(2,1)S(1)} %all_gather.4.w0_hbm), channel_id=1, source_target_pairs={{0,16},{8,24},{16,0},{24,8},{1,17},{9,25},{17,1},{25,9},{2,18},{10... | collective-permute-start | bytes 1572872 | tf_op jit(solution)/shard_map/cond/branch_0_fun/ppermute | solution.py:344
  57.6 4.5 %collective-permute-start.2 = (bf16[512,512]{1,0:T(8,128)(2,1)S(1)}, bf16[512,512]{1,0:T(8,128)(2,1)S(1)}, u32[]{:S(2)}, u32[]{:S(2)}) collective-permute-start(bf16[512,512]{1,0:T(8,128)(2,1)S(1)} %all_gather.4.w0_hbm), channel_id=1, source_target_pairs={{0,8},{8,16},{16,24},{24,0},{1,9},{9,17},{17,25},{25,1},{2,10},{10... | collective-permute-start | bytes 1572872 | tf_op jit(solution)/shard_map/cond/branch_0_fun/ppermute | solution.py:344
  62.1 0.0 all-to-all-done.1
  62.1 0.7 broadcast_in_dim.3
  62.8 11.4 %all-to-all-start.2 = ((bf16[4,32,512]{2,1,0:T(8,128)(2,1)}), bf16[4,32,512]{2,1,0:T(8,128)(2,1)S(1)}, u32[]{:S(2)}, u32[]{:S(2)}) async-start(bf16[4,32,512]{2,1,0:T(8,128)(2,1)} %broadcast_in_dim.3), calls=%async_computation.2 | async-start | bytes 262144 | tf_op jit(solution)/shard_map/cond/branch_0_fun/all_to_all | solution.py:348
  74.2 1.9 %add_convert_fusion = bf16[1,512,512]{2,1,0:T(8,128)(2,1)S(1)} fusion(bf16[4,512,512]{2,1,0:T(8,128)(2,1)} %copy-done.5), kind=kLoop, calls=%fused_computation | loop fusion | flops 2097152 | bytes 2621440 | tf_op jit(solution)/shard_map/cond/branch_0_fun/convert_element_type | solution.py:347
  76.1 0.8 dynamic-slice_bitcast_fusion
  76.9 3.8 %collective-permute-start.8 = (bf16[128,512]{1,0:T(8,128)(2,1)}, bf16[128,512]{1,0:T(8,128)(2,1)S(1)}, u32[]{:S(2)}, u32[]{:S(2)}) collective-permute-start(bf16[128,512]{1,0:T(8,128)(2,1)} %get-tuple-element.67), channel_id=1, source_target_pairs={{0,6},{2,4},{4,2},{6,0},{1,7},{3,5},{5,3},{7,1},{8,14},{10,12},{12... | collective-permute-start | bytes 393224 | tf_op jit(solution)/shard_map/cond/branch_0_fun/ppermute | solution.py:353
  80.7 2.5 %collective-permute-start.7 = (bf16[128,512]{1,0:T(8,128)(2,1)}, bf16[128,512]{1,0:T(8,128)(2,1)S(1)}, u32[]{:S(2)}, u32[]{:S(2)}) collective-permute-start(bf16[128,512]{1,0:T(8,128)(2,1)} %get-tuple-element.68), channel_id=1, source_target_pairs={{0,4},{2,6},{4,0},{6,2},{1,5},{3,7},{5,1},{7,3},{8,12},{10,14},{12... | collective-permute-start | bytes 393224 | tf_op jit(solution)/shard_map/cond/branch_0_fun/ppermute | solution.py:353
  83.2 0.0 collective-permute-done.4.w3_hbm
  83.2 3.8 %collective-permute-start.6 = (bf16[128,512]{1,0:T(8,128)(2,1)}, bf16[128,512]{1,0:T(8,128)(2,1)S(1)}, u32[]{:S(2)}, u32[]{:S(2)}) collective-permute-start(bf16[128,512]{1,0:T(8,128)(2,1)} %get-tuple-element.69), channel_id=1, source_target_pairs={{0,2},{2,0},{4,6},{6,4},{1,3},{3,1},{5,7},{7,5},{8,10},{10,8},{12,... | collective-permute-start | bytes 393224 | tf_op jit(solution)/shard_map/cond/branch_0_fun/ppermute | solution.py:353
  87.0 0.0 collective-permute-done.3.w2_hbm
  87.0 0.0 collective-permute-done.2.w1_hbm
  87.0 0.0 copy-done
  87.0 0.0 copy-done.2
  87.0 3.9 %half_keys.2 = (f32[256,512]{1,0:T(8,128)S(1)}, bf16[256,512]{1,0:T(8,128)(2,1)S(1)}) custom-call(s32[2]{0:T(128)S(1)} %copy-done, bf16[256,4096]{1,0:T(8,128)(2,1)S(1)} %bitcast.46, bf16[256,4096]{1,0:T(8,128)(2,1)} %collective-permute-done.theirs_hbm, bf16[512,512]{1,0:T(8,128)(2,1)S(1)} %all_gather.4.w0_hbm, ...), custom_call_target="tpu_custom_call" | custom-call | flops 1073741824 | bytes 7340032 | tf_op jit(solution)/shard_map/cond/branch_0_fun/half_keys/pallas_call | solution.py:147
  91.0 0.0 copy-start.6
  91.0 2.1 %collective-permute-start.5 = (bf16[256,512]{1,0:T(8,128)(2,1)S(1)}, bf16[256,512]{1,0:T(8,128)(2,1)S(1)}, u32[]{:S(2)}, u32[]{:S(2)}) collective-permute-start(bf16[256,512]{1,0:T(8,128)(2,1)S(1)} %get-tuple-element.31), channel_id=1, source_target_pairs={{0,1},{1,0},{2,3},{3,2},{4,5},{5,4},{6,7},{7,6},{8,9},{9,8},{10,11... | collective-permute-start | bytes 786440 | tf_op jit(solution)/shard_map/cond/branch_0_fun/ppermute | solution.py:356
  93.0 0.0 all-to-all-done.2
  93.1 0.7 broadcast_in_dim.17
  93.7 4.8 %all-to-all-start.3 = ((bf16[4,32,512]{2,1,0:T(8,128)(2,1)}), bf16[4,32,512]{2,1,0:T(8,128)(2,1)S(1)}, u32[]{:S(2)}, u32[]{:S(2)}) async-start(bf16[4,32,512]{2,1,0:T(8,128)(2,1)} %broadcast_in_dim.17), calls=%async_computation.3 | async-start | bytes 262144 | tf_op jit(solution)/shard_map/cond/branch_0_fun/all_to_all | solution.py:349
  98.5 0.0 collective-permute-done.8.refs_3_
  98.5 0.0 collective-permute-done.7.refs_2_
  98.5 0.0 collective-permute-done.6.refs_1_
  98.5 0.0 collective-permute-done.5.other_ref
  98.6 2.0 %update.2 = (f32[1,3,128,512]{3,2,1,0:T(8,128)}, bf16[1,256,512]{2,1,0:T(8,128)(2,1)}) custom-call(f32[1,3,128,512]{3,2,1,0:T(8,128)} %get-tuple-element.24.layers_ref, f32[256,512]{1,0:T(8,128)S(1)} %get-tuple-element.30.own_ref, bf16[256,512]{1,0:T(8,128)(2,1)S(1)} %collective-permute-done.5.other_ref, bf16[128,512]{1,0:T(8,128)(2,1)S(1)} %get-tuple-element.70.refs_0_, ...), custom_call_target="tpu_custom_call" | custom-call | flops 524288 | bytes 3145728 | tf_op jit(solution)/shard_map/cond/branch_0_fun/update/pallas_call | solution.py:185
  100.6 3.9 %all-to-all-done.3 = bf16[4,32,512]{2,1,0:T(8,128)(2,1)S(1)} async-done(((bf16[4,32,512]{2,1,0:T(8,128)(2,1)}), bf16[4,32,512]{2,1,0:T(8,128)(2,1)S(1)}, u32[]{:S(2)}, u32[]{:S(2)}) %all-to-all-start.3) | async-done | bytes 131104 | tf_op jit(solution)/shard_map/cond/branch_0_fun/all_to_all | solution.py:349
  104.5 2.6 %settle.2 = (f32[1,3,128,512]{3,2,1,0:T(8,128)}, f32[128,512]{1,0:T(8,128)}, f32[128,512]{1,0:T(8,128)}) custom-call(s32[1]{0:T(128)} %get-tuple-element.28.chosen_ref, bf16[128,512]{1,0:T(8,128)(2,1)S(1)} %bitcast.42, f32[1,3,128,512]{3,2,1,0:T(8,128)} %get-tuple-element.35.layers_hbm, ...), custom_call_target="tpu_custom_call", output_to_operand_aliasing={{0}: (2, {})} | custom-call | flops 1048576 | bytes 2097152 | tf_op jit(solution)/shard_map/cond/branch_0_fun/settle/pallas_call | solution.py:247
  (7 shorter events, 0.1 us)
Async XLA Ops:
  1.3 6.6 %collective-permute-start = (bf16[256,4096]{1,0:T(8,128)(2,1)}, bf16[256,4096]{1,0:T(8,128)(2,1)}, u32[]{:S(2)}, u32[]{:S(2)}) collective-permute-start(bf16[256,4096]{1,0:T(8,128)(2,1)} %bitcast.44), channel_id=1, source_target_pairs={{0,1},{1,0},{2,3},{3,2},{4,5},{5,4},{6,7},{7,6},{8,9},{9,8},{10,11... | collective-permute-start | bytes 6291464 | tf_op jit(solution)/shard_map/cond/branch_0_fun/ppermute | solution.py:336
  3.2 4.7 %collective-permute-start.1 = (bf16[256,512]{1,0:T(8,128)(2,1)}, bf16[256,512]{1,0:T(8,128)(2,1)S(1)}, u32[]{:S(2)}, u32[]{:S(2)}) collective-permute-start(bf16[256,512]{1,0:T(8,128)(2,1)} %bitcast.53), channel_id=1, source_target_pairs={{0,1},{1,0},{2,3},{3,2},{4,5},{5,4},{6,7},{7,6},{8,9},{9,8},{10,11... | collective-permute-start | bytes 786440 | tf_op jit(solution)/shard_map/cond/branch_0_fun/ppermute | solution.py:337
  7.9 0.7 copy-start.10
  13.8 12.6 %copy-start.3 = (f32[1,3,128,512]{3,2,1,0:T(8,128)S(1)}, f32[1,3,128,512]{3,2,1,0:T(8,128)}, u32[]{:S(2)}) copy-start(f32[1,3,128,512]{3,2,1,0:T(8,128)} %get-tuple-element.24.layers_ref) | copy-start | bytes 2359300 | tf_op jit(solution)/shard_map/cond
  13.8 35.1 %all-to-all-start = ((bf16[4,512,512]{2,1,0:T(8,128)(2,1)}), bf16[4,512,512]{2,1,0:T(8,128)(2,1)S(1)}, u32[]{:S(2)}, u32[]{:S(2)}) async-start(bf16[4,512,512]{2,1,0:T(8,128)(2,1)} %gradient.2.after_ref), calls=%async_computation | async-start | bytes 4194304 | tf_op jit(solution)/shard_map/cond/branch_0_fun/all_to_all | solution.py:342
  48.9 3.4 %copy-start.5 = (bf16[4,512,512]{2,1,0:T(8,128)(2,1)}, bf16[4,512,512]{2,1,0:T(8,128)(2,1)S(1)}, u32[]{:S(2)}) copy-start(bf16[4,512,512]{2,1,0:T(8,128)(2,1)S(1)} %all-to-all-done) | copy-start | bytes 6291460 | tf_op jit(solution)/shard_map/cond
  48.9 13.2 %all-to-all-start.1 = ((bf16[4,32,512]{2,1,0:T(8,128)(2,1)}), bf16[4,32,512]{2,1,0:T(8,128)(2,1)S(1)}, u32[]{:S(2)}, u32[]{:S(2)}) async-start(bf16[4,32,512]{2,1,0:T(8,128)(2,1)} %subtract_convert_fusion), calls=%async_computation.1 | async-start | bytes 262144 | tf_op jit(solution)/shard_map/cond/branch_0_fun/all_to_all | solution.py:346
  52.2 34.8 %copy-start = (s32[2]{0:T(128)S(1)}, s32[2]{0:T(128)}, u32[]{:S(2)}) copy-start(s32[2]{0:T(128)} %pad_add_fusion.place_ref) | copy-start | bytes 28 | tf_op jit(solution)/shard_map/cond
  52.3 30.9 %collective-permute-start.4 = (bf16[512,512]{1,0:T(8,128)(2,1)S(1)}, bf16[512,512]{1,0:T(8,128)(2,1)S(1)}, u32[]{:S(2)}, u32[]{:S(2)}) collective-permute-start(bf16[512,512]{1,0:T(8,128)(2,1)S(1)} %all_gather.4.w0_hbm), channel_id=1, source_target_pairs={{0,24},{8,0},{16,8},{24,16},{1,25},{9,1},{17,9},{25,17},{2,26},{10... | collective-permute-start | bytes 1572872 | tf_op jit(solution)/shard_map/cond/branch_0_fun/ppermute | solution.py:344
  55.6 31.4 %collective-permute-start.3 = (bf16[512,512]{1,0:T(8,128)(2,1)S(1)}, bf16[512,512]{1,0:T(8,128)(2,1)S(1)}, u32[]{:S(2)}, u32[]{:S(2)}) collective-permute-start(bf16[512,512]{1,0:T(8,128)(2,1)S(1)} %all_gather.4.w0_hbm), channel_id=1, source_target_pairs={{0,16},{8,24},{16,0},{24,8},{1,17},{9,25},{17,1},{25,9},{2,18},{10... | collective-permute-start | bytes 1572872 | tf_op jit(solution)/shard_map/cond/branch_0_fun/ppermute | solution.py:344
  57.6 29.5 %collective-permute-start.2 = (bf16[512,512]{1,0:T(8,128)(2,1)S(1)}, bf16[512,512]{1,0:T(8,128)(2,1)S(1)}, u32[]{:S(2)}, u32[]{:S(2)}) collective-permute-start(bf16[512,512]{1,0:T(8,128)(2,1)S(1)} %all_gather.4.w0_hbm), channel_id=1, source_target_pairs={{0,8},{8,16},{16,24},{24,0},{1,9},{9,17},{17,25},{25,1},{2,10},{10... | collective-permute-start | bytes 1572872 | tf_op jit(solution)/shard_map/cond/branch_0_fun/ppermute | solution.py:344
  62.8 30.2 %all-to-all-start.2 = ((bf16[4,32,512]{2,1,0:T(8,128)(2,1)}), bf16[4,32,512]{2,1,0:T(8,128)(2,1)S(1)}, u32[]{:S(2)}, u32[]{:S(2)}) async-start(bf16[4,32,512]{2,1,0:T(8,128)(2,1)} %broadcast_in_dim.3), calls=%async_computation.2 | async-start | bytes 262144 | tf_op jit(solution)/shard_map/cond/branch_0_fun/all_to_all | solution.py:348
  74.2 12.9 %copy-start.2 = (bf16[1,256,4096]{2,1,0:T(8,128)(2,1)S(1)}, bf16[1,256,4096]{2,1,0:T(8,128)(2,1)}, u32[]{:S(2)}) copy-start(bf16[1,256,4096]{2,1,0:T(8,128)(2,1)} %get-tuple-element.25) | copy-start | bytes 6291460 | tf_op jit(solution)/shard_map/cond
  76.9 21.7 %collective-permute-start.8 = (bf16[128,512]{1,0:T(8,128)(2,1)}, bf16[128,512]{1,0:T(8,128)(2,1)S(1)}, u32[]{:S(2)}, u32[]{:S(2)}) collective-permute-start(bf16[128,512]{1,0:T(8,128)(2,1)} %get-tuple-element.67), channel_id=1, source_target_pairs={{0,6},{2,4},{4,2},{6,0},{1,7},{3,5},{5,3},{7,1},{8,14},{10,12},{12... | collective-permute-start | bytes 393224 | tf_op jit(solution)/shard_map/cond/branch_0_fun/ppermute | solution.py:353
  80.7 17.8 %collective-permute-start.7 = (bf16[128,512]{1,0:T(8,128)(2,1)}, bf16[128,512]{1,0:T(8,128)(2,1)S(1)}, u32[]{:S(2)}, u32[]{:S(2)}) collective-permute-start(bf16[128,512]{1,0:T(8,128)(2,1)} %get-tuple-element.68), channel_id=1, source_target_pairs={{0,4},{2,6},{4,0},{6,2},{1,5},{3,7},{5,1},{7,3},{8,12},{10,14},{12... | collective-permute-start | bytes 393224 | tf_op jit(solution)/shard_map/cond/branch_0_fun/ppermute | solution.py:353
  83.2 15.4 %collective-permute-start.6 = (bf16[128,512]{1,0:T(8,128)(2,1)}, bf16[128,512]{1,0:T(8,128)(2,1)S(1)}, u32[]{:S(2)}, u32[]{:S(2)}) collective-permute-start(bf16[128,512]{1,0:T(8,128)(2,1)} %get-tuple-element.69), channel_id=1, source_target_pairs={{0,2},{2,0},{4,6},{6,4},{1,3},{3,1},{5,7},{7,5},{8,10},{10,8},{12,... | collective-permute-start | bytes 393224 | tf_op jit(solution)/shard_map/cond/branch_0_fun/ppermute | solution.py:353
  91.0 13.6 %copy-start.6 = (f32[3,128,512]{2,1,0:T(8,128)S(1)}, f32[3,128,512]{2,1,0:T(8,128)}, u32[]{:S(2)}) copy-start(f32[3,128,512]{2,1,0:T(8,128)} %get-tuple-element.27.outer_hbm) | copy-start | bytes 2359300 | tf_op jit(solution)/shard_map/cond
  91.0 7.6 %collective-permute-start.5 = (bf16[256,512]{1,0:T(8,128)(2,1)S(1)}, bf16[256,512]{1,0:T(8,128)(2,1)S(1)}, u32[]{:S(2)}, u32[]{:S(2)}) collective-permute-start(bf16[256,512]{1,0:T(8,128)(2,1)S(1)} %get-tuple-element.31), channel_id=1, source_target_pairs={{0,1},{1,0},{2,3},{3,2},{4,5},{5,4},{6,7},{7,6},{8,9},{9,8},{10,11... | collective-permute-start | bytes 786440 | tf_op jit(solution)/shard_map/cond/branch_0_fun/ppermute | solution.py:356
  93.7 10.8 %all-to-all-start.3 = ((bf16[4,32,512]{2,1,0:T(8,128)(2,1)}), bf16[4,32,512]{2,1,0:T(8,128)(2,1)S(1)}, u32[]{:S(2)}, u32[]{:S(2)}) async-start(bf16[4,32,512]{2,1,0:T(8,128)(2,1)} %broadcast_in_dim.17), calls=%async_computation.3 | async-start | bytes 262144 | tf_op jit(solution)/shard_map/cond/branch_0_fun/all_to_all | solution.py:349
